TPU v7x, 128 devices: a whole 4x4x4 slice. The times are simulated.
128 devices in a mesh: phase: 2 (over z_hi), seq: 32 (over y, x, core), dp: 2 (over z_lo).
Axes of the slice: x: 4, y: 4, z: 4 (z_hi: 2, z_lo: 2; z = z_hi * 2 + z_lo), core: 2. Of those that a mesh axis runs over, the one named last changes fastest.
Arguments:
- bin_activations: bfloat16 [4, 8192, 768], P('dp', 'seq'), may hold values from -6 to 6
- spaced_filter_coefs: bfloat16 [3, 768, 768], replicated, may hold values from -0.125 to 0.125
- merged_bin_projector: bfloat16 [768, 1536], replicated, may hold values from -0.21875 to 0.21875
- backbone_rms_gain: float32 [1536], replicated, may hold values from 0.5 to 1.5
- asking_projector: bfloat16 [1536, 1024], replicated, may hold values from -0.15625 to 0.15625
- common_lookup_projector: bfloat16 [1536, 256], replicated, may hold values from -0.15625 to 0.15625
- attention_exit_projector: bfloat16 [1024, 1536], replicated, may hold values from -0.1875 to 0.1875
- lane_logit_factor: float32 [8], replicated, may hold values from 1 to 40
- splice_readout_lines: bfloat16 [2, 4, 4096, 1536], P('phase', 'dp', 'seq'), may hold values from -6 to 6
- couple_embedding_cotangent: bfloat16 [2, 4, 4096, 768], P('phase', 'dp', 'seq'), may hold values from -6 to 6
- splice_site_projector: bfloat16 [2, 1536, 768], replicated, may hold values from -0.21875 to 0.21875
- site_locator_code: int32 [2, 4, 32, 32, 16], P('phase', 'dp', 'seq'), may hold values from 0 to 255
- site_local_line: int32 [2, 4, 32, 32, 16], P('phase', 'dp', 'seq'), may hold values from 0 to 127
- filled_slot_totals: int32 [2, 4, 32, 32], P('phase', 'dp', 'seq'), may hold values from 1 to 16, as said below
Outputs:
- phase_rows: bfloat16 [2, 4, 4096, 1536], P('phase', 'dp', 'seq')
- row_grad: bfloat16 [2, 4, 4096, 1536], P('phase', 'dp', 'seq')
- weight_grad: float32 [2, 2, 1536, 768], P('phase', None, ('seq', 'dp'))
Inputs may be any that keep to these rules, and one draw needn't show every extreme that they name: `filled_slot_totals`: in each micro-batch and sequence, one receiving shard gets 16 valid slots from every listing shard; the other blocks hold 1 to 8.
All inputs are finite; a program needn't handle non-finite values.
Results may differ from a plain program's by a relative error of at most 0.034.
Values may be sent and summed in bfloat16 or wider, within the bound.
No kernel may reach another device: no remote copies, remote signals or barrier semaphores. Data moves between devices by JAX's collectives and lax.ppermute only.
A program may use at most 128 MiB of HBM per device.

v0:
```python
import math

import jax
import jax.numpy as jnp
from jax import lax
from jax.sharding import PartitionSpec as P

DILATION_STEP = 2


def padded(block, sides, width):
    for axis, dim in sides:
        count = lax.axis_size(axis)
        forward = [(i, i + 1) for i in range(count - 1)]
        backward = [(target, source) for source, target in forward]
        low = lax.ppermute(
            lax.slice_in_dim(block, block.shape[dim] - width, None, axis=dim), axis, forward
        )
        high = lax.ppermute(lax.slice_in_dim(block, 0, width, axis=dim), axis, backward)
        block = jnp.concatenate([low, block, high], axis=dim)
    return block


def shifted(value, axis, steps):
    count = lax.axis_size(axis)
    initial, last = (max(0, -steps), min(count, count - steps))
    return lax.ppermute(value, axis, [(source, source + steps) for source in range(initial, last)])


def body(
    bin_activations,
    spaced_filter_coefs,
    merged_bin_projector,
    backbone_rms_gain,
    asking_projector,
    common_lookup_projector,
    attention_exit_projector,
    lane_logit_factor,
    splice_readout_lines,
    couple_embedding_cotangent,
    splice_site_projector,
    site_locator_code,
    site_local_line,
    filled_slot_totals,
):
    phase = lax.axis_index("phase")
    batch, cell_positions, chans = bin_activations.shape
    rows_dev = cell_positions // 2
    width = merged_bin_projector.shape[1]
    kernel_taps = spaced_filter_coefs.shape[0]
    receptive_extent = DILATION_STEP * (kernel_taps // 2)
    asking_lanes = lane_logit_factor.shape[0]
    attn_lane_size = common_lookup_projector.shape[1] // 2
    logit_multiplier = lane_logit_factor / math.sqrt(attn_lane_size)
    count = bin_activations.shape[0]
    padded_input = padded(bin_activations, (("seq", 1),), receptive_extent)

    def encoder():
        running_sum = jnp.zeros((count, cell_positions, chans), jnp.float32)
        for kernel_tap in range(kernel_taps):
            running_sum = running_sum + jnp.einsum(
                "bpc,cd->bpd",
                padded_input[
                    :, kernel_tap * DILATION_STEP : kernel_tap * DILATION_STEP + cell_positions
                ],
                spaced_filter_coefs[kernel_tap],
                preferred_element_type=jnp.float32,
            )
        hidden = padded_input[:, receptive_extent : receptive_extent + cell_positions].astype(
            jnp.float32
        ) + jax.nn.gelu(running_sum)
        pooled = hidden.reshape(count, rows_dev, 2, chans).mean(axis=2).astype(jnp.bfloat16)
        return jnp.einsum(
            "brc,cd->brd", pooled, merged_bin_projector, preferred_element_type=jnp.float32
        ).astype(jnp.bfloat16)

    def project(rows_in):
        wide = rows_in.astype(jnp.float32)
        normed = (
            wide
            * lax.rsqrt(jnp.mean(wide * wide, axis=-1, keepdims=True) + 1e-06)
            * backbone_rms_gain
        ).astype(jnp.bfloat16)
        queries = jnp.einsum(
            "brd,de->bre", normed, asking_projector, preferred_element_type=jnp.float32
        ).astype(jnp.bfloat16)
        keyvals = jnp.einsum(
            "brd,de->bre", normed, common_lookup_projector, preferred_element_type=jnp.float32
        ).astype(jnp.bfloat16)
        return (queries, keyvals)

    def attend_one(operands):
        query, keyval = operands
        query = query.reshape(rows_dev, asking_lanes, attn_lane_size)
        scores = (
            jnp.einsum(
                "qhe,ke->hqk", query, keyval[:, :attn_lane_size], preferred_element_type=jnp.float32
            )
            * logit_multiplier[:, None, None]
        )
        top = jnp.max(scores, axis=-1, keepdims=True)
        expo = jnp.exp(scores - top)
        weights = (expo / jnp.sum(expo, axis=-1, keepdims=True)).astype(jnp.bfloat16)
        mixed = jnp.einsum(
            "hqk,ke->qhe", weights, keyval[:, attn_lane_size:], preferred_element_type=jnp.float32
        ).astype(jnp.bfloat16)
        return mixed.reshape(rows_dev, asking_lanes * attn_lane_size)

    def attend(rows_in, queries, gathered):
        attended = lax.map(attend_one, (queries, gathered))
        mixed = jnp.einsum(
            "brh,hd->brd", attended, attention_exit_projector, preferred_element_type=jnp.float32
        )
        return (rows_in.astype(jnp.float32) + mixed).astype(jnp.bfloat16)

    def no_rows():
        return jnp.zeros((batch, rows_dev, width), jnp.bfloat16)

    embedded_bins = lax.cond(phase == 0, encoder, no_rows)
    handed = shifted(embedded_bins, "phase", 1)

    def no_project():
        return (
            jnp.zeros((batch, rows_dev, asking_lanes * attn_lane_size), jnp.bfloat16),
            jnp.zeros((batch, rows_dev, 2 * attn_lane_size), jnp.bfloat16),
        )

    queries, keyvals = lax.cond(phase == 1, lambda: project(handed), no_project)
    gathered = lax.all_gather(keyvals, "seq", axis=1, tiled=True)

    def keep_rows():
        return embedded_bins

    phase_rows = lax.cond(phase == 1, lambda: attend(handed, queries, gathered), keep_rows)[None]
    cotangent = couple_embedding_cotangent[0]
    ids = site_locator_code[0, :, 0]
    rows_at = site_local_line[0, :, 0]
    counts = filled_slot_totals[0, :, 0]
    junc_dev = cotangent.shape[1]
    embed = cotangent.shape[2]
    shards = lax.axis_size("seq")
    slots = ids.shape[-1]
    slot_iota = jnp.arange(slots, dtype=jnp.int32)
    take_rows = jax.vmap(lambda table, index: jnp.take(table, index, axis=0))
    everything = lax.all_gather(cotangent, "seq", axis=1, tiled=True)
    ids_in, rows_in, counts_in = (
        lax.all_to_all(ids, "seq", split_axis=1, concat_axis=1, tiled=True),
        lax.all_to_all(rows_at, "seq", split_axis=1, concat_axis=1, tiled=True),
        lax.all_to_all(counts, "seq", split_axis=1, concat_axis=1, tiled=True),
    )
    valid = slot_iota[None, None, :] < counts_in[..., None]
    source_shard = jnp.arange(shards, dtype=jnp.int32)[None, :, None]
    which = source_shard * junc_dev + ids_in % junc_dev
    picked = take_rows(everything, which.reshape(batch, -1))
    arrived = jnp.where(valid.reshape(batch, -1, 1), picked, jnp.zeros_like(picked))
    codes = jnp.where(valid, ids_in // junc_dev * rows_dev + rows_in, -1).reshape(batch, -1)
    targets = jnp.arange(2 * rows_dev, dtype=jnp.int32)
    onehot = (codes[:, None, :] == targets[None, :, None]).astype(jnp.bfloat16)
    ends = jnp.einsum("bte,bep->btp", onehot, arrived, preferred_element_type=jnp.float32).astype(
        jnp.bfloat16
    )
    ends = ends.reshape(batch, 2, rows_dev, embed)
    row_grad = jnp.einsum(
        "bkrp,kdp->brd", ends, splice_site_projector, preferred_element_type=jnp.float32
    ).astype(jnp.bfloat16)[None]
    portion = splice_readout_lines[0]
    summed = lax.psum_scatter(
        jnp.einsum("brd,bkrp->dkp", portion, ends, preferred_element_type=jnp.float32),
        ("seq", "dp"),
        scatter_dimension=0,
        tiled=True,
    )
    weight_grad = jnp.transpose(summed, (1, 0, 2))[None]
    return (phase_rows, row_grad, weight_grad)


def solution(mesh):
    return jax.shard_map(
        body,
        mesh=mesh,
        in_specs=(
            P("dp", "seq", None),
            P(),
            P(),
            P(),
            P(),
            P(),
            P(),
            P(),
            P("phase", "dp", "seq", None),
            P("phase", "dp", "seq", None),
            P(),
            P("phase", "dp", "seq", None, None),
            P("phase", "dp", "seq", None, None),
            P("phase", "dp", "seq", None),
        ),
        out_specs=(
            P("phase", "dp", "seq", None),
            P("phase", "dp", "seq", None),
            P("phase", None, ("seq", "dp"), None),
        ),
        check_vma=False,
    )
```

profile of v0, /device:TPU:64, one launch (start us, length us, event | category | flops | bytes accessed | tf_op | source)
XLA Modules:
  0.0 726.9 jit_solution(12408204056932710371)
XLA Ops:
  8.7 1.7 collective-permute-start
  11.8 3.0 collective-permute-done.1
  18.4 30.0 %collective-permute-done.2 = bf16[2,128,1536]{2,1,0:T(8,128)(2,1)} collective-permute-done((bf16[2,128,1536]{2,1,0:T(8,128)(2,1)}, bf16[2,128,1536]{2,1,0:T(8,128)(2,1)}, u32[]{:S(2)}, u32[]{:S(2)}) %collective-permute-start.2) | collective-permute-done | bytes 786464 | tf_op jit(solution)/shard_map/ppermute | solution.py:27
  48.5 6.5 conditional.4
  49.9 3.5 fusion.26
  56.4 9.4 %all-to-all-start = ((s32[2,32,1]{0,2,1:T(1,128)}), s32[2,32,1]{0,2,1:T(1,128)S(1)}, u32[]{:S(2)}, u32[]{:S(2)}) async-start(s32[2,32,1]{0,2,1:T(1,128)} %copy.62), calls=%async_computation | async-start | bytes 32768 | tf_op jit(solution)/shard_map/all_to_all | solution.py:149
  66.5 6.6 all-to-all-done
  73.1 3.8 all-to-all-start.1
  77.6 6.7 all-to-all-done.1
  84.3 3.9 all-to-all-start.2
  88.9 6.8 all-to-all-done.2
  96.2 14.5 %gather_fusion = bf16[1024,768]{1,0:T(8,128)(2,1)S(1)} fusion(bf16[2,4096,768]{2,1,0:T(8,128)(2,1)} %bitcast.157, s32[1024]{0:T(1024)S(1)} %bitcast.156), kind=kCustom, calls=%fused_computation | custom fusion | bytes 3153920 | tf_op jit(solution)/shard_map/vmap(jit(_take))/gather | solution.py:144
  112.8 5.1 convolution_bitcast_fusion
  117.9 14.9 %copy.76 = f32[1536,2,768]{2,1,0:T(2,128)} copy(f32[1536,2,768]{0,2,1:T(8,128)} %convolution_bitcast_fusion) | data formatting | bytes 18874368 | tf_op jit(solution)/shard_map/brd,bkrp->dkp/dot_general | solution.py:168
  134.7 35.6 %conditional.5 = (bf16[1,2,128,1536]{3,2,1,0:T(8,128)(2,1)}) conditional(s32[]{:T(128)} %convert_element_type.52, bf16[2,128,1536]{2,1,0:T(8,128)(2,1)} %get-tuple-element.212, (bf16[2,128,1536]{2,1,0:T(8,128)(2,1)}, f32[8]{0:T(128)S(1)}, bf16[2,4096,256]{2,1,0:T(8,128)(2,1)}, bf16[2,128,1024]{2,1,0:T(8,128)(2,1)S(1)}, ...), branch_computations={%region_6.0_spmd, %region_7.12_spmd} | conditional | flops 4057211904 | bytes 14951661 | solution.py:134
  134.7 31.4 %while.12 = (s32[]{:T(128)}, bf16[2,128,1024]{1,2,0:T(8,128)(2,1)}, bf16[2,4096,256]{2,1,0:T(8,128)(2,1)}, bf16[2,128,1024]{2,1,0:T(8,128)(2,1)S(1)}, f32[8]{0:T(128)S(1)}, /*index=5*/s32[]{:T(128)}) while((s32[]{:T(128)}, bf16[2,128,1024]{1,2,0:T(8,128)(2,1)}, bf16[2,4096,256]{2,1,0:T(8,128)(2,1)}, bf16[2,128,1024]{2,1,0:T(8,128)(2,1)S(1)}, ...), condition=%wide.region_11.11_spmd, body=%wide.region_8.10_spmd.sunk | while | flops 3250725888 | bytes 9708653 | solution.py:110
  136.7 5.4 fusion.117
  142.1 7.6 %fusion.118 = bf16[128,8,128]{2,0,1:T(8,128)(2,1)S(1)} fusion(f32[8,128]{1,0:T(8,128)S(1)} %fusion.117, bf16[4096,256]{1,0:T(8,128)(2,1)S(1)} %dynamic-slice_bitcast_fusion.3, f32[8]{0:T(128)S(1)} %get-tuple-element.204, bf16[128,8,128]{0,2,1:T(8,128)(2,1)S(1)} %bitcast.160), kind=kOutput, calls=%fused_computation.47.clone.1 | convolution fusion | flops 2164397056 | bytes 2625568 | tf_op jit(solution)/shard_map/cond/branch_1_fun/while/body/eval_jaxpr/hqk,ke->qhe/dot_general | solution.py:104
  150.4 1.7 dynamic-slice_bitcast_fusion.3
  152.4 5.4 fusion.117
  157.8 7.6 %fusion.118 = bf16[128,8,128]{2,0,1:T(8,128)(2,1)S(1)} fusion(f32[8,128]{1,0:T(8,128)S(1)} %fusion.117, bf16[4096,256]{1,0:T(8,128)(2,1)S(1)} %dynamic-slice_bitcast_fusion.3, f32[8]{0:T(128)S(1)} %get-tuple-element.204, bf16[128,8,128]{0,2,1:T(8,128)(2,1)S(1)} %bitcast.160), kind=kOutput, calls=%fused_computation.47.clone.1 | convolution fusion | flops 2164397056 | bytes 2625568 | tf_op jit(solution)/shard_map/cond/branch_1_fun/while/body/eval_jaxpr/hqk,ke->qhe/dot_general | solution.py:104
  166.1 4.1 fusion.61
  170.3 4.9 fusion.72
  175.2 543.6 %all-reduce.3.cloned.1.call-done = f32[1536,2,768]{2,1,0:T(2,128)} async-done(((f32[1536,2,768]{2,1,0:T(2,128)}), f32[1536,2,768]{2,1,0:T(2,128)}) %all-reduce.3.cloned.1.call-update) | async-done | bytes 9437200
  (75 shorter events, 22.7 us)
Async XLA Ops:
  7.2 105.6 %copy-start = (bf16[1,2,128,1536]{3,2,1,0:T(8,128)(2,1)S(1)}, bf16[1,2,128,1536]{3,2,1,0:T(8,128)(2,1)}, u32[]{:S(2)}) copy-start(bf16[1,2,128,1536]{3,2,1,0:T(8,128)(2,1)} %param.30) | copy-start | bytes 2359300
  7.2 9.0 %copy-start.2 = (bf16[2,256,768]{2,1,0:T(8,128)(2,1)S(1)}, bf16[2,256,768]{2,1,0:T(8,128)(2,1)}, u32[]{:S(2)}) copy-start(bf16[2,256,768]{2,1,0:T(8,128)(2,1)} %param.22) | copy-start | bytes 2359300
  7.2 89.0 %all-gather.6.cloned.1.call-start = ((), (), s32[]{:S(2)}) async-start(), calls=%async_computation.4 | async-start | bytes 12976128 | tf_op jit(solution)/shard_map/all_gather | solution.py:145
  7.9 126.8 %all-gather.4.cloned.1.call-start = ((), (), s32[]{:S(2)}) async-start(), calls=%async_computation.3 | async-start | bytes 4325376 | tf_op jit(solution)/shard_map/all_gather | solution.py:129
  8.7 3.1 collective-permute-start
  10.5 4.3 collective-permute-start.1
  16.2 32.3 %copy-start.10 = (f32[1536]{0:T(1024)S(1)}, f32[1536]{0:T(1024)}, u32[]{:S(2)}) copy-start(f32[1536]{0:T(1024)} %param.25) | copy-start | bytes 18436
  17.1 31.3 %collective-permute-start.2 = (bf16[2,128,1536]{2,1,0:T(8,128)(2,1)}, bf16[2,128,1536]{2,1,0:T(8,128)(2,1)}, u32[]{:S(2)}, u32[]{:S(2)}) collective-permute-start(bf16[2,128,1536]{2,1,0:T(8,128)(2,1)} %get-tuple-element.212), channel_id=1, source_target_pairs={{0,64},{1,65},{2,66},{3,67},{4,68},{5,69},{6,70},{7,71},{8,72},{9,... | collective-permute-start | bytes 2359304 | tf_op jit(solution)/shard_map/ppermute | solution.py:27
  48.5 7.2 copy-start.7
  48.5 17.3 %copy-start.5 = (s32[1,2,1,32,16]{3,4,2,1,0:T(8,128)S(1)}, s32[1,2,1,32,16]{3,4,2,1,0:T(8,128)}, u32[]{:S(2)}) copy-start(s32[1,2,1,32,16]{3,4,2,1,0:T(8,128)} %param.33) | copy-start | bytes 12292
  48.5 28.5 %copy-start.6 = (s32[1,2,1,32,16]{3,4,2,1,0:T(8,128)S(1)}, s32[1,2,1,32,16]{3,4,2,1,0:T(8,128)}, u32[]{:S(2)}) copy-start(s32[1,2,1,32,16]{3,4,2,1,0:T(8,128)} %param.34) | copy-start | bytes 12292
  49.9 3.5 copy-start.9
  55.0 0.7 copy-start.4
  56.4 16.7 %all-to-all-start = ((s32[2,32,1]{0,2,1:T(1,128)}), s32[2,32,1]{0,2,1:T(1,128)S(1)}, u32[]{:S(2)}, u32[]{:S(2)}) async-start(s32[2,32,1]{0,2,1:T(1,128)} %copy.62), calls=%async_computation | async-start | bytes 32768 | tf_op jit(solution)/shard_map/all_to_all | solution.py:149
  73.1 11.2 %all-to-all-start.1 = ((s32[2,32,16]{2,0,1:T(2,128)}), s32[2,32,16]{2,0,1:T(2,128)S(1)}, u32[]{:S(2)}, u32[]{:S(2)}) async-start(s32[2,32,16]{2,0,1:T(2,128)} %bitcast.21), calls=%async_computation.1 | async-start | bytes 65536 | tf_op jit(solution)/shard_map/all_to_all | solution.py:147
  84.3 11.3 %all-to-all-start.2 = ((s32[2,32,16]{2,0,1:T(2,128)}), s32[2,32,16]{2,0,1:T(2,128)S(1)}, u32[]{:S(2)}, u32[]{:S(2)}) async-start(s32[2,32,16]{2,0,1:T(2,128)} %bitcast.22), calls=%async_computation.2 | async-start | bytes 65536 | tf_op jit(solution)/shard_map/all_to_all | solution.py:148
  88.2 630.6 %all-reduce.3.cloned.1.call-start = ((), (), s32[]{:S(2)}) async-start(), calls=%async_computation.5 | async-start | bytes 18874368
  111.9 0.9 copy-start.3
  132.8 0.7 copy-start.12
  132.8 1.9 copy-start.11
  170.3 550.1 %copy-start.1 = (bf16[1,2,128,1536]{3,2,1,0:T(8,128)(2,1)S(1)}, bf16[1,2,128,1536]{3,2,1,0:T(8,128)(2,1)}, u32[]{:S(2)}) copy-start(bf16[1,2,128,1536]{3,2,1,0:T(8,128)(2,1)} %param.30) | copy-start | bytes 2359300
Sparse Core Ops, SparseCore 0:
  10.3 64.5 all-gather.5
  77.8 45.5 all-gather.3
  132.9 585.8 all-reduce.2
where the time goes:
time: 730 us; the launch traced here: 727 us
  waiting for transfers between devices  597 us (82%)
  matrix products  46.3 us (6%)
  local copies, waits for them, and re-layouts  43.8 us (6%)
  starting transfers between devices  21.7 us (3%)
  between operations  14.7 us (2%)
    unnamed x4, waiting for transfers between devices  544 us
    ppermute x1, waiting for transfers between devices, shifted(): lax.ppermute(value, axis, [(source, source + steps) for source in range(i...  30 us
    dot_general x2, matrix products, attend_one(): jnp.einsum('hqk,ke->qhe', weights, keyval[:, attn_lane_size:], preferred_...  15.3 us
    dot_general x1, local copies, waits for them, and re-layouts, body(): jnp.einsum('brd,bkrp->dkp', portion, ends, preferred_element_type=jnp.flo...  14.9 us
  transfers between devices with their start and end apart: 9, of which 6 were waited for; matrix products, arithmetic and copies ran while one was open for 12% of the time, Pallas kernels for 0%

commit v1 on v0

v1 whole, which is shorter than its diff:
```python
import math

import jax
import jax.numpy as jnp
from jax import lax
from jax.sharding import Mesh
from jax.sharding import PartitionSpec as P

DILATION_STEP = 2
SEQ = ("y", "x", "core")
F32 = jnp.float32
BF16 = jnp.bfloat16


def dot(a, b, dims=(((1,), (0,)), ((), ()))):
    return lax.dot_general(a, b, dims, preferred_element_type=F32)


def halo(block, width):
    count = lax.axis_size(SEQ)
    forward = [(i, i + 1) for i in range(count - 1)]
    backward = [(b, a) for a, b in forward]
    low = lax.ppermute(block[:, -width:], SEQ, forward)
    high = lax.ppermute(block[:, :width], SEQ, backward)
    return jnp.concatenate([low, block, high], axis=1)


def body(
    bin_activations,
    spaced_filter_coefs,
    merged_bin_projector,
    backbone_rms_gain,
    asking_projector,
    common_lookup_projector,
    attention_exit_projector,
    lane_logit_factor,
    splice_readout_lines,
    couple_embedding_cotangent,
    splice_site_projector,
    site_locator_code,
    site_local_line,
    filled_slot_totals,
):
    phase = lax.axis_index("phase")
    core = lax.axis_index("core")
    batch, cells, chans = bin_activations.shape
    rows = cells // 2
    width = merged_bin_projector.shape[1]
    taps = spaced_filter_coefs.shape[0]
    extent = DILATION_STEP * (taps // 2)
    heads = lane_logit_factor.shape[0]
    lane = common_lookup_projector.shape[1] // 2
    swap = [(0, 1), (1, 0)]

    cotangent = couple_embedding_cotangent[0]
    junc = cotangent.shape[1]
    embed = cotangent.shape[2]
    ids = site_locator_code[0, :, 0]
    lines = site_local_line[0, :, 0]
    counts = filled_slot_totals[0, :, 0]
    shards, slots = ids.shape[1:]
    valid = lax.broadcasted_iota(jnp.int32, ids.shape, 2) < counts[..., None]
    codes = jnp.where(valid, ids // junc * rows + lines, -1)
    which = jnp.where(valid, ids % junc, -1)
    pick = (
        which.reshape(batch, shards * slots, 1) == jnp.arange(junc, dtype=jnp.int32)
    ).astype(BF16)
    picked = dot(pick, cotangent, (((2,), (1,)), ((0,), (0,)))).astype(BF16)
    tags = jnp.broadcast_to(
        codes.astype(BF16).reshape(batch, shards * slots, 1), (batch, shards * slots, 128)
    )
    payload = jnp.concatenate([picked, tags], axis=-1)
    payload = payload.reshape(batch, shards, slots, embed + 128).transpose(1, 0, 2, 3)
    arrived = lax.all_to_all(payload, SEQ, 0, 0, tiled=True)

    padded_input = halo(bin_activations, extent)
    total = jnp.zeros((batch, cells, chans), F32)
    for tap in range(taps):
        total = total + jnp.einsum(
            "bpc,cd->bpd",
            padded_input[:, tap * DILATION_STEP : tap * DILATION_STEP + cells],
            spaced_filter_coefs[tap],
            preferred_element_type=F32,
        )
    hidden = bin_activations.astype(F32) + jax.nn.gelu(total)
    pooled = hidden.reshape(batch, rows, 2, chans).mean(axis=2).astype(BF16)
    encoded = jnp.einsum(
        "brc,cd->brd", pooled, merged_bin_projector, preferred_element_type=F32
    ).astype(BF16)

    wide = encoded.astype(F32)
    normed = (
        wide
        * lax.rsqrt(jnp.mean(wide * wide, axis=-1, keepdims=True) + 1e-06)
        * backbone_rms_gain
    ).astype(BF16)
    keyvals = jnp.einsum(
        "brd,de->bre", normed, common_lookup_projector, preferred_element_type=F32
    ).astype(BF16)
    gathered = lax.all_gather(keyvals, SEQ, axis=1, tiled=True)
    queries = jnp.einsum(
        "brd,de->bre", normed, asking_projector, preferred_element_type=F32
    ).astype(BF16)

    portion = splice_readout_lines[0].reshape(batch * rows, width)
    blocks = shards // 2
    lines_t = portion.T.reshape(blocks, 2, width // (2 * blocks), batch * rows)
    mine = lax.dynamic_index_in_dim(lines_t, core, 1, keepdims=False)
    other = lax.dynamic_index_in_dim(lines_t, 1 - core, 1, keepdims=False)
    other = lax.ppermute(other, "core", swap)
    lines_t = jnp.concatenate([mine, other], axis=2).reshape(width // 2, 2 * batch * rows)

    data = arrived[..., :embed].transpose(1, 0, 2, 3).reshape(batch, shards * slots, embed)
    tag = arrived[..., embed:].transpose(1, 0, 2, 3).reshape(batch, shards * slots, 128)
    ends = []
    for kind in range(2):
        target = (jnp.arange(rows, dtype=jnp.int32) + kind * rows).astype(BF16)
        onehot = (tag[:, :, :rows] == target).astype(BF16)
        ends.append(dot(onehot, data, (((1,), (1,)), ((0,), (0,)))).astype(BF16))
    ends = jnp.concatenate(ends, axis=-1).reshape(batch * rows, 2 * embed)
    ends_other = lax.ppermute(ends, "core", swap)
    partial = dot(lines_t, jnp.concatenate([ends, ends_other], axis=0)).astype(BF16)
    partial = partial.reshape(shards, width // (2 * shards), 2 * embed)
    pieces = lax.all_to_all(partial, ("y", "x", "dp"), 0, 0, tiled=True)

    row_grad = (
        dot(ends[:, :embed], splice_site_projector[0], (((1,), (1,)), ((), ())))
        + dot(ends[:, embed:], splice_site_projector[1], (((1,), (1,)), ((), ())))
    ).astype(BF16)
    row_grad = row_grad.reshape(batch, rows, width)[None]

    logit = lane_logit_factor / math.sqrt(lane)

    def attend_one(operands):
        query, keyval = operands
        query = query.reshape(rows, heads, lane)
        scores = (
            jnp.einsum("qhe,ke->hqk", query, keyval[:, :lane], preferred_element_type=F32)
            * logit[:, None, None]
        )
        top = jnp.max(scores, axis=-1, keepdims=True)
        expo = jnp.exp(scores - top)
        weights = (expo / jnp.sum(expo, axis=-1, keepdims=True)).astype(BF16)
        mixed = jnp.einsum(
            "hqk,ke->qhe", weights, keyval[:, lane:], preferred_element_type=F32
        ).astype(BF16)
        return mixed.reshape(rows, heads * lane)

    def trunk():
        attended = lax.map(attend_one, (queries, gathered))
        mixed = jnp.einsum(
            "brh,hd->brd", attended, attention_exit_projector, preferred_element_type=F32
        )
        return (encoded.astype(F32) + mixed).astype(BF16)

    phase_rows = lax.cond(phase == 1, trunk, lambda: encoded)[None]

    summed = jnp.sum(pieces.astype(F32), axis=0)
    weight_grad = summed.reshape(-1, 2, embed).transpose(1, 0, 2)[None]
    return (phase_rows, row_grad, weight_grad)


def solution(mesh):
    shape = dict(mesh.shape)
    side = math.isqrt(shape["seq"] // 2)
    fine = Mesh(
        mesh.devices.reshape(shape["phase"], side, side, 2, shape["dp"]),
        ("phase", "y", "x", "core", "dp"),
    )
    return jax.shard_map(
        body,
        mesh=fine,
        in_specs=(
            P("dp", SEQ, None),
            P(),
            P(),
            P(),
            P(),
            P(),
            P(),
            P(),
            P("phase", "dp", SEQ, None),
            P("phase", "dp", SEQ, None),
            P(),
            P("phase", "dp", SEQ, None, None),
            P("phase", "dp", SEQ, None, None),
            P("phase", "dp", SEQ, None),
        ),
        out_specs=(
            P("phase", "dp", SEQ, None),
            P("phase", "dp", SEQ, None),
            P("phase", None, SEQ + ("dp",), None),
        ),
        check_vma=False,
    )
```

time: 730 us -> 194 us (0.27)
  waiting for transfers between devices: 597 us -> 57.3 us
  matrix products: 46.3 us -> 61 us
  local copies, waits for them, and re-layouts: 43.8 us -> 33 us
    unnamed x4 -> x1, waiting for transfers between devices: 544 us -> 0.02 us
    all_to_all x3 -> x2, waiting for transfers between devices: 20.1 us -> 55.9 us  [the longest x1 28.5 us: body(): arrived = lax.all_to_all(payload, SEQ, 0, 0, tiled=True)]
    ppermute x3 -> x4, waiting for transfers between devices: 33.1 us -> 1.36 us  [the longest x1 1.35 us: body(): other = lax.ppermute(other, 'core', swap)]
    dot_general x1 -> x0, local copies, waits for them, and re-layouts: 14.9 us -> none  [body(): jnp.einsum('brd,bkrp->dkp', portion, ends, preferred_element_type=jnp.flo...]
    gather x1 -> x0, local copies, waits for them, and re-layouts: 14.5 us -> none  [body(): take_rows = jax.vmap(lambda table, index: jnp.take(table, index, axis=0))]
    dot_general x8 -> x15, matrix products: 35.6 us -> 48.8 us  [the longest x2 18 us: attend_one(): jnp.einsum('hqk,ke->qhe', weights, keyval[:, lane:], preferred_element_ty...]
    all_to_all x3 -> x2, starting transfers between devices: 17.1 us -> 14.9 us  [the longest x1 9.97 us: body(): arrived = lax.all_to_all(payload, SEQ, 0, 0, tiled=True)]
  transfers between devices with their start and end apart: 9 -> 7, of which waited for: 6 -> 3; matrix products, arithmetic and copies ran while one was open for 12% -> 20% of each run, Pallas kernels for 0% -> 0%
where the time goes in v1:
time: 194 us; the launch traced here: 192 us
  matrix products  61 us (31%)
  waiting for transfers between devices  57.3 us (30%)
  local copies, waits for them, and re-layouts  33 us (17%)
  starting transfers between devices  18.7 us (10%)
  between operations  14.3 us (7%)
  other arithmetic  8.01 us (4%)
    all_to_all x1, waiting for transfers between devices, body(): arrived = lax.all_to_all(payload, SEQ, 0, 0, tiled=True)  28.5 us
    all_to_all x1, waiting for transfers between devices, body(): pieces = lax.all_to_all(partial, ('y', 'x', 'dp'), 0, 0, tiled=True)  27.5 us
    dot_general x2, matrix products, attend_one(): jnp.einsum('hqk,ke->qhe', weights, keyval[:, lane:], preferred_element_ty...  18 us
    sub x2, matrix products, attend_one(): expo = jnp.exp(scores - top)  12.2 us
    dot_general x6, matrix products, dot(): return lax.dot_general(a, b, dims, preferred_element_type=F32)  11.8 us
    all_to_all x1, starting transfers between devices, body(): arrived = lax.all_to_all(payload, SEQ, 0, 0, tiled=True)  9.97 us
    dot_general x3, matrix products, body(): jnp.einsum('bpc,cd->bpd', padded_input[:, tap * DILATION_STEP:tap * DILAT...  8.03 us
    squeeze x2, local copies, waits for them, and re-layouts, trunk(): attended = lax.map(attend_one, (queries, gathered))  6.18 us
  transfers between devices with their start and end apart: 7, of which 3 were waited for; matrix products, arithmetic and copies ran while one was open for 20% of the time, Pallas kernels for 0%

profile of v1, /device:TPU:64, one launch (start us, length us, event | category | flops | bytes accessed | tf_op | source)
XLA Modules:
  0.0 192.4 jit_solution(697377688413310412)
XLA Ops:
  11.3 2.3 %fusion.62 = f32[2,256,768]{2,1,0:T(8,128)S(1)} fusion(bf16[2,256,768]{2,1,0:T(8,128)(2,1)} %param.18, bf16[3,768,768]{2,1,0:T(8,128)(2,1)} %param.19), kind=kOutput, calls=%fused_computation.63 | convolution fusion | flops 603979776 | bytes 3538944 | tf_op jit(solution)/shard_map/bpc,cd->bpd/dot_general | solution.py:79
  13.7 2.1 %fusion.64 = f32[2,256,768]{2,1,0:T(8,128)S(1)} fusion(bf16[3,768,768]{2,1,0:T(8,128)(2,1)} %param.19, bf16[2,256,768]{2,1,0:T(8,128)(2,1)S(1)} %copy-done.7, bf16[2,2,768]{2,1,0:T(2,128)(2,1)S(1)} %collective-permute-done), kind=kOutput, calls=%fused_computation.65 | convolution fusion | flops 605552640 | bytes 3545088 | tf_op jit(solution)/shard_map/bpc,cd->bpd/dot_general | solution.py:79
  15.7 3.7 %fusion.51 = f32[2,256,768]{2,1,0:T(8,128)} fusion(f32[2,256,768]{2,1,0:T(8,128)S(1)} %fusion.64, f32[2,256,768]{2,1,0:T(8,128)S(1)} %fusion.62, bf16[2,256,768]{2,1,0:T(8,128)(2,1)S(1)} %copy-done.7, bf16[3,768,768]{2,1,0:T(8,128)(2,1)} %param.19, bf16[2,2,768]{2,1,0:T(2,128)(2,1)S(1)} %collective-permute-done.1), kind=kOutput, calls=%fused_computation.53 | convolution fusion | flops 610271232 | bytes 7477248 | tf_op jit(solution)/shard_map/bpc,cd->bpd/dot_general | solution.py:79
  19.4 3.0 %reshape.148 = f32[2,128,2,768]{3,2,1,0:T(2,128)} reshape(f32[2,256,768]{2,1,0:T(8,128)} %fusion.51) | data formatting | bytes 3145728 | tf_op jit(solution)/shard_map/reshape | solution.py:86
  22.4 4.2 %reduce_sum.36 = f32[2,128,768]{2,1,0:T(8,128)} reduce(f32[2,128,2,768]{3,2,1,0:T(2,128)} %reshape.148, f32[]{:T(128)} %constant.82.clone.1), dimensions={2}, to_apply=%region_0.1 | reduce | flops 196608 | bytes 2359300 | tf_op jit(solution)/shard_map/reduce_sum | solution.py:86
  26.6 2.8 %fusion.41 = (f32[2,128]{1,0:T(2,128)S(1)}, bf16[2,128,1536]{2,1,0:T(8,128)(2,1)S(1)}) fusion(bf16[768,1536]{1,0:T(8,128)(2,1)} %param.20, f32[2,128,768]{2,1,0:T(8,128)} %reduce_sum.36), kind=kOutput, calls=%fused_computation.43 | convolution fusion | flops 605945600 | bytes 3933184 | tf_op jit(solution)/shard_map/brc,cd->brd/dot_general | solution.py:87
  43.0 10.0 %all-to-all-start = ((bf16[32,2,16,896]{3,2,1,0:T(8,128)(2,1)}), bf16[32,2,16,896]{3,2,1,0:T(8,128)(2,1)}, u32[]{:S(2)}, u32[]{:S(2)}) async-start(bf16[32,2,16,896]{3,2,1,0:T(8,128)(2,1)} %bitcast.159), calls=%async_computation | async-start | bytes 3670016 | tf_op jit(solution)/shard_map/all_to_all | solution.py:74
  53.0 28.5 %all-to-all-done = bf16[32,2,16,896]{3,2,1,0:T(8,128)(2,1)} async-done(((bf16[32,2,16,896]{3,2,1,0:T(8,128)(2,1)}), bf16[32,2,16,896]{3,2,1,0:T(8,128)(2,1)}, u32[]{:S(2)}, u32[]{:S(2)}) %all-to-all-start) | async-done | bytes 1835040 | tf_op jit(solution)/shard_map/all_to_all | solution.py:74
  86.0 2.3 %copy.55 = bf16[256,1536]{0,1:T(8,128)(2,1)} copy(bf16[256,1536]{1,0:T(8,128)(2,1)} %bitcast.169) | data formatting | bytes 1572864 | tf_op jit(solution)/shard_map/reshape;squeeze | solution.py:105
  91.4 4.2 %convolution_convert_fusion = bf16[768,1536]{1,0:T(8,128)(2,1)} fusion(bf16[256,1536]{1,0:T(8,128)(2,1)} %collective-permute-done.3, bf16[256,1536]{1,0:T(8,128)(2,1)} %bitcast.28, bf16[768,256]{1,0:T(8,128)(2,1)S(1)} %bitcast.173, bf16[768,256]{1,0:T(8,128)(2,1)S(1)} %bitcast.171), kind=kOutput, calls=%fused_computation.25 | convolution fusion | flops 1213857792 | bytes 4718592 | tf_op jit(solution)/shard_map/dot_general | solution.py:16
  95.6 4.9 %all-to-all-start.1 = ((bf16[32,24,1536]{2,1,0:T(8,128)(2,1)}), bf16[32,24,1536]{2,1,0:T(8,128)(2,1)}, u32[]{:S(2)}, u32[]{:S(2)}) async-start(bf16[32,24,1536]{2,1,0:T(8,128)(2,1)} %bitcast.167), calls=%async_computation.1 | async-start | bytes 4718592 | tf_op jit(solution)/shard_map/all_to_all | solution.py:124
  100.6 3.0 %fusion.55 = bf16[2,128,1024]{2,1,0:T(8,128)(2,1)} fusion(bf16[1536,1024]{1,0:T(8,128)(2,1)S(1)} %copy-done, bf16[2,128,1536]{2,1,0:T(8,128)(2,1)} %copy-done.2, f32[1536]{0:T(1024)S(1)} %copy-done.10, f32[2,128]{1,0:T(2,128)S(1)} %copy-done.6), kind=kOutput, calls=%fused_computation.58 | convolution fusion | flops 807141376 | bytes 4463616 | tf_op jit(solution)/shard_map/brd,de->bre/dot_general | solution.py:101
  103.6 2.6 %fusion.36 = f32[256,1536]{1,0:T(8,128)S(1)} fusion(bf16[2,1536,768]{2,1,0:T(8,128)(2,1)} %param.28, bf16[256,1536]{1,0:T(8,128)(2,1)} %bitcast.28), kind=kOutput, calls=%fused_computation.33 | convolution fusion | flops 603979776 | bytes 4325376 | tf_op jit(solution)/shard_map/dot_general | solution.py:16
  106.2 3.5 %fusion.34 = bf16[256,1536]{1,0:T(8,128)(2,1)} fusion(f32[256,1536]{1,0:T(8,128)S(1)} %fusion.36, bf16[2,1536,768]{2,1,0:T(8,128)(2,1)} %param.28, bf16[256,1536]{1,0:T(8,128)(2,1)} %bitcast.28), kind=kOutput, calls=%fused_computation.30 | convolution fusion | flops 604766208 | bytes 5111808 | tf_op jit(solution)/shard_map/dot_general | solution.py:16
  109.7 27.5 %all-to-all-done.1 = bf16[32,24,1536]{2,1,0:T(8,128)(2,1)} async-done(((bf16[32,24,1536]{2,1,0:T(8,128)(2,1)}), bf16[32,24,1536]{2,1,0:T(8,128)(2,1)}, u32[]{:S(2)}, u32[]{:S(2)}) %all-to-all-start.1) | async-done | bytes 2359328 | tf_op jit(solution)/shard_map/all_to_all | solution.py:124
  139.9 45.6 %conditional.1 = (bf16[1,2,128,1536]{3,2,1,0:T(8,128)(2,1)}) conditional(s32[]{:T(128)} %convert_element_type.86, bf16[2,128,1536]{2,1,0:T(8,128)(2,1)} %copy-done.2, (bf16[2,128,1536]{2,1,0:T(8,128)(2,1)}, f32[8]{0:T(128)S(1)}, bf16[2,4096,256]{2,1,0:T(8,128)(2,1)}, bf16[2,128,1024]{2,1,0:T(8,128)(2,1)}, bf16[1024,1536]{1,0:T(8,128)(2,1)}) %tuple.60), branch_computations={%region_2.3_spmd, %region_3.8_spmd} | conditional | flops 4057211904 | bytes 15999285 | solution.py:156
  140.0 41.5 %while.12 = (s32[]{:T(128)}, bf16[2,128,1024]{1,2,0:T(8,128)(2,1)}, bf16[2,4096,256]{2,1,0:T(8,128)(2,1)}, bf16[2,128,1024]{2,1,0:T(8,128)(2,1)}, f32[8]{0:T(128)S(1)}, /*index=5*/s32[]{:T(128)}) while((s32[]{:T(128)}, bf16[2,128,1024]{1,2,0:T(8,128)(2,1)}, bf16[2,4096,256]{2,1,0:T(8,128)(2,1)}, bf16[2,128,1024]{2,1,0:T(8,128)(2,1)}, ...), condition=%wide.region_7.7_spmd, body=%wide.region_4.6_spmd.sunk | while | flops 3250725888 | bytes 10756277 | solution.py:150
  141.8 3.1 %dynamic-slice_bitcast_fusion.3 = bf16[4096,256]{1,0:T(8,128)(2,1)} fusion(bf16[2,4096,256]{2,1,0:T(8,128)(2,1)} %get-tuple-element.152, s32[]{:T(128)S(6)} %copy.65), kind=kLoop, calls=%fused_computation.10.clone.1 | loop fusion | bytes 4194308 | tf_op jit(solution)/shard_map/cond/branch_1_fun/while/body/jit(dynamic_index_in_dim)/squeeze | solution.py:150
  144.9 6.1 %fusion.109 = f32[8,128]{1,0:T(8,128)S(1)} fusion(f32[8]{0:T(128)S(1)} %get-tuple-element.154, bf16[128,8,128]{0,2,1:T(8,128)(2,1)S(1)} %bitcast.163, bf16[4096,256]{1,0:T(8,128)(2,1)} %dynamic-slice_bitcast_fusion.3), kind=kOutput, calls=%fused_computation.110.clone.1 | convolution fusion | flops 1086328832 | bytes 1314848 | tf_op jit(solution)/shard_map/cond/branch_1_fun/while/body/eval_jaxpr/sub | solution.py:142
  151.0 9.0 %fusion.110 = bf16[128,8,128]{2,0,1:T(8,128)(2,1)S(1)} fusion(f32[8,128]{1,0:T(8,128)S(1)} %fusion.109, bf16[4096,256]{1,0:T(8,128)(2,1)} %dynamic-slice_bitcast_fusion.3, f32[8]{0:T(128)S(1)} %get-tuple-element.154, bf16[128,8,128]{0,2,1:T(8,128)(2,1)} %bitcast.162), kind=kOutput, calls=%fused_computation.11.clone.1 | convolution fusion | flops 2164397056 | bytes 2625568 | tf_op jit(solution)/shard_map/cond/branch_1_fun/while/body/eval_jaxpr/hqk,ke->qhe/dot_general | solution.py:144
  162.5 3.1 %dynamic-slice_bitcast_fusion.3 = bf16[4096,256]{1,0:T(8,128)(2,1)} fusion(bf16[2,4096,256]{2,1,0:T(8,128)(2,1)} %get-tuple-element.152, s32[]{:T(128)S(6)} %copy.65), kind=kLoop, calls=%fused_computation.10.clone.1 | loop fusion | bytes 4194308 | tf_op jit(solution)/shard_map/cond/branch_1_fun/while/body/jit(dynamic_index_in_dim)/squeeze | solution.py:150
  165.6 6.1 %fusion.109 = f32[8,128]{1,0:T(8,128)S(1)} fusion(f32[8]{0:T(128)S(1)} %get-tuple-element.154, bf16[128,8,128]{0,2,1:T(8,128)(2,1)S(1)} %bitcast.163, bf16[4096,256]{1,0:T(8,128)(2,1)} %dynamic-slice_bitcast_fusion.3), kind=kOutput, calls=%fused_computation.110.clone.1 | convolution fusion | flops 1086328832 | bytes 1314848 | tf_op jit(solution)/shard_map/cond/branch_1_fun/while/body/eval_jaxpr/sub | solution.py:142
  171.7 9.0 %fusion.110 = bf16[128,8,128]{2,0,1:T(8,128)(2,1)S(1)} fusion(f32[8,128]{1,0:T(8,128)S(1)} %fusion.109, bf16[4096,256]{1,0:T(8,128)(2,1)} %dynamic-slice_bitcast_fusion.3, f32[8]{0:T(128)S(1)} %get-tuple-element.154, bf16[128,8,128]{0,2,1:T(8,128)(2,1)} %bitcast.162), kind=kOutput, calls=%fused_computation.11.clone.1 | convolution fusion | flops 2164397056 | bytes 2625568 | tf_op jit(solution)/shard_map/cond/branch_1_fun/while/body/eval_jaxpr/hqk,ke->qhe/dot_general | solution.py:144
  181.5 4.1 %fusion.29 = bf16[1,2,128,1536]{3,2,1,0:T(8,128)(2,1)} fusion(bf16[2,128,1024]{1,2,0:T(8,128)(2,1)} %get-tuple-element.63, bf16[1024,1536]{1,0:T(8,128)(2,1)} %get-tuple-element.72, bf16[2,128,1536]{2,1,0:T(8,128)(2,1)} %get-tuple-element.59), kind=kOutput, calls=%fused_computation.22 | convolution fusion | flops 806486016 | bytes 5242880 | tf_op jit(solution)/shard_map/cond/branch_1_fun/brh,hd->brd/dot_general | solution.py:151
  (74 shorter events, 33.1 us)
Async XLA Ops:
  7.2 93.4 %copy-start = (bf16[1536,1024]{1,0:T(8,128)(2,1)S(1)}, bf16[1536,1024]{1,0:T(8,128)(2,1)}, u32[]{:S(2)}) copy-start(bf16[1536,1024]{1,0:T(8,128)(2,1)} %param.22) | copy-start | bytes 9437188
  7.2 132.8 %all-gather.2.cloned.1.call-start = ((), (), s32[]{:S(2)}) async-start(), calls=%async_computation.2 | async-start | bytes 4325376 | tf_op jit(solution)/shard_map/all_gather | solution.py:100
  8.1 5.5 %collective-permute-start = (bf16[2,2,768]{2,1,0:T(2,128)(2,1)S(1)}, bf16[2,2,768]{2,1,0:T(2,128)(2,1)S(1)}, u32[]{:S(2)}, u32[]{:S(2)}) collective-permute-start(bf16[2,2,768]{2,1,0:T(2,128)(2,1)S(1)} %get-tuple-element.102), channel_id=1, source_target_pairs={{0,2},{2,4},{4,6},{6,8},{8,10},{10,12},{12,14},{14,16},{16,18},{18... | collective-permute-start | bytes 18440 | tf_op jit(solution)/shard_map/ppermute | solution.py:23
  9.9 3.8 %copy-start.7 = (bf16[2,256,768]{2,1,0:T(8,128)(2,1)S(1)}, bf16[2,256,768]{2,1,0:T(8,128)(2,1)}, u32[]{:S(2)}) copy-start(bf16[2,256,768]{2,1,0:T(8,128)(2,1)} %param.18) | copy-start | bytes 2359300
  9.9 5.8 %collective-permute-start.1 = (bf16[2,2,768]{2,1,0:T(2,128)(2,1)S(1)}, bf16[2,2,768]{2,1,0:T(2,128)(2,1)S(1)}, u32[]{:S(2)}, u32[]{:S(2)}) collective-permute-start(bf16[2,2,768]{2,1,0:T(2,128)(2,1)S(1)} %get-tuple-element.101), channel_id=1, source_target_pairs={{2,0},{4,2},{6,4},{8,6},{10,8},{12,10},{14,12},{16,14},{18,16},{20... | collective-permute-start | bytes 18440 | tf_op jit(solution)/shard_map/ppermute | solution.py:24
  26.6 4.3 %copy-start.8 = (bf16[1536,256]{1,0:T(8,128)(2,1)S(1)}, bf16[1536,256]{1,0:T(8,128)(2,1)}, u32[]{:S(2)}) copy-start(bf16[1536,256]{1,0:T(8,128)(2,1)} %param.23) | copy-start | bytes 2359300
  26.6 4.3 %copy-start.9 = (f32[1536]{0:T(1024)S(1)}, f32[1536]{0:T(1024)}, u32[]{:S(2)}) copy-start(f32[1536]{0:T(1024)} %param.21) | copy-start | bytes 18436
  29.4 0.9 copy-start.2
  29.4 2.6 %copy-start.4 = (s32[1,2,1,32,16]{3,4,2,1,0:T(8,128)S(1)}, s32[1,2,1,32,16]{3,4,2,1,0:T(8,128)}, u32[]{:S(2)}) copy-start(s32[1,2,1,32,16]{3,4,2,1,0:T(8,128)} %param.29) | copy-start | bytes 12292
  29.5 11.2 %copy-start.3 = (bf16[1,2,128,768]{3,2,1,0:T(8,128)(2,1)S(1)}, bf16[1,2,128,768]{3,2,1,0:T(8,128)(2,1)}, u32[]{:S(2)}) copy-start(bf16[1,2,128,768]{3,2,1,0:T(8,128)(2,1)} %param.27) | copy-start | bytes 1179652
  30.3 0.6 copy-start.5
  43.0 38.5 %all-to-all-start = ((bf16[32,2,16,896]{3,2,1,0:T(8,128)(2,1)}), bf16[32,2,16,896]{3,2,1,0:T(8,128)(2,1)}, u32[]{:S(2)}, u32[]{:S(2)}) async-start(bf16[32,2,16,896]{3,2,1,0:T(8,128)(2,1)} %bitcast.159), calls=%async_computation | async-start | bytes 3670016 | tf_op jit(solution)/shard_map/all_to_all | solution.py:74
  86.0 5.4 %collective-permute-start.3 = (bf16[256,1536]{1,0:T(8,128)(2,1)}, bf16[256,1536]{1,0:T(8,128)(2,1)}, u32[]{:S(2)}, u32[]{:S(2)}) collective-permute-start(bf16[256,1536]{1,0:T(8,128)(2,1)} %bitcast.28), channel_id=1, source_target_pairs={{0,2},{2,0},{1,3},{3,1},{4,6},{6,4},{5,7},{7,5},{8,10},{10,8},{9,1... | collective-permute-start | bytes 2359304 | tf_op jit(solution)/shard_map/ppermute | solution.py:121
  89.5 1.9 %collective-permute-start.2 = (bf16[16,48,256]{2,1,0:T(8,128)(2,1)S(1)}, bf16[16,48,256]{2,1,0:T(8,128)(2,1)S(1)}, u32[]{:S(2)}, u32[]{:S(2)}) collective-permute-start(bf16[16,48,256]{2,1,0:T(8,128)(2,1)S(1)} %get-tuple-element.100), channel_id=1, source_target_pairs={{0,2},{2,0},{1,3},{3,1},{4,6},{6,4},{5,7},{7,5},{8,10},{10,8},{9,1... | collective-permute-start | bytes 1179656 | tf_op jit(solution)/shard_map/ppermute | solution.py:110
  95.6 5.0 %copy-start.6 = (f32[2,128]{1,0:T(2,128)S(1)}, f32[2,128]{1,0:T(2,128)}, u32[]{:S(2)}) copy-start(f32[2,128]{1,0:T(2,128)} %copy-done.5) | copy-start | bytes 3076
  95.6 5.0 %copy-start.10 = (f32[1536]{0:T(1024)S(1)}, f32[1536]{0:T(1024)}, u32[]{:S(2)}) copy-start(f32[1536]{0:T(1024)} %param.21) | copy-start | bytes 18436
  95.6 41.6 %all-to-all-start.1 = ((bf16[32,24,1536]{2,1,0:T(8,128)(2,1)}), bf16[32,24,1536]{2,1,0:T(8,128)(2,1)}, u32[]{:S(2)}, u32[]{:S(2)}) async-start(bf16[32,24,1536]{2,1,0:T(8,128)(2,1)} %bitcast.167), calls=%async_computation.1 | async-start | bytes 4718592 | tf_op jit(solution)/shard_map/all_to_all | solution.py:124
  109.7 30.3 %copy-start.11 = (f32[8]{0:T(128)S(1)}, f32[8]{0:T(128)}, u32[]{:S(2)}) copy-start(f32[8]{0:T(128)} %param.25) | copy-start | bytes 100
  141.8 3.1 %copy-start.1 = (bf16[1,128,1024]{1,2,0:T(8,128)(2,1)S(1)}, bf16[1,128,1024]{1,2,0:T(8,128)(2,1)}, u32[]{:S(2)}) copy-start(bf16[1,128,1024]{1,2,0:T(8,128)(2,1)} %copy.61) | copy-start | bytes 786436 | tf_op jit(solution)/shard_map/cond/branch_1_fun/while
  162.5 3.1 %copy-start.1 = (bf16[1,128,1024]{1,2,0:T(8,128)(2,1)S(1)}, bf16[1,128,1024]{1,2,0:T(8,128)(2,1)}, u32[]{:S(2)}) copy-start(bf16[1,128,1024]{1,2,0:T(8,128)(2,1)} %copy.61) | copy-start | bytes 786436 | tf_op jit(solution)/shard_map/cond/branch_1_fun/while
Sparse Core Ops, SparseCore 0:
  32.1 58.1 all-gather.1

commit v2 on v1

v2 whole, which is shorter than its diff:
```python
import functools
import math

import jax
import jax.numpy as jnp
from jax import lax
from jax.experimental import pallas as pl
from jax.experimental.pallas import tpu as pltpu
from jax.sharding import Mesh
from jax.sharding import PartitionSpec as P

DILATION_STEP = 2
SEQ = ("y", "x", "core")
F32 = jnp.float32
BF16 = jnp.bfloat16
I32 = jnp.int32
TAG = 128
NT = (((1,), (1,)), ((), ()))
TN = (((0,), (0,)), ((), ()))
VMEM = pl.BlockSpec(memory_space=pltpu.VMEM)
SMEM = pl.BlockSpec(memory_space=pltpu.SMEM)
ANY = pl.BlockSpec(memory_space=pl.ANY)


def dot(a, b, dims=(((1,), (0,)), ((), ()))):
    return lax.dot_general(a, b, dims, preferred_element_type=F32)


def params(mib):
    return pltpu.CompilerParams(vmem_limit_bytes=mib << 20)


def cost(flops, nbytes):
    return pl.CostEstimate(flops=int(flops), bytes_accessed=int(nbytes), transcendentals=0)


def pick_kernel(ids_ref, lines_ref, counts_ref, cot_ref, out_ref):
    batch, shards, slots = ids_ref.shape
    junc, embed = cot_ref.shape[1:]
    n = shards * slots
    owner = lax.broadcasted_iota(I32, (n, shards), 0) // slots
    spread = owner == lax.broadcasted_iota(I32, (n, shards), 1)
    spread16 = spread.astype(F32).astype(BF16)
    slot = lax.broadcasted_iota(I32, (n, slots), 0) % slots
    own = slot == lax.broadcasted_iota(I32, (n, slots), 1)

    def column(values):
        wide = dot(spread16, values.astype(F32).astype(BF16))
        return jnp.sum(jnp.where(own, wide, 0.0), axis=1, keepdims=True)

    for b in range(batch):
        ids = ids_ref[b]
        junction = column(ids % junc)
        code = column(ids // junc) * float(junc) + column(lines_ref[b])
        count = jnp.sum(
            jnp.where(spread, counts_ref[b : b + 1, :].astype(F32), 0.0), axis=1, keepdims=True
        )
        valid = slot[:, :1].astype(F32) < count
        junction = jnp.where(valid, junction, -1.0).astype(I32)
        code = jnp.where(valid, code, -1.0)
        onehot = (junction == lax.broadcasted_iota(I32, (n, junc), 1)).astype(F32).astype(BF16)
        picked = dot(onehot, cot_ref[b]).astype(BF16)
        out_ref[:, b, :, :embed] = picked.reshape(shards, slots, embed)
        tags = jnp.broadcast_to(code, (n, TAG)).astype(BF16)
        out_ref[:, b, :, embed:] = tags.reshape(shards, slots, TAG)


def pick(ids, lines, counts, cotangent):
    batch, shards, slots = ids.shape
    embed = cotangent.shape[2]
    return pl.pallas_call(
        pick_kernel,
        out_shape=jax.ShapeDtypeStruct((shards, batch, slots, embed + TAG), BF16),
        in_specs=[VMEM] * 4,
        out_specs=VMEM,
        compiler_params=params(32),
        cost_estimate=cost(2 * 10**8, 3 * 10**6),
        name="pick",
    )(ids, lines, counts, cotangent)


def ends_kernel(arrived_ref, out_ref):
    shards, batch, slots, wide = arrived_ref.shape
    embed = wide - TAG
    n = shards * slots
    rows = out_ref.shape[0] // batch
    for b in range(batch):
        data = arrived_ref[:, b, :, :embed].reshape(n, embed)
        tag = arrived_ref[:, b, :, embed:].reshape(n, TAG).astype(F32)
        for kind in range(2):
            target = lax.broadcasted_iota(I32, (n, rows), 1) + kind * rows
            onehot = (tag == target.astype(F32)).astype(F32).astype(BF16)
            out_ref[b * rows : (b + 1) * rows, kind * embed : (kind + 1) * embed] = dot(
                onehot, data, TN
            ).astype(BF16)


def make_ends(arrived, rows):
    batch, embed = arrived.shape[1], arrived.shape[3] - TAG
    return pl.pallas_call(
        ends_kernel,
        out_shape=jax.ShapeDtypeStruct((batch * rows, 2 * embed), BF16),
        in_specs=[VMEM],
        out_specs=VMEM,
        compiler_params=params(32),
        cost_estimate=cost(4 * 10**8, 3 * 10**6),
        name="ends",
    )(arrived)


def turn_kernel(core_ref, lines_ref, mine_ref, other_ref):
    blocks, part, n = mine_ref.shape
    first = core_ref[0] == 0
    turned = lines_ref[...].T.reshape(blocks, 2, part, n)
    low, high = turned[:, 0], turned[:, 1]
    mine_ref[...] = jnp.where(first, low, high)
    other_ref[...] = jnp.where(first, high, low)


def turn(core, lines, blocks):
    n, width = lines.shape
    half = jax.ShapeDtypeStruct((blocks, width // (2 * blocks), n), BF16)
    return pl.pallas_call(
        turn_kernel,
        out_shape=(half, half),
        in_specs=[SMEM, VMEM],
        out_specs=(VMEM, VMEM),
        compiler_params=params(32),
        cost_estimate=cost(10**6, 2 * 10**6),
        name="turn",
    )(core.reshape(1), lines)


def partial_kernel(mine_ref, other_ref, ends_ref, ends_other_ref, out_ref):
    rows, n = mine_ref.shape[0] * mine_ref.shape[1], mine_ref.shape[2]
    total = dot(mine_ref[...].reshape(rows, n), ends_ref[...])
    total = total + dot(other_ref[...].reshape(rows, n), ends_other_ref[...])
    out_ref[...] = total.astype(BF16).reshape(out_ref.shape)


def partial_grad(mine, other, ends, ends_other, pieces):
    rows, width = mine.shape[0] * mine.shape[1], ends.shape[1]
    return pl.pallas_call(
        partial_kernel,
        out_shape=jax.ShapeDtypeStruct((pieces, rows // pieces, width), BF16),
        in_specs=[VMEM] * 4,
        out_specs=VMEM,
        compiler_params=params(40),
        cost_estimate=cost(1.2 * 10**9, 5 * 10**6),
        name="partial_grad",
    )(mine, other, ends, ends_other)


def encoder_kernel(
    x_ref,
    low_ref,
    high_ref,
    gain_ref,
    taps_hbm,
    merge_hbm,
    look_hbm,
    ask_hbm,
    rows_ref,
    query_ref,
    keyval_ref,
    taps,
    merge,
    look,
    ask,
    pad,
    hidden,
    sems,
):
    copies = [
        pltpu.make_async_copy(source, target, sems.at[i])
        for i, (source, target) in enumerate(
            ((taps_hbm, taps), (merge_hbm, merge), (look_hbm, look), (ask_hbm, ask))
        )
    ]
    for copy in copies:
        copy.start()
    batch, cells, chans = x_ref.shape
    extent = low_ref.shape[1]
    base = 8
    for b in range(batch):
        pad[b, base - extent : base, :] = low_ref[b].astype(F32)
        pad[b, base : base + cells, :] = x_ref[b].astype(F32)
        pad[b, base + cells : base + cells + extent, :] = high_ref[b].astype(F32)
    copies[0].wait()
    for b in range(batch):
        total = dot(x_ref[b], taps[1])
        total += dot(pad[b, base - extent : base - extent + cells, :].astype(BF16), taps[0])
        total += dot(pad[b, base + extent : base + extent + cells, :].astype(BF16), taps[2])
        total = pad[b, base : base + cells, :] + jax.nn.gelu(total)
        for j in range(hidden.shape[0]):
            hidden[j, b * cells : (b + 1) * cells, :] = total[:, j * 128 : (j + 1) * 128]
    n = batch * cells // 2
    pooled = jnp.concatenate(
        [
            ((hidden[j, pl.ds(0, n, 2), :] + hidden[j, pl.ds(1, n, 2), :]) * 0.5).astype(BF16)
            for j in range(hidden.shape[0])
        ],
        axis=1,
    )
    copies[1].wait()
    rows = dot(pooled, merge[...]).astype(BF16)
    rows_ref[...] = rows
    wide = rows.astype(F32)
    scale = lax.rsqrt(jnp.mean(wide * wide, axis=-1, keepdims=True) + 1e-06)
    normed = (wide * scale * gain_ref[...]).astype(BF16)
    copies[2].wait()
    keyval_ref[...] = dot(normed, look[...]).astype(BF16)
    copies[3].wait()
    query_ref[...] = dot(normed, ask[...]).astype(BF16)


def encode(x, low, high, gain, taps, merge, look, ask):
    batch, cells, chans = x.shape
    n = batch * cells // 2
    width = merge.shape[1]
    return pl.pallas_call(
        encoder_kernel,
        out_shape=(
            jax.ShapeDtypeStruct((n, width), BF16),
            jax.ShapeDtypeStruct((n, ask.shape[1]), BF16),
            jax.ShapeDtypeStruct((n, look.shape[1]), BF16),
        ),
        in_specs=[VMEM] * 4 + [ANY] * 4,
        out_specs=(VMEM,) * 3,
        scratch_shapes=[
            pltpu.VMEM(taps.shape, BF16),
            pltpu.VMEM(merge.shape, BF16),
            pltpu.VMEM(look.shape, BF16),
            pltpu.VMEM(ask.shape, BF16),
            pltpu.VMEM((batch, cells + 16, chans), F32),
            pltpu.VMEM((chans // 128, batch * cells, 128), F32),
            pltpu.SemaphoreType.DMA((4,)),
        ],
        compiler_params=params(48),
        cost_estimate=cost(3.4 * 10**9, 12 * 10**6),
        name="encode",
    )(x, low, high, gain.reshape(1, width), taps, merge, look, ask)


def trunk_kernel(
    phase_ref, logit_ref, query_ref, keyval_ref, rows_ref, exit_ref, out_ref, attended
):
    b, pair = pl.program_id(0), pl.program_id(1)
    pairs = pl.num_programs(1)
    lane = keyval_ref.shape[2] // 2
    rows = query_ref.shape[0]
    last = jnp.logical_and(b == pl.num_programs(0) - 1, pair == pairs - 1)
    on = phase_ref[0] == 1

    @pl.when(on)
    def _():
        query = jnp.concatenate([query_ref[:, :lane], query_ref[:, lane:]], axis=0)
        scores = dot(query, keyval_ref[0, :, :lane], NT)
        upper = lax.broadcasted_iota(I32, (2 * rows, 1), 0) < rows
        factor = jnp.where(upper, logit_ref[2 * pair], logit_ref[2 * pair + 1])
        top = jnp.max(scores, axis=-1, keepdims=True)
        expo = jnp.exp2(scores * factor - top * factor)
        total = jnp.sum(expo, axis=-1, keepdims=True)
        mixed = dot(expo.astype(BF16), keyval_ref[0, :, lane:])
        mixed = (mixed / total).astype(BF16)
        attended[pair, pl.ds(pl.multiple_of(b * rows, rows), rows), :lane] = mixed[:rows]
        attended[pair, pl.ds(pl.multiple_of(b * rows, rows), rows), lane:] = mixed[rows:]

    @pl.when(jnp.logical_and(on, last))
    def _():
        out = rows_ref[...].astype(F32)
        for i in range(attended.shape[0]):
            out += dot(attended[i], exit_ref[2 * i * lane : 2 * (i + 1) * lane, :])
        out_ref[...] = out.astype(BF16)

    @pl.when(jnp.logical_and(jnp.logical_not(on), last))
    def _():
        out_ref[...] = rows_ref[...]


def trunk(phase, logit, queries, gathered, encoded, exit_projector):
    batch, keys, both = gathered.shape
    n, width = encoded.shape
    rows = n // batch
    pairs = queries.shape[1] // both
    return pl.pallas_call(
        trunk_kernel,
        grid=(batch, pairs),
        out_shape=jax.ShapeDtypeStruct((n, width), BF16),
        in_specs=[
            SMEM,
            SMEM,
            pl.BlockSpec((rows, both), lambda b, p: (b, p)),
            pl.BlockSpec((1, keys, both), lambda b, p: (b, 0, 0)),
            pl.BlockSpec((n, width), lambda b, p: (0, 0)),
            pl.BlockSpec(exit_projector.shape, lambda b, p: (0, 0)),
        ],
        out_specs=pl.BlockSpec((n, width), lambda b, p: (0, 0)),
        scratch_shapes=[pltpu.VMEM((pairs, n, both), BF16)],
        compiler_params=params(56),
        cost_estimate=cost(5.2 * 10**9, 9 * 10**6),
        name="trunk",
    )(phase.reshape(1), logit, queries, gathered, encoded, exit_projector)


def halo(block, width):
    count = lax.axis_size(SEQ)
    forward = [(i, i + 1) for i in range(count - 1)]
    backward = [(b, a) for a, b in forward]
    low = lax.ppermute(block[:, -width:], SEQ, forward)
    high = lax.ppermute(block[:, :width], SEQ, backward)
    return low, high


def body(
    bin_activations,
    spaced_filter_coefs,
    merged_bin_projector,
    backbone_rms_gain,
    asking_projector,
    common_lookup_projector,
    attention_exit_projector,
    lane_logit_factor,
    splice_readout_lines,
    couple_embedding_cotangent,
    splice_site_projector,
    site_locator_code,
    site_local_line,
    filled_slot_totals,
):
    phase = lax.axis_index("phase")
    core = lax.axis_index("core")
    batch, cells, chans = bin_activations.shape
    rows = cells // 2
    width = merged_bin_projector.shape[1]
    extent = DILATION_STEP * (spaced_filter_coefs.shape[0] // 2)
    lane = common_lookup_projector.shape[1] // 2
    embed = couple_embedding_cotangent.shape[3]
    shards = site_locator_code.shape[3]
    swap = [(0, 1), (1, 0)]

    low, high = halo(bin_activations, extent)
    payload = pick(
        site_locator_code[0, :, 0],
        site_local_line[0, :, 0],
        filled_slot_totals[0, :, 0],
        couple_embedding_cotangent[0],
    )
    arrived = lax.all_to_all(payload, SEQ, 0, 0, tiled=True)

    encoded, queries, keyvals = encode(
        bin_activations,
        low,
        high,
        backbone_rms_gain,
        spaced_filter_coefs,
        merged_bin_projector,
        common_lookup_projector,
        asking_projector,
    )
    gathered = lax.all_gather(keyvals.reshape(batch, rows, 2 * lane), SEQ, axis=1, tiled=True)

    portion = splice_readout_lines[0].reshape(batch * rows, width)
    mine, other = turn(core, portion, shards // 2)
    other = lax.ppermute(other, "core", swap)

    ends = make_ends(arrived, rows)
    ends_other = lax.ppermute(ends, "core", swap)
    partial = partial_grad(mine, other, ends, ends_other, shards)
    pieces = lax.all_to_all(partial, ("y", "x", "dp"), 0, 0, tiled=True)

    row_grad = (
        dot(ends[:, :embed], splice_site_projector[0], NT)
        + dot(ends[:, embed:], splice_site_projector[1], NT)
    ).astype(BF16)
    row_grad = row_grad.reshape(batch, rows, width)[None]

    logit = lane_logit_factor * (math.log2(math.e) / math.sqrt(lane))
    phase_rows = trunk(phase, logit, queries, gathered, encoded, attention_exit_projector)
    phase_rows = phase_rows.reshape(batch, rows, width)[None]

    summed = jnp.sum(pieces.astype(F32), axis=0)
    weight_grad = summed.reshape(-1, 2, embed).transpose(1, 0, 2)[None]
    return (phase_rows, row_grad, weight_grad)


def solution(mesh):
    shape = dict(mesh.shape)
    side = math.isqrt(shape["seq"] // 2)
    fine = Mesh(
        mesh.devices.reshape(shape["phase"], side, side, 2, shape["dp"]),
        ("phase", "y", "x", "core", "dp"),
    )
    return jax.shard_map(
        body,
        mesh=fine,
        in_specs=(
            P("dp", SEQ, None),
            P(),
            P(),
            P(),
            P(),
            P(),
            P(),
            P(),
            P("phase", "dp", SEQ, None),
            P("phase", "dp", SEQ, None),
            P(),
            P("phase", "dp", SEQ, None, None),
            P("phase", "dp", SEQ, None, None),
            P("phase", "dp", SEQ, None),
        ),
        out_specs=(
            P("phase", "dp", SEQ, None),
            P("phase", "dp", SEQ, None),
            P("phase", None, SEQ + ("dp",), None),
        ),
        check_vma=False,
    )
```

time: 194 us -> 148 us (0.76)
  the two profiles are of different devices: /device:TPU:64 before, /device:TPU:73 now
where the time goes in v2:
time: 148 us
  waiting for transfers between devices  36.7 us (25%)
  blocking collectives  34.9 us (24%)
  Pallas kernels  34.4 us (23%)
  between operations  14.2 us (10%)
  starting transfers between devices  12.4 us (8%)
  local copies, waits for them, and re-layouts  8.03 us (5%)
  matrix products  6.01 us (4%)
    all_to_all x1, blocking collectives, body(): arrived = lax.all_to_all(payload, SEQ, 0, 0, tiled=True)  34.9 us
    all_to_all x1, waiting for transfers between devices, body(): pieces = lax.all_to_all(partial, ('y', 'x', 'dp'), 0, 0, tiled=True)  32.3 us
    pallas_call x1, Pallas kernels, trunk(): pl.pallas_call(trunk_kernel, grid=(batch, pairs), out_shape=jax.ShapeDtyp...  21.3 us
    pallas_call x1, Pallas kernels, encode(): pl.pallas_call(encoder_kernel, out_shape=(jax.ShapeDtypeStruct((n, width)...  8.39 us
    unnamed x25, local copies, waits for them, and re-layouts  6.46 us
    all_to_all x1, starting transfers between devices, body(): pieces = lax.all_to_all(partial, ('y', 'x', 'dp'), 0, 0, tiled=True)  6.14 us
    dot_general x2, matrix products, dot(): return lax.dot_general(a, b, dims, preferred_element_type=F32)  6.01 us
    ppermute x1, starting transfers between devices, halo(): low = lax.ppermute(block[:, -width:], SEQ, forward)  3.68 us
  transfers between devices with their start and end apart: 6, of which 3 were waited for; matrix products, arithmetic and copies ran while one was open for 6% of the time, Pallas kernels for 3%

profile of v2, /device:TPU:73, one launch (start us, length us, event | category | flops | bytes accessed | tf_op | source)
XLA Modules:
  0.0 147.5 jit_solution(2369464264219661534)
XLA Ops:
  7.2 0.8 fusion.8
  8.0 3.7 %collective-permute-start = (bf16[2,2,768]{2,1,0:T(2,128)(2,1)S(1)}, bf16[2,2,768]{2,1,0:T(2,128)(2,1)S(1)}, u32[]{:S(2)}, u32[]{:S(2)}) collective-permute-start(bf16[2,2,768]{2,1,0:T(2,128)(2,1)S(1)} %get-tuple-element.17), channel_id=1, source_target_pairs={{0,2},{2,4},{4,6},{6,8},{8,10},{10,12},{12,14},{14,16},{16,18},{18... | collective-permute-start | bytes 18440 | tf_op jit(solution)/shard_map/ppermute | solution.py:310
  11.7 1.9 %collective-permute-start.1 = (bf16[2,2,768]{2,1,0:T(2,128)(2,1)S(1)}, bf16[2,2,768]{2,1,0:T(2,128)(2,1)S(1)}, u32[]{:S(2)}, u32[]{:S(2)}) collective-permute-start(bf16[2,2,768]{2,1,0:T(2,128)(2,1)S(1)} %get-tuple-element.16), channel_id=1, source_target_pairs={{2,0},{4,2},{6,4},{8,6},{10,8},{12,10},{14,12},{16,14},{18,16},{20... | collective-permute-start | bytes 18440 | tf_op jit(solution)/shard_map/ppermute | solution.py:311
  13.6 0.7 reshape.22.gain_ref
  14.3 2.3 %collective-permute-done.1.high_ref = bf16[2,2,768]{2,1,0:T(2,128)(2,1)S(1)} collective-permute-done((bf16[2,2,768]{2,1,0:T(2,128)(2,1)S(1)}, bf16[2,2,768]{2,1,0:T(2,128)(2,1)S(1)}, u32[]{:S(2)}, u32[]{:S(2)}) %collective-permute-start.1) | collective-permute-done | bytes 6176 | tf_op jit(solution)/shard_map/ppermute | solution.py:311
  16.6 1.1 copy-done.3
  17.8 1.7 %copy-done.4 = bf16[768,1536]{1,0:T(8,128)(2,1)S(1)} copy-done((bf16[768,1536]{1,0:T(8,128)(2,1)S(1)}, bf16[768,1536]{1,0:T(8,128)(2,1)}, u32[]{:S(2)}) %copy-start.4) | copy-done | bytes 2359320
  19.4 1.1 copy-done.5
  20.6 8.4 %encode.1 = (bf16[256,1536]{1,0:T(8,128)(2,1)S(1)}, bf16[256,1024]{1,0:T(8,128)(2,1)S(1)}, bf16[256,256]{1,0:T(8,128)(2,1)}) custom-call(bf16[2,256,768]{2,1,0:T(8,128)(2,1)S(1)} %copy-done.3, bf16[2,2,768]{2,1,0:T(2,128)(2,1)S(1)} %collective-permute-done.low_ref, bf16[2,2,768]{2,1,0:T(2,128)(2,1)S(1)} %collective-permute-done.1.high_ref, ...), custom_call_target="tpu_custom_call" | custom-call | flops 3400000000 | bytes 12000000 | tf_op jit(solution)/shard_map/encode/pallas_call | solution.py:221
  29.0 0.9 copy-done.6
  29.8 0.8 copy-done.7
  30.8 1.0 pick.1
  31.9 34.9 %all_to_all.10.arrived_ref = bf16[32,2,16,896]{3,2,1,0:T(8,128)(2,1)S(1)} all-to-all(bf16[32,2,16,896]{3,2,1,0:T(8,128)(2,1)S(1)} %pick.1), channel_id=1, replica_groups=mesh['phase'=2,'y'=4,'x'=4,'core'=2,'dp'=2] {'y','x','core'}, dimensions={0} | all-to-all | bytes 3670016 | tf_op jit(solution)/shard_map/all_to_all | solution.py:349
  66.8 0.6 ends.1.ends_ref
  67.8 0.6 collective-permute-start.2
  68.4 2.0 %collective-permute-done.2.other_ref = bf16[16,48,256]{2,1,0:T(8,128)(2,1)S(1)} collective-permute-done((bf16[16,48,256]{2,1,0:T(8,128)(2,1)S(1)}, bf16[16,48,256]{2,1,0:T(8,128)(2,1)S(1)}, u32[]{:S(2)}, u32[]{:S(2)}) %collective-permute-start.2) | collective-permute-done | bytes 393248 | tf_op jit(solution)/shard_map/ppermute | solution.py:365
  70.4 2.9 %partial_grad.1 = bf16[32,24,1536]{2,1,0:T(8,128)(2,1)} custom-call(bf16[16,48,256]{2,1,0:T(8,128)(2,1)S(1)} %get-tuple-element.11.mine_ref, bf16[16,48,256]{2,1,0:T(8,128)(2,1)S(1)} %collective-permute-done.2.other_ref, bf16[256,1536]{1,0:T(8,128)(2,1)S(1)} %ends.1.ends_ref, bf16[256,1536]{1,0:T(8,128)(2,1)S(1)} %collective-permute-done.3.ends_other_ref), custom_call_target="tpu_custom_call" | custom-call | flops 1200000000 | bytes 5000000 | tf_op jit(solution)/shard_map/partial_grad/pallas_call | solution.py:143
  73.2 6.1 %all-to-all-start.1 = ((bf16[32,24,1536]{2,1,0:T(8,128)(2,1)}), bf16[32,24,1536]{2,1,0:T(8,128)(2,1)S(1)}, u32[]{:S(2)}, u32[]{:S(2)}) async-start(bf16[32,24,1536]{2,1,0:T(8,128)(2,1)} %partial_grad.1), calls=%async_computation.1 | async-start | bytes 4718592 | tf_op jit(solution)/shard_map/all_to_all | solution.py:370
  79.4 0.5 broadcast_multiply_fusion.logit_ref
  79.9 2.6 %fusion.2 = f32[256,1536]{1,0:T(8,128)S(1)} fusion(bf16[2,1536,768]{2,1,0:T(8,128)(2,1)} %param.24, bf16[256,1536]{1,0:T(8,128)(2,1)S(1)} %ends.1.ends_ref), kind=kOutput, calls=%fused_computation.4 | convolution fusion | flops 603979776 | bytes 4325376 | tf_op jit(solution)/shard_map/dot_general | solution.py:26
  82.5 3.5 %fusion = bf16[256,1536]{1,0:T(8,128)(2,1)} fusion(f32[256,1536]{1,0:T(8,128)S(1)} %fusion.2, bf16[2,1536,768]{2,1,0:T(8,128)(2,1)} %param.24, bf16[256,1536]{1,0:T(8,128)(2,1)S(1)} %ends.1.ends_ref), kind=kOutput, calls=%fused_computation.2 | convolution fusion | flops 604766208 | bytes 5111808 | tf_op jit(solution)/shard_map/dot_general | solution.py:26
  85.9 32.3 %all-to-all-done.1 = bf16[32,24,1536]{2,1,0:T(8,128)(2,1)S(1)} async-done(((bf16[32,24,1536]{2,1,0:T(8,128)(2,1)}), bf16[32,24,1536]{2,1,0:T(8,128)(2,1)S(1)}, u32[]{:S(2)}, u32[]{:S(2)}) %all-to-all-start.1) | async-done | bytes 2359328 | tf_op jit(solution)/shard_map/all_to_all | solution.py:370
  118.7 0.7 copy.21
  119.4 21.3 %trunk.1 = bf16[256,1536]{1,0:T(8,128)(2,1)} custom-call(s32[1]{0:T(128)} %bitcast.phase_ref, f32[8]{0:T(128)} %broadcast_multiply_fusion.logit_ref, bf16[256,1024]{1,0:T(8,128)(2,1)} %copy-done.7, bf16[2,4096,256]{2,1,0:T(8,128)(2,1)} %all-gather.2.cloned.1.call-done.keyval_ref, bf16[256,1536]{1,0:T(8,128)(2,1)} %copy-done.6, bf16[1024,1536]{1,0:T(8,128)(2,1)} %exit_ref.1), custom_call_target="tpu_custom_call" | custom-call | flops 5200000000 | bytes 9000000 | tf_op jit(solution)/shard_map/trunk/pallas_call | solution.py:286
  (28 shorter events, 1.0 us)
Async XLA Ops:
  7.2 112.2 %all-gather.2.cloned.1.call-start = ((), (), s32[]{:S(2)}) async-start(), calls=%async_computation.2 | async-start | bytes 4325376 | tf_op jit(solution)/shard_map/all_gather | solution.py:361
  8.0 6.3 %collective-permute-start = (bf16[2,2,768]{2,1,0:T(2,128)(2,1)S(1)}, bf16[2,2,768]{2,1,0:T(2,128)(2,1)S(1)}, u32[]{:S(2)}, u32[]{:S(2)}) collective-permute-start(bf16[2,2,768]{2,1,0:T(2,128)(2,1)S(1)} %get-tuple-element.17), channel_id=1, source_target_pairs={{0,2},{2,4},{4,6},{6,8},{8,10},{10,12},{12,14},{14,16},{16,18},{18... | collective-permute-start | bytes 18440 | tf_op jit(solution)/shard_map/ppermute | solution.py:310
  11.7 4.9 %collective-permute-start.1 = (bf16[2,2,768]{2,1,0:T(2,128)(2,1)S(1)}, bf16[2,2,768]{2,1,0:T(2,128)(2,1)S(1)}, u32[]{:S(2)}, u32[]{:S(2)}) collective-permute-start(bf16[2,2,768]{2,1,0:T(2,128)(2,1)S(1)} %get-tuple-element.16), channel_id=1, source_target_pairs={{2,0},{4,2},{6,4},{8,6},{10,8},{12,10},{14,12},{16,14},{18,16},{20... | collective-permute-start | bytes 18440 | tf_op jit(solution)/shard_map/ppermute | solution.py:311
  14.3 16.5 %copy-start.1 = (bf16[1,2,128,768]{3,2,1,0:T(8,128)(2,1)S(1)}, bf16[1,2,128,768]{3,2,1,0:T(8,128)(2,1)}, u32[]{:S(2)}) copy-start(bf16[1,2,128,768]{3,2,1,0:T(8,128)(2,1)} %param.23) | copy-start | bytes 1179652
  14.3 16.5 %copy-start.2 = (s32[1,2,1,32]{3,2,1,0:T(1,128)S(1)}, s32[1,2,1,32]{3,2,1,0:T(1,128)}, u32[]{:S(2)}) copy-start(s32[1,2,1,32]{3,2,1,0:T(1,128)} %param.27) | copy-start | bytes 772
  16.6 1.1 copy-start.3
  17.8 1.7 %copy-start.4 = (bf16[768,1536]{1,0:T(8,128)(2,1)S(1)}, bf16[768,1536]{1,0:T(8,128)(2,1)}, u32[]{:S(2)}) copy-start(bf16[768,1536]{1,0:T(8,128)(2,1)} %merge_hbm.1) | copy-start | bytes 7077892
  19.4 1.1 copy-start.5
  20.6 10.1 %copy-start.8 = (s32[1,2,1,32,16]{3,4,2,1,0:T(8,128)S(1)}, s32[1,2,1,32,16]{3,4,2,1,0:T(8,128)}, u32[]{:S(2)}) copy-start(s32[1,2,1,32,16]{3,4,2,1,0:T(8,128)} %param.25) | copy-start | bytes 12292
  20.6 10.2 %copy-start.9 = (s32[1,2,1,32,16]{3,4,2,1,0:T(8,128)S(1)}, s32[1,2,1,32,16]{3,4,2,1,0:T(8,128)}, u32[]{:S(2)}) copy-start(s32[1,2,1,32,16]{3,4,2,1,0:T(8,128)} %param.26) | copy-start | bytes 12292
  29.0 0.9 copy-start.6
  29.8 0.8 copy-start.7
  31.9 35.7 %copy-start = (bf16[1,2,128,1536]{3,2,1,0:T(8,128)(2,1)S(1)}, bf16[1,2,128,1536]{3,2,1,0:T(8,128)(2,1)}, u32[]{:S(2)}) copy-start(bf16[1,2,128,1536]{3,2,1,0:T(8,128)(2,1)} %param.22) | copy-start | bytes 2359300
  67.4 2.9 %collective-permute-start.3 = (bf16[256,1536]{1,0:T(8,128)(2,1)S(1)}, bf16[256,1536]{1,0:T(8,128)(2,1)S(1)}, u32[]{:S(2)}, u32[]{:S(2)}) collective-permute-start(bf16[256,1536]{1,0:T(8,128)(2,1)S(1)} %ends.1.ends_ref), channel_id=1, source_target_pairs={{0,2},{2,0},{1,3},{3,1},{4,6},{6,4},{5,7},{7,5},{8,10},{10,8},{9,1... | collective-permute-start | bytes 2359304 | tf_op jit(solution)/shard_map/ppermute | solution.py:368
  67.8 2.6 %collective-permute-start.2 = (bf16[16,48,256]{2,1,0:T(8,128)(2,1)S(1)}, bf16[16,48,256]{2,1,0:T(8,128)(2,1)S(1)}, u32[]{:S(2)}, u32[]{:S(2)}) collective-permute-start(bf16[16,48,256]{2,1,0:T(8,128)(2,1)S(1)} %get-tuple-element.12), channel_id=1, source_target_pairs={{0,2},{2,0},{1,3},{3,1},{4,6},{6,4},{5,7},{7,5},{8,10},{10,8},{9,1... | collective-permute-start | bytes 1179656 | tf_op jit(solution)/shard_map/ppermute | solution.py:365
  73.2 6.2 %copy-start.10 = (f32[8]{0:T(128)S(1)}, f32[8]{0:T(128)}, u32[]{:S(2)}) copy-start(f32[8]{0:T(128)} %param.21) | copy-start | bytes 100
  73.2 45.0 %all-to-all-start.1 = ((bf16[32,24,1536]{2,1,0:T(8,128)(2,1)}), bf16[32,24,1536]{2,1,0:T(8,128)(2,1)S(1)}, u32[]{:S(2)}, u32[]{:S(2)}) async-start(bf16[32,24,1536]{2,1,0:T(8,128)(2,1)} %partial_grad.1), calls=%async_computation.1 | async-start | bytes 4718592 | tf_op jit(solution)/shard_map/all_to_all | solution.py:370
Sparse Core Ops, SparseCore 0:
  30.8 77.1 all-gather.1

commit v3 on v2

v3 whole, which is shorter than its diff:
```python
import functools
import math

import jax
import jax.numpy as jnp
from jax import lax
from jax.experimental import pallas as pl
from jax.experimental.pallas import tpu as pltpu
from jax.sharding import Mesh
from jax.sharding import PartitionSpec as P

DILATION_STEP = 2
SEQ = ("y", "x", "core")
F32 = jnp.float32
BF16 = jnp.bfloat16
I32 = jnp.int32
TAG = 128
NT = (((1,), (1,)), ((), ()))
TN = (((0,), (0,)), ((), ()))
VMEM = pl.BlockSpec(memory_space=pltpu.VMEM)
SMEM = pl.BlockSpec(memory_space=pltpu.SMEM)
ANY = pl.BlockSpec(memory_space=pl.ANY)
HBM = pl.BlockSpec(memory_space=pltpu.HBM)


def dot(a, b, dims=(((1,), (0,)), ((), ()))):
    return lax.dot_general(a, b, dims, preferred_element_type=F32)


def params(mib):
    return pltpu.CompilerParams(vmem_limit_bytes=mib << 20)


TOKEN = jax.ShapeDtypeStruct((8, 128), F32)


def cost(flops, nbytes):
    return pl.CostEstimate(flops=int(flops), bytes_accessed=int(nbytes), transcendentals=0)


def pick_kernel(
    ids_hbm,
    lines_hbm,
    counts_hbm,
    cot_hbm,
    _low,
    _high,
    out_ref,
    token_ref,
    ids_ref,
    lines_ref,
    counts_ref,
    cot_ref,
    sems,
):
    pairs = ((ids_hbm, ids_ref), (lines_hbm, lines_ref), (counts_hbm, counts_ref), (cot_hbm, cot_ref))
    copies = [
        pltpu.make_async_copy(source, target, sems.at[i])
        for i, (source, target) in enumerate(pairs)
    ]
    for copy in copies:
        copy.start()
    token_ref[...] = jnp.zeros_like(token_ref)
    batch, slots, shards = ids_ref.shape
    junc, embed = cot_ref.shape[1:]
    n = shards * slots
    owner = lax.broadcasted_iota(I32, (n, shards), 0) // slots
    spread = owner == lax.broadcasted_iota(I32, (n, shards), 1)
    spread16 = spread.astype(F32).astype(BF16)
    slot = lax.broadcasted_iota(I32, (n, slots), 0) % slots
    own = slot == lax.broadcasted_iota(I32, (n, slots), 1)

    def column(values):
        wide = dot(spread16, values.astype(F32).astype(BF16), NT)
        return jnp.sum(jnp.where(own, wide, 0.0), axis=1, keepdims=True)

    for copy in copies:
        copy.wait()
    for b in range(batch):
        ids = ids_ref[b]
        junction = column(ids % junc)
        code = column(ids // junc) * float(junc) + column(lines_ref[b])
        count = jnp.sum(
            jnp.where(spread, counts_ref[b : b + 1, :].astype(F32), 0.0), axis=1, keepdims=True
        )
        valid = slot[:, :1].astype(F32) < count
        junction = jnp.where(valid, junction, -1.0).astype(I32)
        code = jnp.where(valid, code, -1.0)
        onehot = (junction == lax.broadcasted_iota(I32, (n, junc), 1)).astype(F32).astype(BF16)
        picked = dot(onehot, cot_ref[b]).astype(BF16)
        out_ref[:, b, :, :embed] = picked.reshape(shards, slots, embed)
        tags = jnp.broadcast_to(code, (n, TAG)).astype(BF16)
        out_ref[:, b, :, embed:] = tags.reshape(shards, slots, TAG)


def pick(ids, lines, counts, cotangent, low, high):
    batch, slots, shards = ids.shape
    embed = cotangent.shape[2]
    return pl.pallas_call(
        pick_kernel,
        out_shape=(
            jax.ShapeDtypeStruct((shards, batch, slots, embed + TAG), BF16),
            TOKEN,
        ),
        in_specs=[ANY] * 6,
        out_specs=(VMEM, VMEM),
        scratch_shapes=[
            pltpu.VMEM(ids.shape, I32),
            pltpu.VMEM(lines.shape, I32),
            pltpu.VMEM(counts.shape, I32),
            pltpu.VMEM(cotangent.shape, BF16),
            pltpu.SemaphoreType.DMA((4,)),
        ],
        compiler_params=params(56),
        cost_estimate=cost(2 * 10**8, 3 * 10**6),
        name="pick",
    )(ids, lines, counts, cotangent, low, high)


def ends_kernel(arrived_ref, _, out_ref):
    shards, batch, slots, wide = arrived_ref.shape
    embed = wide - TAG
    n = shards * slots
    rows = out_ref.shape[0] // batch
    for b in range(batch):
        data = arrived_ref[:, b, :, :embed].reshape(n, embed)
        tag = arrived_ref[:, b, :, embed:].reshape(n, TAG).astype(F32)
        for kind in range(2):
            target = lax.broadcasted_iota(I32, (n, rows), 1) + kind * rows
            onehot = (tag == target.astype(F32)).astype(F32).astype(BF16)
            out_ref[b * rows : (b + 1) * rows, kind * embed : (kind + 1) * embed] = dot(
                onehot, data, TN
            ).astype(BF16)


def make_ends(arrived, rows, after):
    batch, embed = arrived.shape[1], arrived.shape[3] - TAG
    return pl.pallas_call(
        ends_kernel,
        out_shape=jax.ShapeDtypeStruct((batch * rows, 2 * embed), BF16),
        in_specs=[VMEM, ANY],
        out_specs=VMEM,
        compiler_params=params(32),
        cost_estimate=cost(4 * 10**8, 3 * 10**6),
        name="ends",
    )(arrived, after)


def turn_kernel(core_ref, lines_ref, mine_ref, other_ref):
    blocks, part, n = mine_ref.shape
    first = core_ref[0] == 0
    turned = lines_ref[...].T.reshape(blocks, 2, part, n)
    low, high = turned[:, 0], turned[:, 1]
    mine_ref[...] = jnp.where(first, low, high)
    other_ref[...] = jnp.where(first, high, low)


def turn(core, lines, blocks):
    n, width = lines.shape
    half = jax.ShapeDtypeStruct((blocks, width // (2 * blocks), n), BF16)
    return pl.pallas_call(
        turn_kernel,
        out_shape=(half, half),
        in_specs=[SMEM, VMEM],
        out_specs=(VMEM, VMEM),
        compiler_params=params(32),
        cost_estimate=cost(10**6, 2 * 10**6),
        name="turn",
    )(core.reshape(1), lines)


def partial_kernel(mine_ref, other_ref, ends_ref, ends_other_ref, out_ref, token_ref):
    token_ref[...] = jnp.zeros_like(token_ref)
    rows, n = mine_ref.shape[0] * mine_ref.shape[1], mine_ref.shape[2]
    total = dot(mine_ref[...].reshape(rows, n), ends_ref[...])
    total = total + dot(other_ref[...].reshape(rows, n), ends_other_ref[...])
    out_ref[...] = total.astype(BF16).reshape(out_ref.shape)


def partial_grad(mine, other, ends, ends_other, pieces):
    rows, width = mine.shape[0] * mine.shape[1], ends.shape[1]
    return pl.pallas_call(
        partial_kernel,
        out_shape=(jax.ShapeDtypeStruct((pieces, rows // pieces, width), BF16), TOKEN),
        in_specs=[VMEM] * 4,
        out_specs=(VMEM, VMEM),
        compiler_params=params(40),
        cost_estimate=cost(1.2 * 10**9, 5 * 10**6),
        name="partial_grad",
    )(mine, other, ends, ends_other)


def encoder_kernel(
    core_ref,
    low_ref,
    high_ref,
    gain_ref,
    x_hbm,
    taps_hbm,
    merge_hbm,
    look_hbm,
    ask_hbm,
    after_ref,
    rows_hbm,
    key_own_ref,
    key_out_ref,
    query_own_ref,
    query_out_ref,
    token_ref,
    x_ref,
    taps,
    merge,
    look,
    ask,
    pad,
    hidden,
    rows_ref,
    sems,
):
    pairs = ((x_hbm, x_ref), (taps_hbm, taps), (merge_hbm, merge), (look_hbm, look), (ask_hbm, ask))
    copies = [
        pltpu.make_async_copy(source, target, sems.at[i])
        for i, (source, target) in enumerate(pairs)
    ]
    for copy in copies:
        copy.start()
    out_copy = pltpu.make_async_copy(rows_ref, rows_hbm, sems.at[len(pairs)])
    batch, cells, chans = x_ref.shape
    extent = low_ref.shape[1]
    base = 8
    copies[0].wait()
    for b in range(batch):
        pad[b, base - extent : base, :] = low_ref[b].astype(F32)
        pad[b, base : base + cells, :] = x_ref[b].astype(F32)
        pad[b, base + cells : base + cells + extent, :] = high_ref[b].astype(F32)
    copies[1].wait()
    for b in range(batch):
        total = dot(x_ref[b], taps[1])
        total += dot(pad[b, base - extent : base - extent + cells, :].astype(BF16), taps[0])
        total += dot(pad[b, base + extent : base + extent + cells, :].astype(BF16), taps[2])
        total = pad[b, base : base + cells, :] + jax.nn.gelu(total)
        for j in range(hidden.shape[0]):
            hidden[j, b * cells : (b + 1) * cells, :] = total[:, j * 128 : (j + 1) * 128]
    n = batch * cells // 2
    pooled = jnp.concatenate(
        [
            ((hidden[j, pl.ds(0, n, 2), :] + hidden[j, pl.ds(1, n, 2), :]) * 0.5).astype(BF16)
            for j in range(hidden.shape[0])
        ],
        axis=1,
    )
    copies[2].wait()
    rows = dot(pooled, merge[...]).astype(BF16)
    rows_ref[...] = rows
    out_copy.start()
    wide = rows.astype(F32)
    scale = lax.rsqrt(jnp.mean(wide * wide, axis=-1, keepdims=True) + 1e-06)
    normed = (wide * scale * gain_ref[...]).astype(BF16)
    half = n // 2
    first = core_ref[0] == 0

    def halves(value, own_ref, out_ref):
        own_ref[...] = jnp.where(first, value[:half], value[half:])
        out_ref[...] = jnp.where(first, value[half:], value[:half])

    copies[3].wait()
    halves(dot(normed, look[...]).astype(BF16), key_own_ref, key_out_ref)
    copies[4].wait()
    halves(dot(normed, ask[...]).astype(BF16), query_own_ref, query_out_ref)
    token_ref[...] = jnp.zeros_like(token_ref)
    out_copy.wait()


def encode(core, x, low, high, gain, taps, merge, look, ask, after):
    batch, cells, chans = x.shape
    n = batch * cells // 2
    width = merge.shape[1]
    key = jax.ShapeDtypeStruct((n // 2, look.shape[1]), BF16)
    query = jax.ShapeDtypeStruct((n // 2, ask.shape[1]), BF16)
    return pl.pallas_call(
        encoder_kernel,
        out_shape=(jax.ShapeDtypeStruct((n, width), BF16), key, key, query, query, TOKEN),
        in_specs=[SMEM] + [VMEM] * 3 + [HBM] * 5 + [ANY],
        out_specs=(HBM,) + (VMEM,) * 5,
        scratch_shapes=[
            pltpu.VMEM(x.shape, BF16),
            pltpu.VMEM(taps.shape, BF16),
            pltpu.VMEM(merge.shape, BF16),
            pltpu.VMEM(look.shape, BF16),
            pltpu.VMEM(ask.shape, BF16),
            pltpu.VMEM((batch, cells + 16, chans), F32),
            pltpu.VMEM((chans // 128, batch * cells, 128), F32),
            pltpu.VMEM((n, width), BF16),
            pltpu.SemaphoreType.DMA((6,)),
        ],
        compiler_params=params(56),
        cost_estimate=cost(3.4 * 10**9, 12 * 10**6),
        name="encode",
    )(core.reshape(1), low, high, gain.reshape(1, width), x, taps, merge, look, ask, after)


def attend_kernel(
    phase_ref, logit_ref, query_own_ref, query_in_ref, *refs
):
    keys, (_, own_ref, out_ref) = refs[:-3], refs[-3:]
    rows, width = query_own_ref.shape
    lane = keys[0].shape[1] // 2
    pieces = [key.at[i : i + 512] for key in keys for i in range(0, key.shape[0], 512)]

    def head(h):
        span = pl.ds(pl.multiple_of(h * lane, lane), lane)
        query = jnp.concatenate([query_own_ref[:, span], query_in_ref[:, span]], axis=0)
        factor = logit_ref[h]
        scores = [dot(query, piece[:, :lane], NT) for piece in pieces]
        top = functools.reduce(jnp.maximum, scores)
        top = jnp.max(top, axis=-1, keepdims=True) * factor
        mixed, total = 0.0, 0.0
        for score, piece in zip(scores, pieces):
            expo = jnp.exp2(score * factor - top)
            total = total + expo
            mixed = mixed + dot(expo.astype(BF16), piece[:, lane:])
        total = jnp.sum(total, axis=-1, keepdims=True)
        mixed = (mixed / total).astype(BF16)
        own_ref[:, span] = mixed[:rows]
        out_ref[:, span] = mixed[rows:]

    @pl.when(phase_ref[0] == 1)
    def _():
        @pl.loop(0, width // lane // 2)
        def _(i):
            head(2 * i)
            head(2 * i + 1)


def attend(phase, logit, query_own, query_in, keys, after):
    shape = jax.ShapeDtypeStruct(query_own.shape, BF16)
    return pl.pallas_call(
        attend_kernel,
        out_shape=(shape, shape),
        in_specs=[SMEM, SMEM] + [VMEM] * (2 + len(keys)) + [ANY],
        out_specs=(VMEM, VMEM),
        compiler_params=params(24),
        cost_estimate=cost(6 * 10**10, 4 * 10**6),
        name="attend",
    )(phase.reshape(1), logit, query_own, query_in, *keys, after)


def exit_kernel(phase_ref, core_ref, rows_ref, own_ref, in_ref, exit_ref, out_ref, token_ref):
    token_ref[...] = jnp.zeros_like(token_ref)
    n = own_ref.shape[0]
    on = phase_ref[0] == 1

    @pl.when(on)
    def _():
        attended = jnp.concatenate([own_ref[...], in_ref[...]], axis=0)
        mixed = dot(attended, exit_ref[...])
        for i in range(2):
            owner = core_ref[0] if i == 0 else 1 - core_ref[0]
            span = pl.ds(pl.multiple_of(owner * n, n), n)
            out_ref[span, :] = (rows_ref[span, :].astype(F32) + mixed[i * n : (i + 1) * n]).astype(
                BF16
            )

    @pl.when(jnp.logical_not(on))
    def _():
        out_ref[...] = rows_ref[...]


def leave(phase, core, encoded, own, arrived, exit_projector):
    return pl.pallas_call(
        exit_kernel,
        out_shape=(jax.ShapeDtypeStruct(encoded.shape, BF16), TOKEN),
        in_specs=[SMEM, SMEM] + [VMEM] * 4,
        out_specs=(VMEM, VMEM),
        compiler_params=params(32),
        cost_estimate=cost(8 * 10**8, 5 * 10**6),
        name="leave",
    )(phase.reshape(1), core.reshape(1), encoded, own, arrived, exit_projector)


def gather_terms_kernel(pieces_ref, _, out_ref):
    embed = out_ref.shape[2]
    total = jnp.sum(pieces_ref[...].astype(F32), axis=0)
    for kind in range(2):
        out_ref[kind] = total[:, kind * embed : (kind + 1) * embed]


def sum_terms(pieces, after):
    _, rows, width = pieces.shape
    return pl.pallas_call(
        gather_terms_kernel,
        out_shape=jax.ShapeDtypeStruct((2, rows, width // 2), F32),
        in_specs=[VMEM, ANY],
        out_specs=VMEM,
        compiler_params=params(32),
        cost_estimate=cost(10**6, 3 * 10**6),
        name="sum_terms",
    )(pieces, after)


def stack_kernel(*refs):
    blocks, (out_ref, token_ref) = refs[:-2], refs[-2:]
    rows = blocks[0].shape[0]
    for i, block in enumerate(blocks):
        out_ref[i * rows : (i + 1) * rows, :] = block[...]
    token_ref[...] = jnp.zeros_like(token_ref)


def stack(blocks):
    rows, width = blocks[0].shape
    return pl.pallas_call(
        stack_kernel,
        out_shape=(jax.ShapeDtypeStruct((len(blocks) * rows, width), BF16), TOKEN),
        in_specs=[VMEM] * len(blocks),
        out_specs=(VMEM, VMEM),
        compiler_params=params(8),
        cost_estimate=cost(10**5, 10**6),
        name="stack",
    )(*blocks)


def spread(block, side, first):
    received = []
    for distance in (1, side - 1, 2):
        pairs = []
        for y in range(side):
            for x in range(side):
                for core in range(2):
                    along_x = (core == 0) == first
                    to_x = (x + distance) % side if along_x else x
                    to_y = y if along_x else (y + distance) % side
                    pairs.append(((y * side + x) * 2 + core, (to_y * side + to_x) * 2 + core))
        received.append(lax.ppermute(block, SEQ, pairs))
    return received


def halo(block, width):
    count = lax.axis_size(SEQ)
    forward = [(i, i + 1) for i in range(count - 1)]
    backward = [(b, a) for a, b in forward]
    low = lax.ppermute(block[:, -width:], SEQ, forward)
    high = lax.ppermute(block[:, :width], SEQ, backward)
    return low, high


def body(
    bin_activations,
    spaced_filter_coefs,
    merged_bin_projector,
    backbone_rms_gain,
    asking_projector,
    common_lookup_projector,
    attention_exit_projector,
    lane_logit_factor,
    splice_readout_lines,
    couple_embedding_cotangent,
    splice_site_projector,
    site_locator_code,
    site_local_line,
    filled_slot_totals,
):
    phase = lax.axis_index("phase")
    core = lax.axis_index("core")
    batch, cells, chans = bin_activations.shape
    rows = cells // 2
    width = merged_bin_projector.shape[1]
    extent = DILATION_STEP * (spaced_filter_coefs.shape[0] // 2)
    lane = common_lookup_projector.shape[1] // 2
    embed = couple_embedding_cotangent.shape[3]
    shards = site_locator_code.shape[3]
    swap = [(0, 1), (1, 0)]
    side = lax.axis_size("y")

    low, high = halo(bin_activations, extent)
    payload, picked = pick(
        jnp.swapaxes(site_locator_code[0, :, 0], 1, 2),
        jnp.swapaxes(site_local_line[0, :, 0], 1, 2),
        filled_slot_totals[0, :, 0],
        couple_embedding_cotangent[0],
        low,
        high,
    )
    arrived = lax.all_to_all(payload, SEQ, 0, 0, tiled=True)

    encoded, key_own, key_out, query_own, query_out, _ = encode(
        core,
        bin_activations,
        low,
        high,
        backbone_rms_gain,
        spaced_filter_coefs,
        merged_bin_projector,
        common_lookup_projector,
        asking_projector,
        picked,
    )
    chip_keys, _ = stack([key_own, lax.ppermute(key_out, "core", swap)])
    line_keys, line_done = stack([chip_keys] + spread(chip_keys, side, True))
    keys = [line_keys] + spread(line_keys, side, False)
    query_in = lax.ppermute(query_out, "core", swap)

    portion = splice_readout_lines[0].reshape(batch * rows, width)
    mine, other = turn(core, portion, shards // 2)
    other = lax.ppermute(other, "core", swap)

    ends = make_ends(arrived, rows, line_done)
    ends_other = lax.ppermute(ends, "core", swap)
    partial, terms_done = partial_grad(mine, other, ends, ends_other, shards)
    pieces = lax.all_to_all(partial, ("y", "x", "dp"), 0, 0, tiled=True)

    row_grad = (
        dot(ends[:, :embed], splice_site_projector[0], NT)
        + dot(ends[:, embed:], splice_site_projector[1], NT)
    ).astype(BF16)
    row_grad = row_grad.reshape(batch, rows, width)[None]

    logit = lane_logit_factor * (math.log2(math.e) / math.sqrt(lane))
    own, out = attend(phase, logit, query_own, query_in, keys, terms_done)
    rows_out, left = leave(
        phase, core, encoded, own, lax.ppermute(out, "core", swap), attention_exit_projector
    )
    phase_rows = rows_out.reshape(batch, rows, width)[None]

    weight_grad = sum_terms(pieces, left)[None]
    return (phase_rows, row_grad, weight_grad)


def solution(mesh):
    shape = dict(mesh.shape)
    side = math.isqrt(shape["seq"] // 2)
    fine = Mesh(
        mesh.devices.reshape(shape["phase"], side, side, 2, shape["dp"]),
        ("phase", "y", "x", "core", "dp"),
    )
    return jax.shard_map(
        body,
        mesh=fine,
        in_specs=(
            P("dp", SEQ, None),
            P(),
            P(),
            P(),
            P(),
            P(),
            P(),
            P(),
            P("phase", "dp", SEQ, None),
            P("phase", "dp", SEQ, None),
            P(),
            P("phase", "dp", SEQ, None, None),
            P("phase", "dp", SEQ, None, None),
            P("phase", "dp", SEQ, None),
        ),
        out_specs=(
            P("phase", "dp", SEQ, None),
            P("phase", "dp", SEQ, None),
            P("phase", None, SEQ + ("dp",), None),
        ),
        check_vma=False,
    )
```

time: 148 us -> 106 us (0.72)
  the two profiles are of different devices: /device:TPU:73 before, /device:TPU:64 now
where the time goes in v3:
time: 106 us
  Pallas kernels  37.8 us (36%)
  starting transfers between devices  31.5 us (30%)
  waiting for transfers between devices  23.1 us (22%)
  matrix products  7.16 us (7%)
  local copies, waits for them, and re-layouts  5.17 us (5%)
    pallas_call x1, Pallas kernels, attend(): pl.pallas_call(attend_kernel, out_shape=(shape, shape), in_specs=[SMEM, S...  17 us
    all_to_all x1, starting transfers between devices, body(): arrived = lax.all_to_all(payload, SEQ, 0, 0, tiled=True)  10.9 us
    ppermute x6, starting transfers between devices, spread(): received.append(lax.ppermute(block, SEQ, pairs))  10.4 us
    pallas_call x1, Pallas kernels, encode(): pl.pallas_call(encoder_kernel, out_shape=(jax.ShapeDtypeStruct((n, width)...  10.2 us
    all_to_all x1, waiting for transfers between devices, body(): pieces = lax.all_to_all(partial, ('y', 'x', 'dp'), 0, 0, tiled=True)  10.2 us
    ppermute x6, waiting for transfers between devices, spread(): received.append(lax.ppermute(block, SEQ, pairs))  8.7 us
    dot_general x2, matrix products, dot(): return lax.dot_general(a, b, dims, preferred_element_type=F32)  7.16 us
    all_to_all x1, starting transfers between devices, body(): pieces = lax.all_to_all(partial, ('y', 'x', 'dp'), 0, 0, tiled=True)  6.06 us
  transfers between devices with their start and end apart: 15, of which 5 were waited for; matrix products, arithmetic and copies ran while one was open for 7% of the time, Pallas kernels for 31%

profile of v3, /device:TPU:64, one launch (start us, length us, event | category | flops | bytes accessed | tf_op | source)
XLA Modules:
  0.0 105.6 jit_solution(11947986615421970416)
XLA Ops:
  1.4 1.7 %collective-permute-start = (bf16[2,2,768]{2,1,0:T(2,128)(2,1)S(1)}, bf16[2,2,768]{2,1,0:T(2,128)(2,1)S(1)}, u32[]{:S(2)}, u32[]{:S(2)}) collective-permute-start(bf16[2,2,768]{2,1,0:T(2,128)(2,1)S(1)} %get-tuple-element.40), channel_id=1, source_target_pairs={{0,2},{2,4},{4,6},{6,8},{8,10},{10,12},{12,14},{14,16},{16,18},{18... | collective-permute-start | bytes 18440 | tf_op jit(solution)/shard_map/ppermute | solution.py:441
  3.2 1.3 %collective-permute-start.1 = (bf16[2,2,768]{2,1,0:T(2,128)(2,1)S(1)}, bf16[2,2,768]{2,1,0:T(2,128)(2,1)S(1)}, u32[]{:S(2)}, u32[]{:S(2)}) collective-permute-start(bf16[2,2,768]{2,1,0:T(2,128)(2,1)S(1)} %get-tuple-element.39), channel_id=1, source_target_pairs={{2,0},{4,2},{6,4},{8,6},{10,8},{12,10},{14,12},{16,14},{18,16},{20... | collective-permute-start | bytes 18440 | tf_op jit(solution)/shard_map/ppermute | solution.py:442
  4.5 3.0 %collective-permute-done.1._high.high_ref = bf16[2,2,768]{2,1,0:T(2,128)(2,1)S(1)} collective-permute-done((bf16[2,2,768]{2,1,0:T(2,128)(2,1)S(1)}, bf16[2,2,768]{2,1,0:T(2,128)(2,1)S(1)}, u32[]{:S(2)}, u32[]{:S(2)}) %collective-permute-start.1) | collective-permute-done | bytes 6176 | tf_op jit(solution)/shard_map/ppermute | solution.py:442
  8.1 3.3 %pick.1 = (bf16[32,2,16,896]{3,2,1,0:T(8,128)(2,1)}, f32[8,128]{1,0:T(8,128)}) custom-call(s32[2,16,32]{2,1,0:T(8,128)} %bitcast.24, s32[2,16,32]{2,1,0:T(8,128)} %bitcast.25, s32[2,32]{1,0:T(2,128)} %bitcast.26, bf16[2,128,768]{2,1,0:T(8,128)(2,1)} %bitcast.23, bf16[2,2,768]{2,1,0:T(2,128)(2,1)} %copy-done.7, bf16[2,2,768]{2,1,0:T(2,128)(2,1)} %copy-done.8), custom_call_target="tpu_custom_call" | custom-call | flops 200000000 | bytes 3000000 | tf_op jit(solution)/shard_map/pick/pallas_call | solution.py:99
  11.4 10.9 %all-to-all-start = ((bf16[32,2,16,896]{3,2,1,0:T(8,128)(2,1)}), bf16[32,2,16,896]{3,2,1,0:T(8,128)(2,1)S(1)}, u32[]{:S(2)}, u32[]{:S(2)}) async-start(bf16[32,2,16,896]{3,2,1,0:T(8,128)(2,1)} %get-tuple-element.31), calls=%async_computation | async-start | bytes 3670016 | tf_op jit(solution)/shard_map/all_to_all | solution.py:483
  22.9 10.2 %encode.1 = (bf16[256,1536]{1,0:T(8,128)(2,1)}, bf16[128,256]{1,0:T(8,128)(2,1)}, bf16[128,256]{1,0:T(8,128)(2,1)}, bf16[128,1024]{1,0:T(8,128)(2,1)}, bf16[128,1024]{1,0:T(8,128)(2,1)}, /*index=5*/f32[8,128]{1,0:T(8,128)}) custom-call(s32[1]{0:T(128)} %bitcast.1.core_ref, bf16[2,2,768]{2,1,0:T(2,128)(2,1)} %copy-done.7, bf16[2,2,768]{2,1,0:T(2,128)(2,1)} %copy-done.8, ...), custom_call_target="tpu_custom_call" | custom-call | flops 3400000000 | bytes 12000000 | tf_op jit(solution)/shard_map/encode/pallas_call | solution.py:280
  33.5 1.2 %collective-permute-done.3.refs_1_ = bf16[128,256]{1,0:T(8,128)(2,1)S(1)} collective-permute-done((bf16[128,256]{1,0:T(8,128)(2,1)}, bf16[128,256]{1,0:T(8,128)(2,1)S(1)}, u32[]{:S(2)}, u32[]{:S(2)}) %collective-permute-start.3) | collective-permute-done | bytes 65568 | tf_op jit(solution)/shard_map/ppermute | solution.py:497
  36.1 1.8 %collective-permute-start.4 = (bf16[256,256]{1,0:T(8,128)(2,1)S(1)}, bf16[256,256]{1,0:T(8,128)(2,1)S(1)}, u32[]{:S(2)}, u32[]{:S(2)}) collective-permute-start(bf16[256,256]{1,0:T(8,128)(2,1)S(1)} %get-tuple-element.27.refs_0_), channel_id=1, source_target_pairs={{0,4},{2,18},{4,8},{6,22},{8,12},{10,26},{12,0},{14,30},{16,20},{1... | collective-permute-start | bytes 393224 | tf_op jit(solution)/shard_map/ppermute | solution.py:433
  37.9 1.4 %collective-permute-start.5 = (bf16[256,256]{1,0:T(8,128)(2,1)S(1)}, bf16[256,256]{1,0:T(8,128)(2,1)S(1)}, u32[]{:S(2)}, u32[]{:S(2)}) collective-permute-start(bf16[256,256]{1,0:T(8,128)(2,1)S(1)} %get-tuple-element.27.refs_0_), channel_id=1, source_target_pairs={{0,12},{2,50},{4,0},{6,54},{8,4},{10,58},{12,8},{14,62},{16,28},{1... | collective-permute-start | bytes 393224 | tf_op jit(solution)/shard_map/ppermute | solution.py:433
  39.4 2.1 %collective-permute-start.6 = (bf16[256,256]{1,0:T(8,128)(2,1)S(1)}, bf16[256,256]{1,0:T(8,128)(2,1)S(1)}, u32[]{:S(2)}, u32[]{:S(2)}) collective-permute-start(bf16[256,256]{1,0:T(8,128)(2,1)S(1)} %get-tuple-element.27.refs_0_), channel_id=1, source_target_pairs={{0,8},{2,34},{4,12},{6,38},{8,0},{10,42},{12,4},{14,46},{16,24},{1... | collective-permute-start | bytes 393224 | tf_op jit(solution)/shard_map/ppermute | solution.py:433
  41.4 6.0 %collective-permute-done.4.refs_1_ = bf16[256,256]{1,0:T(8,128)(2,1)S(1)} collective-permute-done((bf16[256,256]{1,0:T(8,128)(2,1)S(1)}, bf16[256,256]{1,0:T(8,128)(2,1)S(1)}, u32[]{:S(2)}, u32[]{:S(2)}) %collective-permute-start.4) | collective-permute-done | bytes 131104 | tf_op jit(solution)/shard_map/ppermute | solution.py:433
  47.5 2.7 %collective-permute-done.6.refs_3_ = bf16[256,256]{1,0:T(8,128)(2,1)S(1)} collective-permute-done((bf16[256,256]{1,0:T(8,128)(2,1)S(1)}, bf16[256,256]{1,0:T(8,128)(2,1)S(1)}, u32[]{:S(2)}, u32[]{:S(2)}) %collective-permute-start.6) | collective-permute-done | bytes 131104 | tf_op jit(solution)/shard_map/ppermute | solution.py:433
  51.7 1.0 turn.1
  53.2 1.8 %collective-permute-start.7 = (bf16[1024,256]{1,0:T(8,128)(2,1)}, bf16[1024,256]{1,0:T(8,128)(2,1)}, u32[]{:S(2)}, u32[]{:S(2)}) collective-permute-start(bf16[1024,256]{1,0:T(8,128)(2,1)} %get-tuple-element.28.refs_0_), channel_id=1, source_target_pairs={{0,16},{2,6},{4,20},{6,10},{8,24},{10,14},{12,28},{14,2},{16,32},{... | collective-permute-start | bytes 1572872 | tf_op jit(solution)/shard_map/ppermute | solution.py:433
  55.0 1.4 %collective-permute-start.8 = (bf16[1024,256]{1,0:T(8,128)(2,1)}, bf16[1024,256]{1,0:T(8,128)(2,1)}, u32[]{:S(2)}, u32[]{:S(2)}) collective-permute-start(bf16[1024,256]{1,0:T(8,128)(2,1)} %get-tuple-element.28.refs_0_), channel_id=1, source_target_pairs={{0,48},{2,14},{4,52},{6,2},{8,56},{10,6},{12,60},{14,10},{16,0},{1... | collective-permute-start | bytes 1572872 | tf_op jit(solution)/shard_map/ppermute | solution.py:433
  56.4 1.9 %collective-permute-start.9 = (bf16[1024,256]{1,0:T(8,128)(2,1)}, bf16[1024,256]{1,0:T(8,128)(2,1)}, u32[]{:S(2)}, u32[]{:S(2)}) collective-permute-start(bf16[1024,256]{1,0:T(8,128)(2,1)} %get-tuple-element.28.refs_0_), channel_id=1, source_target_pairs={{0,32},{2,10},{4,36},{6,14},{8,40},{10,2},{12,44},{14,6},{16,48},{... | collective-permute-start | bytes 1572872 | tf_op jit(solution)/shard_map/ppermute | solution.py:433
  58.4 3.6 %fusion.1 = f32[256,1536]{1,0:T(8,128)} fusion(bf16[2,1536,768]{2,1,0:T(8,128)(2,1)} %param.24, bf16[256,1536]{1,0:T(8,128)(2,1)S(1)} %ends.1.ends_ref), kind=kOutput, calls=%fused_computation.2 | convolution fusion | flops 603979776 | bytes 4325376 | tf_op jit(solution)/shard_map/dot_general | solution.py:27
  62.0 1.4 %partial_grad.1 = (bf16[32,24,1536]{2,1,0:T(8,128)(2,1)S(1)}, f32[8,128]{1,0:T(8,128)S(1)}) custom-call(bf16[16,48,256]{2,1,0:T(8,128)(2,1)S(1)} %get-tuple-element.29.mine_ref, bf16[16,48,256]{2,1,0:T(8,128)(2,1)S(1)} %collective-permute-done.10.other_ref, bf16[256,1536]{1,0:T(8,128)(2,1)S(1)} %ends.1.ends_ref, ...), custom_call_target="tpu_custom_call" | custom-call | flops 1200000000 | bytes 5000000 | tf_op jit(solution)/shard_map/partial_grad/pallas_call | solution.py:182
  63.4 1.4 %copy-done.1 = bf16[32,24,1536]{2,1,0:T(8,128)(2,1)} copy-done((bf16[32,24,1536]{2,1,0:T(8,128)(2,1)}, bf16[32,24,1536]{2,1,0:T(8,128)(2,1)S(1)}, u32[]{:S(2)}) %copy-start.1) | copy-done | bytes 2359320
  64.9 6.1 %all-to-all-start.1 = ((bf16[32,24,1536]{2,1,0:T(8,128)(2,1)}), bf16[32,24,1536]{2,1,0:T(8,128)(2,1)S(1)}, u32[]{:S(2)}, u32[]{:S(2)}) async-start(bf16[32,24,1536]{2,1,0:T(8,128)(2,1)} %copy-done.1), calls=%async_computation.1 | async-start | bytes 4718592 | tf_op jit(solution)/shard_map/all_to_all | solution.py:509
  71.9 17.0 %attend.1 = (bf16[128,1024]{1,0:T(8,128)(2,1)S(1)}, bf16[128,1024]{1,0:T(8,128)(2,1)S(1)}) custom-call(s32[1]{0:T(128)} %bitcast.phase_ref, f32[8]{0:T(128)S(1)} %broadcast_multiply_fusion.logit_ref, bf16[128,1024]{1,0:T(8,128)(2,1)S(1)} %copy-done.5, bf16[128,1024]{1,0:T(8,128)(2,1)S(1)} %collective-permute-done.2.query_in_ref, ...), custom_call_target="tpu_custom_call" | custom-call | flops 60000002048 | bytes 4000000 | tf_op jit(solution)/shard_map/attend/pallas_call | solution.py:337
  89.0 3.5 %fusion = bf16[256,1536]{1,0:T(8,128)(2,1)} fusion(f32[256,1536]{1,0:T(8,128)S(1)} %copy-done.10, bf16[2,1536,768]{2,1,0:T(8,128)(2,1)} %param.24, bf16[256,1536]{1,0:T(8,128)(2,1)S(1)} %ends.1.ends_ref), kind=kOutput, calls=%fused_computation.1 | convolution fusion | flops 604766208 | bytes 5111808 | tf_op jit(solution)/shard_map/dot_general | solution.py:27
  92.6 1.9 %leave.1 = (bf16[256,1536]{1,0:T(8,128)(2,1)}, f32[8,128]{1,0:T(8,128)S(1)}) custom-call(s32[1]{0:T(128)} %bitcast.phase_ref, s32[1]{0:T(128)} %bitcast.1.core_ref, bf16[256,1536]{1,0:T(8,128)(2,1)S(1)} %copy-done.2, bf16[128,1024]{1,0:T(8,128)(2,1)S(1)} %get-tuple-element.34.own_ref, bf16[128,1024]{1,0:T(8,128)(2,1)S(1)} %collective-permute-done.12.in_ref, ...), custom_call_target="tpu_custom_call" | custom-call | flops 800000000 | bytes 5000000 | tf_op jit(solution)/shard_map/leave/pallas_call | solution.py:370
  94.4 10.2 %all-to-all-done.1.pieces_ref = bf16[32,24,1536]{2,1,0:T(8,128)(2,1)S(1)} async-done(((bf16[32,24,1536]{2,1,0:T(8,128)(2,1)}), bf16[32,24,1536]{2,1,0:T(8,128)(2,1)S(1)}, u32[]{:S(2)}, u32[]{:S(2)}) %all-to-all-start.1) | async-done | bytes 2359328 | tf_op jit(solution)/shard_map/all_to_all | solution.py:509
  (43 shorter events, 7.9 us)
Async XLA Ops:
  0.6 21.7 %copy-start.6 = (f32[1536]{0:T(1024)S(1)}, f32[1536]{0:T(1024)}, u32[]{:S(2)}) copy-start(f32[1536]{0:T(1024)} %param.17) | copy-start | bytes 18436
  1.4 3.0 %collective-permute-start = (bf16[2,2,768]{2,1,0:T(2,128)(2,1)S(1)}, bf16[2,2,768]{2,1,0:T(2,128)(2,1)S(1)}, u32[]{:S(2)}, u32[]{:S(2)}) collective-permute-start(bf16[2,2,768]{2,1,0:T(2,128)(2,1)S(1)} %get-tuple-element.40), channel_id=1, source_target_pairs={{0,2},{2,4},{4,6},{6,8},{8,10},{10,12},{12,14},{14,16},{16,18},{18... | collective-permute-start | bytes 18440 | tf_op jit(solution)/shard_map/ppermute | solution.py:441
  3.2 4.3 %collective-permute-start.1 = (bf16[2,2,768]{2,1,0:T(2,128)(2,1)S(1)}, bf16[2,2,768]{2,1,0:T(2,128)(2,1)S(1)}, u32[]{:S(2)}, u32[]{:S(2)}) collective-permute-start(bf16[2,2,768]{2,1,0:T(2,128)(2,1)S(1)} %get-tuple-element.39), channel_id=1, source_target_pairs={{2,0},{4,2},{6,4},{8,6},{10,8},{12,10},{14,12},{16,14},{18,16},{20... | collective-permute-start | bytes 18440 | tf_op jit(solution)/shard_map/ppermute | solution.py:442
  4.5 3.0 %copy-start.7 = (bf16[2,2,768]{2,1,0:T(2,128)(2,1)}, bf16[2,2,768]{2,1,0:T(2,128)(2,1)S(1)}, u32[]{:S(2)}) copy-start(bf16[2,2,768]{2,1,0:T(2,128)(2,1)S(1)} %collective-permute-done._low.low_ref) | copy-start | bytes 18436
  11.4 39.6 %all-to-all-start = ((bf16[32,2,16,896]{3,2,1,0:T(8,128)(2,1)}), bf16[32,2,16,896]{3,2,1,0:T(8,128)(2,1)S(1)}, u32[]{:S(2)}, u32[]{:S(2)}) async-start(bf16[32,2,16,896]{3,2,1,0:T(8,128)(2,1)} %get-tuple-element.31), calls=%async_computation | async-start | bytes 3670016 | tf_op jit(solution)/shard_map/all_to_all | solution.py:483
  22.9 35.4 %copy-start.9 = (f32[8]{0:T(128)S(1)}, f32[8]{0:T(128)}, u32[]{:S(2)}) copy-start(f32[8]{0:T(128)} %param.21) | copy-start | bytes 100
  33.1 18.6 %copy-start.3 = (bf16[1,2,128,1536]{3,2,1,0:T(8,128)(2,1)S(1)}, bf16[1,2,128,1536]{3,2,1,0:T(8,128)(2,1)}, u32[]{:S(2)}) copy-start(bf16[1,2,128,1536]{3,2,1,0:T(8,128)(2,1)} %param.22) | copy-start | bytes 2359300
  33.1 1.5 %collective-permute-start.3 = (bf16[128,256]{1,0:T(8,128)(2,1)}, bf16[128,256]{1,0:T(8,128)(2,1)S(1)}, u32[]{:S(2)}, u32[]{:S(2)}) collective-permute-start(bf16[128,256]{1,0:T(8,128)(2,1)} %get-tuple-element.26), channel_id=1, source_target_pairs={{0,2},{2,0},{1,3},{3,1},{4,6},{6,4},{5,7},{7,5},{8,10},{10,8},{9,1... | collective-permute-start | bytes 196616 | tf_op jit(solution)/shard_map/ppermute | solution.py:497
  36.1 11.3 %collective-permute-start.4 = (bf16[256,256]{1,0:T(8,128)(2,1)S(1)}, bf16[256,256]{1,0:T(8,128)(2,1)S(1)}, u32[]{:S(2)}, u32[]{:S(2)}) collective-permute-start(bf16[256,256]{1,0:T(8,128)(2,1)S(1)} %get-tuple-element.27.refs_0_), channel_id=1, source_target_pairs={{0,4},{2,18},{4,8},{6,22},{8,12},{10,26},{12,0},{14,30},{16,20},{1... | collective-permute-start | bytes 393224 | tf_op jit(solution)/shard_map/ppermute | solution.py:433
  37.9 9.6 %collective-permute-start.5 = (bf16[256,256]{1,0:T(8,128)(2,1)S(1)}, bf16[256,256]{1,0:T(8,128)(2,1)S(1)}, u32[]{:S(2)}, u32[]{:S(2)}) collective-permute-start(bf16[256,256]{1,0:T(8,128)(2,1)S(1)} %get-tuple-element.27.refs_0_), channel_id=1, source_target_pairs={{0,12},{2,50},{4,0},{6,54},{8,4},{10,58},{12,8},{14,62},{16,28},{1... | collective-permute-start | bytes 393224 | tf_op jit(solution)/shard_map/ppermute | solution.py:433
  39.4 10.8 %collective-permute-start.6 = (bf16[256,256]{1,0:T(8,128)(2,1)S(1)}, bf16[256,256]{1,0:T(8,128)(2,1)S(1)}, u32[]{:S(2)}, u32[]{:S(2)}) collective-permute-start(bf16[256,256]{1,0:T(8,128)(2,1)S(1)} %get-tuple-element.27.refs_0_), channel_id=1, source_target_pairs={{0,8},{2,34},{4,12},{6,38},{8,0},{10,42},{12,4},{14,46},{16,24},{1... | collective-permute-start | bytes 393224 | tf_op jit(solution)/shard_map/ppermute | solution.py:433
  51.6 10.4 %collective-permute-start.11 = (bf16[256,1536]{1,0:T(8,128)(2,1)S(1)}, bf16[256,1536]{1,0:T(8,128)(2,1)S(1)}, u32[]{:S(2)}, u32[]{:S(2)}) collective-permute-start(bf16[256,1536]{1,0:T(8,128)(2,1)S(1)} %ends.1.ends_ref), channel_id=1, source_target_pairs={{0,2},{2,0},{1,3},{3,1},{4,6},{6,4},{5,7},{7,5},{8,10},{10,8},{9,1... | collective-permute-start | bytes 2359304 | tf_op jit(solution)/shard_map/ppermute | solution.py:507
  52.7 5.6 %collective-permute-start.10 = (bf16[16,48,256]{2,1,0:T(8,128)(2,1)}, bf16[16,48,256]{2,1,0:T(8,128)(2,1)S(1)}, u32[]{:S(2)}, u32[]{:S(2)}) collective-permute-start(bf16[16,48,256]{2,1,0:T(8,128)(2,1)} %get-tuple-element.30), channel_id=1, source_target_pairs={{0,2},{2,0},{1,3},{3,1},{4,6},{6,4},{5,7},{7,5},{8,10},{10,8},{9,1... | collective-permute-start | bytes 1179656 | tf_op jit(solution)/shard_map/ppermute | solution.py:504
  53.2 17.8 %collective-permute-start.7 = (bf16[1024,256]{1,0:T(8,128)(2,1)}, bf16[1024,256]{1,0:T(8,128)(2,1)}, u32[]{:S(2)}, u32[]{:S(2)}) collective-permute-start(bf16[1024,256]{1,0:T(8,128)(2,1)} %get-tuple-element.28.refs_0_), channel_id=1, source_target_pairs={{0,16},{2,6},{4,20},{6,10},{8,24},{10,14},{12,28},{14,2},{16,32},{... | collective-permute-start | bytes 1572872 | tf_op jit(solution)/shard_map/ppermute | solution.py:433
  55.0 16.0 %collective-permute-start.8 = (bf16[1024,256]{1,0:T(8,128)(2,1)}, bf16[1024,256]{1,0:T(8,128)(2,1)}, u32[]{:S(2)}, u32[]{:S(2)}) collective-permute-start(bf16[1024,256]{1,0:T(8,128)(2,1)} %get-tuple-element.28.refs_0_), channel_id=1, source_target_pairs={{0,48},{2,14},{4,52},{6,2},{8,56},{10,6},{12,60},{14,10},{16,0},{1... | collective-permute-start | bytes 1572872 | tf_op jit(solution)/shard_map/ppermute | solution.py:433
  56.4 14.5 %collective-permute-start.9 = (bf16[1024,256]{1,0:T(8,128)(2,1)}, bf16[1024,256]{1,0:T(8,128)(2,1)}, u32[]{:S(2)}, u32[]{:S(2)}) collective-permute-start(bf16[1024,256]{1,0:T(8,128)(2,1)} %get-tuple-element.28.refs_0_), channel_id=1, source_target_pairs={{0,32},{2,10},{4,36},{6,14},{8,40},{10,2},{12,44},{14,6},{16,48},{... | collective-permute-start | bytes 1572872 | tf_op jit(solution)/shard_map/ppermute | solution.py:433
  58.3 12.6 %collective-permute-start.2 = (bf16[128,1024]{1,0:T(8,128)(2,1)}, bf16[128,1024]{1,0:T(8,128)(2,1)S(1)}, u32[]{:S(2)}, u32[]{:S(2)}) collective-permute-start(bf16[128,1024]{1,0:T(8,128)(2,1)} %get-tuple-element.24), channel_id=1, source_target_pairs={{0,2},{2,0},{1,3},{3,1},{4,6},{6,4},{5,7},{7,5},{8,10},{10,8},{9,1... | collective-permute-start | bytes 786440 | tf_op jit(solution)/shard_map/ppermute | solution.py:500
  63.4 1.4 %copy-start.1 = (bf16[32,24,1536]{2,1,0:T(8,128)(2,1)}, bf16[32,24,1536]{2,1,0:T(8,128)(2,1)S(1)}, u32[]{:S(2)}) copy-start(bf16[32,24,1536]{2,1,0:T(8,128)(2,1)S(1)} %get-tuple-element.37) | copy-start | bytes 7077892
  64.9 39.8 %all-to-all-start.1 = ((bf16[32,24,1536]{2,1,0:T(8,128)(2,1)}), bf16[32,24,1536]{2,1,0:T(8,128)(2,1)S(1)}, u32[]{:S(2)}, u32[]{:S(2)}) async-start(bf16[32,24,1536]{2,1,0:T(8,128)(2,1)} %copy-done.1), calls=%async_computation.1 | async-start | bytes 4718592 | tf_op jit(solution)/shard_map/all_to_all | solution.py:509
  71.0 1.0 copy-start.5
  71.9 17.1 %copy-start.10 = (f32[256,1536]{1,0:T(8,128)S(1)}, f32[256,1536]{1,0:T(8,128)}, u32[]{:S(2)}) copy-start(f32[256,1536]{1,0:T(8,128)} %fusion.1) | copy-start | bytes 4718596
  88.9 3.7 %copy-start = (bf16[1024,1536]{1,0:T(8,128)(2,1)S(1)}, bf16[1024,1536]{1,0:T(8,128)(2,1)}, u32[]{:S(2)}) copy-start(bf16[1024,1536]{1,0:T(8,128)(2,1)} %exit_ref.1) | copy-start | bytes 9437188
  88.9 3.7 %copy-start.2 = (bf16[256,1536]{1,0:T(8,128)(2,1)S(1)}, bf16[256,1536]{1,0:T(8,128)(2,1)}, u32[]{:S(2)}) copy-start(bf16[256,1536]{1,0:T(8,128)(2,1)} %get-tuple-element.22.rows_ref) | copy-start | bytes 2359300
  88.9 3.6 %collective-permute-start.12 = (bf16[128,1024]{1,0:T(8,128)(2,1)S(1)}, bf16[128,1024]{1,0:T(8,128)(2,1)S(1)}, u32[]{:S(2)}, u32[]{:S(2)}) collective-permute-start(bf16[128,1024]{1,0:T(8,128)(2,1)S(1)} %get-tuple-element.35), channel_id=1, source_target_pairs={{0,2},{2,0},{1,3},{3,1},{4,6},{6,4},{5,7},{7,5},{8,10},{10,8},{9,1... | collective-permute-start | bytes 786440 | tf_op jit(solution)/shard_map/ppermute | solution.py:520
  (2 other events, 1.4 us)

commit v4 on v3

--- a/solution.py
+++ b/solution.py
@@ -43,8 +43,6 @@
     lines_hbm,
     counts_hbm,
     cot_hbm,
-    _low,
-    _high,
     out_ref,
     token_ref,
     ids_ref,
@@ -76,6 +74,7 @@
 
     for copy in copies:
         copy.wait()
+    tags = []
     for b in range(batch):
         ids = ids_ref[b]
         junction = column(ids % junc)
@@ -85,24 +84,27 @@
         )
         valid = slot[:, :1].astype(F32) < count
         junction = jnp.where(valid, junction, -1.0).astype(I32)
-        code = jnp.where(valid, code, -1.0)
+        tags.append(jnp.broadcast_to(jnp.where(valid, code, -1.0), (n, TAG)))
         onehot = (junction == lax.broadcasted_iota(I32, (n, junc), 1)).astype(F32).astype(BF16)
         picked = dot(onehot, cot_ref[b]).astype(BF16)
-        out_ref[:, b, :, :embed] = picked.reshape(shards, slots, embed)
-        tags = jnp.broadcast_to(code, (n, TAG)).astype(BF16)
-        out_ref[:, b, :, embed:] = tags.reshape(shards, slots, TAG)
-
-
-def pick(ids, lines, counts, cotangent, low, high):
+        out_ref[:, :, b * embed : (b + 1) * embed] = picked.reshape(shards, slots, embed)
+    lane = lax.broadcasted_iota(I32, (n, TAG), 1)
+    tag = tags[0]
+    for b in range(1, batch):
+        tag = jnp.where(lane < b * (TAG // batch), tag, tags[b])
+    out_ref[:, :, batch * embed :] = tag.astype(BF16).reshape(shards, slots, TAG)
+
+
+def pick(ids, lines, counts, cotangent):
     batch, slots, shards = ids.shape
     embed = cotangent.shape[2]
     return pl.pallas_call(
         pick_kernel,
         out_shape=(
-            jax.ShapeDtypeStruct((shards, batch, slots, embed + TAG), BF16),
+            jax.ShapeDtypeStruct((shards, slots, batch * embed + TAG), BF16),
             TOKEN,
         ),
-        in_specs=[ANY] * 6,
+        in_specs=[ANY] * 4,
         out_specs=(VMEM, VMEM),
         scratch_shapes=[
             pltpu.VMEM(ids.shape, I32),
@@ -114,17 +116,31 @@
         compiler_params=params(56),
         cost_estimate=cost(2 * 10**8, 3 * 10**6),
         name="pick",
-    )(ids, lines, counts, cotangent, low, high)
-
-
-def ends_kernel(arrived_ref, _, out_ref):
-    shards, batch, slots, wide = arrived_ref.shape
-    embed = wide - TAG
+    )(ids, lines, counts, cotangent)
+
+
+def follow(value, *after):
+    return pl.pallas_call(
+        lambda *refs: None,
+        out_shape=jax.ShapeDtypeStruct(value.shape, value.dtype),
+        in_specs=[ANY] * (1 + len(after)),
+        out_specs=ANY,
+        input_output_aliases={0: 0},
+        name="follow",
+    )(value, *after)
+
+
+def ends_kernel(arrived_ref, _token, _other, out_ref):
+    shards, slots, wide = arrived_ref.shape
+    embed = out_ref.shape[1] // 2
+    batch = (wide - TAG) // embed
     n = shards * slots
     rows = out_ref.shape[0] // batch
+    tags = arrived_ref[:, :, batch * embed :].reshape(n, TAG).astype(F32)
     for b in range(batch):
-        data = arrived_ref[:, b, :, :embed].reshape(n, embed)
-        tag = arrived_ref[:, b, :, embed:].reshape(n, TAG).astype(F32)
+        data = arrived_ref[:, :, b * embed : (b + 1) * embed].reshape(n, embed)
+        lane = b * (TAG // batch)
+        tag = jnp.broadcast_to(tags[:, lane : lane + 1], (n, rows))
         for kind in range(2):
             target = lax.broadcasted_iota(I32, (n, rows), 1) + kind * rows
             onehot = (tag == target.astype(F32)).astype(F32).astype(BF16)
@@ -133,17 +149,44 @@
             ).astype(BF16)
 
 
-def make_ends(arrived, rows, after):
-    batch, embed = arrived.shape[1], arrived.shape[3] - TAG
+def make_ends(arrived, batch, rows, token, other):
+    embed = (arrived.shape[2] - TAG) // batch
     return pl.pallas_call(
         ends_kernel,
         out_shape=jax.ShapeDtypeStruct((batch * rows, 2 * embed), BF16),
-        in_specs=[VMEM, ANY],
+        in_specs=[VMEM, ANY, ANY],
         out_specs=VMEM,
-        compiler_params=params(32),
+        compiler_params=params(24),
         cost_estimate=cost(4 * 10**8, 3 * 10**6),
         name="ends",
-    )(arrived, after)
+    )(arrived, token, other)
+
+
+def row_grad_kernel(ends_ref, head_ref, _token, out_ref):
+    embed = head_ref.shape[2]
+    total = dot(ends_ref[:, :embed], head_ref[0], NT)
+    total = total + dot(ends_ref[:, embed:], head_ref[1], NT)
+    out_ref[...] = total.astype(BF16)
+
+
+def make_row_grad(ends, head, token):
+    n, both = ends.shape
+    width, embed = head.shape[1:]
+    step = 512
+    return pl.pallas_call(
+        row_grad_kernel,
+        grid=(width // step,),
+        out_shape=jax.ShapeDtypeStruct((n, width), BF16),
+        in_specs=[
+            pl.BlockSpec((n, both), lambda i: (0, 0)),
+            pl.BlockSpec((2, step, embed), lambda i: (0, i, 0)),
+            ANY,
+        ],
+        out_specs=pl.BlockSpec((n, step), lambda i: (0, i)),
+        compiler_params=params(24),
+        cost_estimate=cost(1.2 * 10**9, 6 * 10**6),
+        name="row_grad",
+    )(ends, head, token)
 
 
 def turn_kernel(core_ref, lines_ref, mine_ref, other_ref):
@@ -235,12 +278,15 @@
         pad[b, base + cells : base + cells + extent, :] = high_ref[b].astype(F32)
     copies[1].wait()
     for b in range(batch):
-        total = dot(x_ref[b], taps[1])
-        total += dot(pad[b, base - extent : base - extent + cells, :].astype(BF16), taps[0])
-        total += dot(pad[b, base + extent : base + extent + cells, :].astype(BF16), taps[2])
-        total = pad[b, base : base + cells, :] + jax.nn.gelu(total)
-        for j in range(hidden.shape[0]):
-            hidden[j, b * cells : (b + 1) * cells, :] = total[:, j * 128 : (j + 1) * 128]
+        before = pad[b, base - extent : base - extent + cells, :].astype(BF16)
+        behind = pad[b, base + extent : base + extent + cells, :].astype(BF16)
+        for j in range(0, chans, 256):
+            span = slice(j, j + 256)
+            total = dot(x_ref[b], taps[1, :, span])
+            total += dot(before, taps[0, :, span]) + dot(behind, taps[2, :, span])
+            total = pad[b, base : base + cells, span] + jax.nn.gelu(total)
+            for i in range(0, 256, 128):
+                hidden[(j + i) // 128, b * cells : (b + 1) * cells, :] = total[:, i : i + 128]
     n = batch * cells // 2
     pooled = jnp.concatenate(
         [
@@ -299,47 +345,52 @@
     )(core.reshape(1), low, high, gain.reshape(1, width), x, taps, merge, look, ask, after)
 
 
-def attend_kernel(
-    phase_ref, logit_ref, query_own_ref, query_in_ref, *refs
-):
-    keys, (_, own_ref, out_ref) = refs[:-3], refs[-3:]
+def attend_kernel(phase_ref, logit_ref, query_own_ref, query_in_ref, *refs):
+    keys, (_, own_ref, out_ref, key_t, value) = refs[:-5], refs[-5:]
     rows, width = query_own_ref.shape
-    lane = keys[0].shape[1] // 2
-    pieces = [key.at[i : i + 512] for key in keys for i in range(0, key.shape[0], 512)]
-
-    def head(h):
-        span = pl.ds(pl.multiple_of(h * lane, lane), lane)
-        query = jnp.concatenate([query_own_ref[:, span], query_in_ref[:, span]], axis=0)
-        factor = logit_ref[h]
-        scores = [dot(query, piece[:, :lane], NT) for piece in pieces]
-        top = functools.reduce(jnp.maximum, scores)
-        top = jnp.max(top, axis=-1, keepdims=True) * factor
-        mixed, total = 0.0, 0.0
-        for score, piece in zip(scores, pieces):
-            expo = jnp.exp2(score * factor - top)
-            total = total + expo
-            mixed = mixed + dot(expo.astype(BF16), piece[:, lane:])
-        total = jnp.sum(total, axis=-1, keepdims=True)
-        mixed = (mixed / total).astype(BF16)
-        own_ref[:, span] = mixed[:rows]
-        out_ref[:, span] = mixed[rows:]
+    n, both = keys[0].shape
+    lane = both // 2
+    count = n * len(keys)
+    chunk = 512
 
     @pl.when(phase_ref[0] == 1)
     def _():
-        @pl.loop(0, width // lane // 2)
-        def _(i):
-            head(2 * i)
-            head(2 * i + 1)
+        for i, block in enumerate(keys):
+            span = slice(i * n, (i + 1) * n)
+            turned = block[:, :lane].T
+            key_t[:lane, span] = turned
+            key_t[lane:, span] = turned
+            value[span, :lane] = block[:, lane:]
+            value[span, lane:] = jnp.ones((n, lane), BF16)
+        for head in range(width // lane):
+            span = slice(head * lane, (head + 1) * lane)
+            query = jnp.concatenate([query_own_ref[:, span], query_in_ref[:, span]], axis=0)
+            query = query.astype(F32) * logit_ref[head]
+            coarse = query.astype(BF16)
+            fine = (query - coarse.astype(F32)).astype(BF16)
+            query = jnp.concatenate([coarse, fine], axis=1)
+            scores = [dot(query, key_t[:, j : j + chunk]) for j in range(0, count, chunk)]
+            top = jnp.max(functools.reduce(jnp.maximum, scores), axis=-1, keepdims=True)
+            mixed = 0.0
+            for j, score in enumerate(scores):
+                weight = jnp.exp2(score - top).astype(BF16)
+                mixed = mixed + dot(weight, value[j * chunk : (j + 1) * chunk, :])
+            mixed = (mixed[:, :lane] / mixed[:, lane:]).astype(BF16)
+            own_ref[:, span] = mixed[:rows]
+            out_ref[:, span] = mixed[rows:]
 
 
 def attend(phase, logit, query_own, query_in, keys, after):
     shape = jax.ShapeDtypeStruct(query_own.shape, BF16)
+    n, both = keys[0].shape
+    count = n * len(keys)
     return pl.pallas_call(
         attend_kernel,
         out_shape=(shape, shape),
         in_specs=[SMEM, SMEM] + [VMEM] * (2 + len(keys)) + [ANY],
         out_specs=(VMEM, VMEM),
-        compiler_params=params(24),
+        scratch_shapes=[pltpu.VMEM((both, count), BF16), pltpu.VMEM((count, both), BF16)],
+        compiler_params=params(32),
         cost_estimate=cost(6 * 10**10, 4 * 10**6),
         name="attend",
     )(phase.reshape(1), logit, query_own, query_in, *keys, after)
@@ -434,13 +485,11 @@
     return received
 
 
-def halo(block, width):
+def halo(first, last):
     count = lax.axis_size(SEQ)
     forward = [(i, i + 1) for i in range(count - 1)]
     backward = [(b, a) for a, b in forward]
-    low = lax.ppermute(block[:, -width:], SEQ, forward)
-    high = lax.ppermute(block[:, :width], SEQ, backward)
-    return low, high
+    return lax.ppermute(last, SEQ, forward), lax.ppermute(first, SEQ, backward)
 
 
 def body(
@@ -466,20 +515,19 @@
     width = merged_bin_projector.shape[1]
     extent = DILATION_STEP * (spaced_filter_coefs.shape[0] // 2)
     lane = common_lookup_projector.shape[1] // 2
-    embed = couple_embedding_cotangent.shape[3]
     shards = site_locator_code.shape[3]
     swap = [(0, 1), (1, 0)]
     side = lax.axis_size("y")
 
-    low, high = halo(bin_activations, extent)
+    first, last = bin_activations[:, :extent], bin_activations[:, -extent:]
+    low, high = halo(first, last)
     payload, picked = pick(
         jnp.swapaxes(site_locator_code[0, :, 0], 1, 2),
         jnp.swapaxes(site_local_line[0, :, 0], 1, 2),
         filled_slot_totals[0, :, 0],
         couple_embedding_cotangent[0],
-        low,
-        high,
     )
+    payload = follow(payload, low, high)
     arrived = lax.all_to_all(payload, SEQ, 0, 0, tiled=True)
 
     encoded, key_own, key_out, query_own, query_out, _ = encode(
@@ -503,15 +551,12 @@
     mine, other = turn(core, portion, shards // 2)
     other = lax.ppermute(other, "core", swap)
 
-    ends = make_ends(arrived, rows, line_done)
+    ends = make_ends(arrived, batch, rows, line_done, other)
     ends_other = lax.ppermute(ends, "core", swap)
     partial, terms_done = partial_grad(mine, other, ends, ends_other, shards)
     pieces = lax.all_to_all(partial, ("y", "x", "dp"), 0, 0, tiled=True)
 
-    row_grad = (
-        dot(ends[:, :embed], splice_site_projector[0], NT)
-        + dot(ends[:, embed:], splice_site_projector[1], NT)
-    ).astype(BF16)
+    row_grad = make_row_grad(ends, splice_site_projector, terms_done)
     row_grad = row_grad.reshape(batch, rows, width)[None]
 
     logit = lane_logit_factor * (math.log2(math.e) / math.sqrt(lane))

time: 106 us -> 98.2 us (0.926)
  matrix products: 7.16 us -> 0 us
  Pallas kernels: 37.8 us -> 34.2 us
  local copies, waits for them, and re-layouts: 5.17 us -> 6.56 us
    dot_general x2 -> x0, matrix products: 7.16 us -> none  [dot(): return lax.dot_general(a, b, dims, preferred_element_type=F32)]
    pallas_call x1, Pallas kernels: 17 us -> 12.5 us  [attend(): pl.pallas_call(attend_kernel, out_shape=(shape, shape), in_specs=[SMEM, S...]
    ppermute x2, waiting for transfers between devices: 3.02 us -> 0.01 us  [the longest x1 0.01 us: halo(): lax.ppermute(last, SEQ, forward)]
    pallas_call x1 -> x3, Pallas kernels: 3.32 us -> 6.15 us  [the longest x1 3.28 us: pick(): pl.pallas_call(pick_kernel, out_shape=(jax.ShapeDtypeStruct((shards, slot...]
    ppermute x6, waiting for transfers between devices: 8.7 us -> 11 us  [spread(): received.append(lax.ppermute(block, SEQ, pairs))]
    all_to_all x1, waiting for transfers between devices: 10.2 us -> 11.8 us  [body(): pieces = lax.all_to_all(partial, ('y', 'x', 'dp'), 0, 0, tiled=True)]
    unnamed x22, local copies, waits for them, and re-layouts: 3.8 us -> 5.19 us
    pallas_call x1, Pallas kernels: 10.2 us -> 8.93 us  [encode(): pl.pallas_call(encoder_kernel, out_shape=(jax.ShapeDtypeStruct((n, width)...]
  transfers between devices with their start and end apart: 15 -> 15, of which waited for: 5 -> 5; matrix products, arithmetic and copies ran while one was open for 7% -> 1% of each run, Pallas kernels for 31% -> 33%
where the time goes in v4:
time: 98.2 us; the launch traced here: 97.2 us
  Pallas kernels  34.2 us (35%)
  starting transfers between devices  31.5 us (32%)
  waiting for transfers between devices  24.1 us (25%)
  local copies, waits for them, and re-layouts  6.56 us (7%)
    pallas_call x1, Pallas kernels, attend(): pl.pallas_call(attend_kernel, out_shape=(shape, shape), in_specs=[SMEM, S...  12.5 us
    all_to_all x1, waiting for transfers between devices, body(): pieces = lax.all_to_all(partial, ('y', 'x', 'dp'), 0, 0, tiled=True)  11.8 us
    ppermute x6, waiting for transfers between devices, spread(): received.append(lax.ppermute(block, SEQ, pairs))  11 us
    all_to_all x1, starting transfers between devices, body(): arrived = lax.all_to_all(payload, SEQ, 0, 0, tiled=True)  10.7 us
    ppermute x6, starting transfers between devices, spread(): received.append(lax.ppermute(block, SEQ, pairs))  10.3 us
    pallas_call x1, Pallas kernels, encode(): pl.pallas_call(encoder_kernel, out_shape=(jax.ShapeDtypeStruct((n, width)...  8.93 us
    all_to_all x1, starting transfers between devices, body(): pieces = lax.all_to_all(partial, ('y', 'x', 'dp'), 0, 0, tiled=True)  6.61 us
    unnamed x22, local copies, waits for them, and re-layouts  5.19 us
  transfers between devices with their start and end apart: 15, of which 5 were waited for; matrix products, arithmetic and copies ran while one was open for 1% of the time, Pallas kernels for 33%

profile of v4, /device:TPU:64, one launch (start us, length us, event | category | flops | bytes accessed | tf_op | source)
XLA Modules:
  0.0 97.2 jit_solution(15069854471135450000)
XLA Ops:
  1.4 1.7 %collective-permute-start = (bf16[2,2,768]{2,1,0:T(2,128)(2,1)S(1)}, bf16[2,2,768]{2,1,0:T(2,128)(2,1)S(1)}, u32[]{:S(2)}, u32[]{:S(2)}) collective-permute-start(bf16[2,2,768]{2,1,0:T(2,128)(2,1)S(1)} %get-tuple-element.40), channel_id=1, source_target_pairs={{0,2},{2,4},{4,6},{6,8},{8,10},{10,12},{12,14},{14,16},{16,18},{18... | collective-permute-start | bytes 18440 | tf_op jit(solution)/shard_map/ppermute | solution.py:492
  3.1 1.3 %collective-permute-start.1 = (bf16[2,2,768]{2,1,0:T(2,128)(2,1)S(1)}, bf16[2,2,768]{2,1,0:T(2,128)(2,1)S(1)}, u32[]{:S(2)}, u32[]{:S(2)}) collective-permute-start(bf16[2,2,768]{2,1,0:T(2,128)(2,1)S(1)} %get-tuple-element.39), channel_id=1, source_target_pairs={{2,0},{4,2},{6,4},{8,6},{10,8},{12,10},{14,12},{16,14},{18,16},{20... | collective-permute-start | bytes 18440 | tf_op jit(solution)/shard_map/ppermute | solution.py:492
  4.5 3.3 %pick.1 = (bf16[32,16,1664]{2,1,0:T(8,128)(2,1)}, f32[8,128]{1,0:T(8,128)}) custom-call(s32[2,16,32]{2,1,0:T(8,128)} %bitcast.19, s32[2,16,32]{2,1,0:T(8,128)} %bitcast.20, s32[2,32]{1,0:T(2,128)} %bitcast.21, bf16[2,128,768]{2,1,0:T(8,128)(2,1)} %bitcast.18), custom_call_target="tpu_custom_call" | custom-call | flops 200000000 | bytes 3000000 | tf_op jit(solution)/shard_map/pick/pallas_call | solution.py:101
  8.4 10.7 %all-to-all-start = ((bf16[32,16,1664]{2,1,0:T(8,128)(2,1)}), bf16[32,16,1664]{2,1,0:T(8,128)(2,1)S(1)}, u32[]{:S(2)}, u32[]{:S(2)}) async-start(bf16[32,16,1664]{2,1,0:T(8,128)(2,1)} %follow.1), calls=%async_computation | async-start | bytes 3407872 | tf_op jit(solution)/shard_map/all_to_all | solution.py:531
  20.3 8.9 %encode.1 = (bf16[256,1536]{1,0:T(8,128)(2,1)}, bf16[128,256]{1,0:T(8,128)(2,1)}, bf16[128,256]{1,0:T(8,128)(2,1)}, bf16[128,1024]{1,0:T(8,128)(2,1)}, bf16[128,1024]{1,0:T(8,128)(2,1)}, /*index=5*/f32[8,128]{1,0:T(8,128)}) custom-call(s32[1]{0:T(128)} %bitcast.1.core_ref, bf16[2,2,768]{2,1,0:T(2,128)(2,1)} %copy-done.8, bf16[2,2,768]{2,1,0:T(2,128)(2,1)} %copy-done.9, ...), custom_call_target="tpu_custom_call" | custom-call | flops 3400000000 | bytes 12000000 | tf_op jit(solution)/shard_map/encode/pallas_call | solution.py:326
  29.6 1.2 %collective-permute-done.3.refs_1_ = bf16[128,256]{1,0:T(8,128)(2,1)S(1)} collective-permute-done((bf16[128,256]{1,0:T(8,128)(2,1)}, bf16[128,256]{1,0:T(8,128)(2,1)S(1)}, u32[]{:S(2)}, u32[]{:S(2)}) %collective-permute-start.3) | collective-permute-done | bytes 65568 | tf_op jit(solution)/shard_map/ppermute | solution.py:545
  32.3 1.7 %collective-permute-start.4 = (bf16[256,256]{1,0:T(8,128)(2,1)S(1)}, bf16[256,256]{1,0:T(8,128)(2,1)S(1)}, u32[]{:S(2)}, u32[]{:S(2)}) collective-permute-start(bf16[256,256]{1,0:T(8,128)(2,1)S(1)} %get-tuple-element.27.refs_0_), channel_id=1, source_target_pairs={{0,4},{2,18},{4,8},{6,22},{8,12},{10,26},{12,0},{14,30},{16,20},{1... | collective-permute-start | bytes 393224 | tf_op jit(solution)/shard_map/ppermute | solution.py:484
  33.9 1.6 %collective-permute-start.5 = (bf16[256,256]{1,0:T(8,128)(2,1)S(1)}, bf16[256,256]{1,0:T(8,128)(2,1)S(1)}, u32[]{:S(2)}, u32[]{:S(2)}) collective-permute-start(bf16[256,256]{1,0:T(8,128)(2,1)S(1)} %get-tuple-element.27.refs_0_), channel_id=1, source_target_pairs={{0,12},{2,50},{4,0},{6,54},{8,4},{10,58},{12,8},{14,62},{16,28},{1... | collective-permute-start | bytes 393224 | tf_op jit(solution)/shard_map/ppermute | solution.py:484
  35.5 2.0 %collective-permute-start.6 = (bf16[256,256]{1,0:T(8,128)(2,1)S(1)}, bf16[256,256]{1,0:T(8,128)(2,1)S(1)}, u32[]{:S(2)}, u32[]{:S(2)}) collective-permute-start(bf16[256,256]{1,0:T(8,128)(2,1)S(1)} %get-tuple-element.27.refs_0_), channel_id=1, source_target_pairs={{0,8},{2,34},{4,12},{6,38},{8,0},{10,42},{12,4},{14,46},{16,24},{1... | collective-permute-start | bytes 393224 | tf_op jit(solution)/shard_map/ppermute | solution.py:484
  37.5 5.4 %collective-permute-done.4.refs_1_ = bf16[256,256]{1,0:T(8,128)(2,1)S(1)} collective-permute-done((bf16[256,256]{1,0:T(8,128)(2,1)S(1)}, bf16[256,256]{1,0:T(8,128)(2,1)S(1)}, u32[]{:S(2)}, u32[]{:S(2)}) %collective-permute-start.4) | collective-permute-done | bytes 131104 | tf_op jit(solution)/shard_map/ppermute | solution.py:484
  42.9 2.7 %collective-permute-done.6.refs_3_ = bf16[256,256]{1,0:T(8,128)(2,1)S(1)} collective-permute-done((bf16[256,256]{1,0:T(8,128)(2,1)S(1)}, bf16[256,256]{1,0:T(8,128)(2,1)S(1)}, u32[]{:S(2)}, u32[]{:S(2)}) %collective-permute-start.6) | collective-permute-done | bytes 131104 | tf_op jit(solution)/shard_map/ppermute | solution.py:484
  47.2 1.7 %collective-permute-start.7 = (bf16[1024,256]{1,0:T(8,128)(2,1)}, bf16[1024,256]{1,0:T(8,128)(2,1)}, u32[]{:S(2)}, u32[]{:S(2)}) collective-permute-start(bf16[1024,256]{1,0:T(8,128)(2,1)} %get-tuple-element.28.refs_0_), channel_id=1, source_target_pairs={{0,16},{2,6},{4,20},{6,10},{8,24},{10,14},{12,28},{14,2},{16,32},{... | collective-permute-start | bytes 1572872 | tf_op jit(solution)/shard_map/ppermute | solution.py:484
  48.9 1.6 %collective-permute-start.8 = (bf16[1024,256]{1,0:T(8,128)(2,1)}, bf16[1024,256]{1,0:T(8,128)(2,1)}, u32[]{:S(2)}, u32[]{:S(2)}) collective-permute-start(bf16[1024,256]{1,0:T(8,128)(2,1)} %get-tuple-element.28.refs_0_), channel_id=1, source_target_pairs={{0,48},{2,14},{4,52},{6,2},{8,56},{10,6},{12,60},{14,10},{16,0},{1... | collective-permute-start | bytes 1572872 | tf_op jit(solution)/shard_map/ppermute | solution.py:484
  50.5 1.8 %collective-permute-start.9 = (bf16[1024,256]{1,0:T(8,128)(2,1)}, bf16[1024,256]{1,0:T(8,128)(2,1)}, u32[]{:S(2)}, u32[]{:S(2)}) collective-permute-start(bf16[1024,256]{1,0:T(8,128)(2,1)} %get-tuple-element.28.refs_0_), channel_id=1, source_target_pairs={{0,32},{2,10},{4,36},{6,14},{8,40},{10,2},{12,44},{14,6},{16,48},{... | collective-permute-start | bytes 1572872 | tf_op jit(solution)/shard_map/ppermute | solution.py:484
  52.3 1.4 %partial_grad.1 = (bf16[32,24,1536]{2,1,0:T(8,128)(2,1)S(1)}, f32[8,128]{1,0:T(8,128)S(1)}) custom-call(bf16[16,48,256]{2,1,0:T(8,128)(2,1)S(1)} %get-tuple-element.29.mine_ref, bf16[16,48,256]{2,1,0:T(8,128)(2,1)S(1)} %collective-permute-done.10._other.other_ref, bf16[256,1536]{1,0:T(8,128)(2,1)S(1)} %ends.1.ends_ref, ...), custom_call_target="tpu_custom_call" | custom-call | flops 1200000000 | bytes 5000000 | tf_op jit(solution)/shard_map/partial_grad/pallas_call | solution.py:225
  53.7 1.4 %copy-done.2 = bf16[32,24,1536]{2,1,0:T(8,128)(2,1)} copy-done((bf16[32,24,1536]{2,1,0:T(8,128)(2,1)}, bf16[32,24,1536]{2,1,0:T(8,128)(2,1)S(1)}, u32[]{:S(2)}) %copy-start.2) | copy-done | bytes 2359320
  55.1 6.6 %all-to-all-start.1 = ((bf16[32,24,1536]{2,1,0:T(8,128)(2,1)}), bf16[32,24,1536]{2,1,0:T(8,128)(2,1)S(1)}, u32[]{:S(2)}, u32[]{:S(2)}) async-start(bf16[32,24,1536]{2,1,0:T(8,128)(2,1)} %copy-done.2), calls=%async_computation.1 | async-start | bytes 4718592 | tf_op jit(solution)/shard_map/all_to_all | solution.py:557
  61.8 2.9 %collective-permute-done.9.refs_3_ = bf16[1024,256]{1,0:T(8,128)(2,1)} collective-permute-done((bf16[1024,256]{1,0:T(8,128)(2,1)}, bf16[1024,256]{1,0:T(8,128)(2,1)}, u32[]{:S(2)}, u32[]{:S(2)}) %collective-permute-start.9) | collective-permute-done | bytes 524320 | tf_op jit(solution)/shard_map/ppermute | solution.py:484
  64.7 12.5 %attend.1 = (bf16[128,1024]{1,0:T(8,128)(2,1)S(1)}, bf16[128,1024]{1,0:T(8,128)(2,1)S(1)}) custom-call(s32[1]{0:T(128)} %bitcast.phase_ref, f32[8]{0:T(128)S(1)} %broadcast_multiply_fusion.logit_ref, bf16[128,1024]{1,0:T(8,128)(2,1)S(1)} %copy-done.6, bf16[128,1024]{1,0:T(8,128)(2,1)} %collective-permute-done.2.query_in_ref, ...), custom_call_target="tpu_custom_call" | custom-call | flops 60000002048 | bytes 4000000 | tf_op jit(solution)/shard_map/attend/pallas_call | solution.py:387
  77.3 2.3 %copy-done = bf16[2,1536,768]{2,1,0:T(8,128)(2,1)S(1)} copy-done((bf16[2,1536,768]{2,1,0:T(8,128)(2,1)S(1)}, bf16[2,1536,768]{2,1,0:T(8,128)(2,1)}, u32[]{:S(2)}) %copy-start) | copy-done | bytes 4718616
  79.6 2.9 %row_grad.1 = bf16[256,1536]{1,0:T(8,128)(2,1)} custom-call(bf16[256,1536]{1,0:T(8,128)(2,1)S(1)} %ends.1.ends_ref, bf16[2,1536,768]{2,1,0:T(8,128)(2,1)S(1)} %copy-done, f32[8,128]{1,0:T(8,128)S(1)} %get-tuple-element.33.refs_4_._token), custom_call_target="tpu_custom_call" | custom-call | flops 1200000000 | bytes 6000000 | tf_op jit(solution)/shard_map/row_grad/pallas_call | solution.py:176
  82.5 1.9 %leave.1 = (bf16[256,1536]{1,0:T(8,128)(2,1)}, f32[8,128]{1,0:T(8,128)S(1)}) custom-call(s32[1]{0:T(128)} %bitcast.phase_ref, s32[1]{0:T(128)} %bitcast.1.core_ref, bf16[256,1536]{1,0:T(8,128)(2,1)S(1)} %copy-done.3, bf16[128,1024]{1,0:T(8,128)(2,1)S(1)} %get-tuple-element.34.own_ref, bf16[128,1024]{1,0:T(8,128)(2,1)S(1)} %collective-permute-done.12.in_ref, ...), custom_call_target="tpu_custom_call" | custom-call | flops 800000000 | bytes 5000000 | tf_op jit(solution)/shard_map/leave/pallas_call | solution.py:421
  84.4 11.8 %all-to-all-done.1.pieces_ref = bf16[32,24,1536]{2,1,0:T(8,128)(2,1)S(1)} async-done(((bf16[32,24,1536]{2,1,0:T(8,128)(2,1)}), bf16[32,24,1536]{2,1,0:T(8,128)(2,1)S(1)}, u32[]{:S(2)}, u32[]{:S(2)}) %all-to-all-start.1) | async-done | bytes 2359328 | tf_op jit(solution)/shard_map/all_to_all | solution.py:557
  96.2 1.0 %sum_terms.1 = f32[2,24,768]{2,1,0:T(8,128)} custom-call(bf16[32,24,1536]{2,1,0:T(8,128)(2,1)S(1)} %all-to-all-done.1.pieces_ref, f32[8,128]{1,0:T(8,128)S(1)} %get-tuple-element.38._), custom_call_target="tpu_custom_call" | custom-call | flops 1000000 | bytes 3000000 | tf_op jit(solution)/shard_map/sum_terms/pallas_call | solution.py:441
  (43 shorter events, 6.1 us)
Async XLA Ops:
  1.4 6.3 %collective-permute-start = (bf16[2,2,768]{2,1,0:T(2,128)(2,1)S(1)}, bf16[2,2,768]{2,1,0:T(2,128)(2,1)S(1)}, u32[]{:S(2)}, u32[]{:S(2)}) collective-permute-start(bf16[2,2,768]{2,1,0:T(2,128)(2,1)S(1)} %get-tuple-element.40), channel_id=1, source_target_pairs={{0,2},{2,4},{4,6},{6,8},{8,10},{10,12},{12,14},{14,16},{16,18},{18... | collective-permute-start | bytes 18440 | tf_op jit(solution)/shard_map/ppermute | solution.py:492
  3.1 4.6 %collective-permute-start.1 = (bf16[2,2,768]{2,1,0:T(2,128)(2,1)S(1)}, bf16[2,2,768]{2,1,0:T(2,128)(2,1)S(1)}, u32[]{:S(2)}, u32[]{:S(2)}) collective-permute-start(bf16[2,2,768]{2,1,0:T(2,128)(2,1)S(1)} %get-tuple-element.39), channel_id=1, source_target_pairs={{2,0},{4,2},{6,4},{8,6},{10,8},{12,10},{14,12},{16,14},{18,16},{20... | collective-permute-start | bytes 18440 | tf_op jit(solution)/shard_map/ppermute | solution.py:492
  8.4 10.7 %copy-start.4 = (bf16[1,2,128,1536]{3,2,1,0:T(8,128)(2,1)S(1)}, bf16[1,2,128,1536]{3,2,1,0:T(8,128)(2,1)}, u32[]{:S(2)}) copy-start(bf16[1,2,128,1536]{3,2,1,0:T(8,128)(2,1)} %param.22) | copy-start | bytes 2359300
  8.4 11.4 %copy-start.7 = (f32[1536]{0:T(1024)S(1)}, f32[1536]{0:T(1024)}, u32[]{:S(2)}) copy-start(f32[1536]{0:T(1024)} %param.17) | copy-start | bytes 18436
  8.4 38.0 %all-to-all-start = ((bf16[32,16,1664]{2,1,0:T(8,128)(2,1)}), bf16[32,16,1664]{2,1,0:T(8,128)(2,1)S(1)}, u32[]{:S(2)}, u32[]{:S(2)}) async-start(bf16[32,16,1664]{2,1,0:T(8,128)(2,1)} %follow.1), calls=%async_computation | async-start | bytes 3407872 | tf_op jit(solution)/shard_map/all_to_all | solution.py:531
  19.4 27.0 %collective-permute-start.10 = (bf16[16,48,256]{2,1,0:T(8,128)(2,1)S(1)}, bf16[16,48,256]{2,1,0:T(8,128)(2,1)S(1)}, u32[]{:S(2)}, u32[]{:S(2)}) collective-permute-start(bf16[16,48,256]{2,1,0:T(8,128)(2,1)S(1)} %get-tuple-element.30), channel_id=1, source_target_pairs={{0,2},{2,0},{1,3},{3,1},{4,6},{6,4},{5,7},{7,5},{8,10},{10,8},{9,1... | collective-permute-start | bytes 1179656 | tf_op jit(solution)/shard_map/ppermute | solution.py:552
  29.3 23.0 %copy-start.10 = (f32[8]{0:T(128)S(1)}, f32[8]{0:T(128)}, u32[]{:S(2)}) copy-start(f32[8]{0:T(128)} %param.21) | copy-start | bytes 100
  29.3 1.5 %collective-permute-start.3 = (bf16[128,256]{1,0:T(8,128)(2,1)}, bf16[128,256]{1,0:T(8,128)(2,1)S(1)}, u32[]{:S(2)}, u32[]{:S(2)}) collective-permute-start(bf16[128,256]{1,0:T(8,128)(2,1)} %get-tuple-element.26), channel_id=1, source_target_pairs={{0,2},{2,0},{1,3},{3,1},{4,6},{6,4},{5,7},{7,5},{8,10},{10,8},{9,1... | collective-permute-start | bytes 196616 | tf_op jit(solution)/shard_map/ppermute | solution.py:545
  30.8 0.8 copy-start.5
  32.3 10.6 %collective-permute-start.4 = (bf16[256,256]{1,0:T(8,128)(2,1)S(1)}, bf16[256,256]{1,0:T(8,128)(2,1)S(1)}, u32[]{:S(2)}, u32[]{:S(2)}) collective-permute-start(bf16[256,256]{1,0:T(8,128)(2,1)S(1)} %get-tuple-element.27.refs_0_), channel_id=1, source_target_pairs={{0,4},{2,18},{4,8},{6,22},{8,12},{10,26},{12,0},{14,30},{16,20},{1... | collective-permute-start | bytes 393224 | tf_op jit(solution)/shard_map/ppermute | solution.py:484
  33.9 8.9 %collective-permute-start.5 = (bf16[256,256]{1,0:T(8,128)(2,1)S(1)}, bf16[256,256]{1,0:T(8,128)(2,1)S(1)}, u32[]{:S(2)}, u32[]{:S(2)}) collective-permute-start(bf16[256,256]{1,0:T(8,128)(2,1)S(1)} %get-tuple-element.27.refs_0_), channel_id=1, source_target_pairs={{0,12},{2,50},{4,0},{6,54},{8,4},{10,58},{12,8},{14,62},{16,28},{1... | collective-permute-start | bytes 393224 | tf_op jit(solution)/shard_map/ppermute | solution.py:484
  35.5 10.1 %collective-permute-start.6 = (bf16[256,256]{1,0:T(8,128)(2,1)S(1)}, bf16[256,256]{1,0:T(8,128)(2,1)S(1)}, u32[]{:S(2)}, u32[]{:S(2)}) collective-permute-start(bf16[256,256]{1,0:T(8,128)(2,1)S(1)} %get-tuple-element.27.refs_0_), channel_id=1, source_target_pairs={{0,8},{2,34},{4,12},{6,38},{8,0},{10,42},{12,4},{14,46},{16,24},{1... | collective-permute-start | bytes 393224 | tf_op jit(solution)/shard_map/ppermute | solution.py:484
  47.1 5.2 %collective-permute-start.11 = (bf16[256,1536]{1,0:T(8,128)(2,1)S(1)}, bf16[256,1536]{1,0:T(8,128)(2,1)S(1)}, u32[]{:S(2)}, u32[]{:S(2)}) collective-permute-start(bf16[256,1536]{1,0:T(8,128)(2,1)S(1)} %ends.1.ends_ref), channel_id=1, source_target_pairs={{0,2},{2,0},{1,3},{3,1},{4,6},{6,4},{5,7},{7,5},{8,10},{10,8},{9,1... | collective-permute-start | bytes 2359304 | tf_op jit(solution)/shard_map/ppermute | solution.py:555
  47.2 14.6 %collective-permute-start.7 = (bf16[1024,256]{1,0:T(8,128)(2,1)}, bf16[1024,256]{1,0:T(8,128)(2,1)}, u32[]{:S(2)}, u32[]{:S(2)}) collective-permute-start(bf16[1024,256]{1,0:T(8,128)(2,1)} %get-tuple-element.28.refs_0_), channel_id=1, source_target_pairs={{0,16},{2,6},{4,20},{6,10},{8,24},{10,14},{12,28},{14,2},{16,32},{... | collective-permute-start | bytes 1572872 | tf_op jit(solution)/shard_map/ppermute | solution.py:484
  48.9 12.9 %collective-permute-start.8 = (bf16[1024,256]{1,0:T(8,128)(2,1)}, bf16[1024,256]{1,0:T(8,128)(2,1)}, u32[]{:S(2)}, u32[]{:S(2)}) collective-permute-start(bf16[1024,256]{1,0:T(8,128)(2,1)} %get-tuple-element.28.refs_0_), channel_id=1, source_target_pairs={{0,48},{2,14},{4,52},{6,2},{8,56},{10,6},{12,60},{14,10},{16,0},{1... | collective-permute-start | bytes 1572872 | tf_op jit(solution)/shard_map/ppermute | solution.py:484
  50.5 14.2 %collective-permute-start.9 = (bf16[1024,256]{1,0:T(8,128)(2,1)}, bf16[1024,256]{1,0:T(8,128)(2,1)}, u32[]{:S(2)}, u32[]{:S(2)}) collective-permute-start(bf16[1024,256]{1,0:T(8,128)(2,1)} %get-tuple-element.28.refs_0_), channel_id=1, source_target_pairs={{0,32},{2,10},{4,36},{6,14},{8,40},{10,2},{12,44},{14,6},{16,48},{... | collective-permute-start | bytes 1572872 | tf_op jit(solution)/shard_map/ppermute | solution.py:484
  52.3 9.5 %collective-permute-start.2 = (bf16[128,1024]{1,0:T(8,128)(2,1)}, bf16[128,1024]{1,0:T(8,128)(2,1)}, u32[]{:S(2)}, u32[]{:S(2)}) collective-permute-start(bf16[128,1024]{1,0:T(8,128)(2,1)} %get-tuple-element.24), channel_id=1, source_target_pairs={{0,2},{2,0},{1,3},{3,1},{4,6},{6,4},{5,7},{7,5},{8,10},{10,8},{9,1... | collective-permute-start | bytes 786440 | tf_op jit(solution)/shard_map/ppermute | solution.py:548
  53.7 1.4 %copy-start.2 = (bf16[32,24,1536]{2,1,0:T(8,128)(2,1)}, bf16[32,24,1536]{2,1,0:T(8,128)(2,1)S(1)}, u32[]{:S(2)}) copy-start(bf16[32,24,1536]{2,1,0:T(8,128)(2,1)S(1)} %get-tuple-element.37) | copy-start | bytes 7077892
  55.1 9.6 %copy-start.6 = (bf16[128,1024]{1,0:T(8,128)(2,1)S(1)}, bf16[128,1024]{1,0:T(8,128)(2,1)}, u32[]{:S(2)}) copy-start(bf16[128,1024]{1,0:T(8,128)(2,1)} %get-tuple-element.23.query_own_ref) | copy-start | bytes 786436
  55.1 41.0 %all-to-all-start.1 = ((bf16[32,24,1536]{2,1,0:T(8,128)(2,1)}), bf16[32,24,1536]{2,1,0:T(8,128)(2,1)S(1)}, u32[]{:S(2)}, u32[]{:S(2)}) async-start(bf16[32,24,1536]{2,1,0:T(8,128)(2,1)} %copy-done.2), calls=%async_computation.1 | async-start | bytes 4718592 | tf_op jit(solution)/shard_map/all_to_all | solution.py:557
  77.2 5.3 %collective-permute-start.12 = (bf16[128,1024]{1,0:T(8,128)(2,1)S(1)}, bf16[128,1024]{1,0:T(8,128)(2,1)S(1)}, u32[]{:S(2)}, u32[]{:S(2)}) collective-permute-start(bf16[128,1024]{1,0:T(8,128)(2,1)S(1)} %get-tuple-element.35), channel_id=1, source_target_pairs={{0,2},{2,0},{1,3},{3,1},{4,6},{6,4},{5,7},{7,5},{8,10},{10,8},{9,1... | collective-permute-start | bytes 786440 | tf_op jit(solution)/shard_map/ppermute | solution.py:565
  77.3 2.3 %copy-start = (bf16[2,1536,768]{2,1,0:T(8,128)(2,1)S(1)}, bf16[2,1536,768]{2,1,0:T(8,128)(2,1)}, u32[]{:S(2)}) copy-start(bf16[2,1536,768]{2,1,0:T(8,128)(2,1)} %head_ref.1) | copy-start | bytes 14155780
  79.6 2.9 %copy-start.1 = (bf16[1024,1536]{1,0:T(8,128)(2,1)S(1)}, bf16[1024,1536]{1,0:T(8,128)(2,1)}, u32[]{:S(2)}) copy-start(bf16[1024,1536]{1,0:T(8,128)(2,1)} %exit_ref.1) | copy-start | bytes 9437188
  79.6 2.9 %copy-start.3 = (bf16[256,1536]{1,0:T(8,128)(2,1)S(1)}, bf16[256,1536]{1,0:T(8,128)(2,1)}, u32[]{:S(2)}) copy-start(bf16[256,1536]{1,0:T(8,128)(2,1)} %get-tuple-element.22.rows_ref) | copy-start | bytes 2359300
  (2 other events, 1.2 us)

commit v5 on v4

--- a/solution.py
+++ b/solution.py
@@ -189,48 +189,84 @@
     )(ends, head, token)
 
 
-def turn_kernel(core_ref, lines_ref, mine_ref, other_ref):
+def turn_kernel(place_ref, lines_ref, mine_ref, other_ref, turned):
+    core, spot_y, spot_x = place_ref[0], place_ref[1], place_ref[2]
     blocks, part, n = mine_ref.shape
-    first = core_ref[0] == 0
-    turned = lines_ref[...].T.reshape(blocks, 2, part, n)
-    low, high = turned[:, 0], turned[:, 1]
-    mine_ref[...] = jnp.where(first, low, high)
-    other_ref[...] = jnp.where(first, high, low)
-
-
-def turn(core, lines, blocks):
+    side = math.isqrt(blocks)
+    turned[...] = lines_ref[...].T.reshape(turned.shape)
+
+    def block(core, k, i):
+        on_x = i * side + lax.rem(spot_x + k, side)
+        on_y = lax.rem(spot_y + k, side) * side + i
+        return 2 * jnp.where(core == 0, on_x, on_y) + core
+
+    for k in range(side):
+        for i in range(side):
+            mine_ref[k * side + i] = turned[block(core, k, i)]
+            other_ref[k * side + i] = turned[block(1 - core, k, i)]
+
+
+def turn(place, lines, blocks):
     n, width = lines.shape
-    half = jax.ShapeDtypeStruct((blocks, width // (2 * blocks), n), BF16)
+    part = width // (2 * blocks)
+    half = jax.ShapeDtypeStruct((blocks, part, n), BF16)
     return pl.pallas_call(
         turn_kernel,
         out_shape=(half, half),
         in_specs=[SMEM, VMEM],
         out_specs=(VMEM, VMEM),
-        compiler_params=params(32),
+        scratch_shapes=[pltpu.VMEM((2 * blocks, part, n), BF16)],
+        compiler_params=params(24),
         cost_estimate=cost(10**6, 2 * 10**6),
         name="turn",
-    )(core.reshape(1), lines)
-
-
-def partial_kernel(mine_ref, other_ref, ends_ref, ends_other_ref, out_ref, token_ref):
+    )(place, lines)
+
+
+def partial_kernel(mine_ref, other_ref, ends_ref, ends_other_ref, *out_refs):
+    token_ref = out_refs[-1]
     token_ref[...] = jnp.zeros_like(token_ref)
-    rows, n = mine_ref.shape[0] * mine_ref.shape[1], mine_ref.shape[2]
-    total = dot(mine_ref[...].reshape(rows, n), ends_ref[...])
-    total = total + dot(other_ref[...].reshape(rows, n), ends_other_ref[...])
-    out_ref[...] = total.astype(BF16).reshape(out_ref.shape)
-
-
-def partial_grad(mine, other, ends, ends_other, pieces):
+    n = mine_ref.shape[2]
+    count = len(out_refs) - 1
+    step = mine_ref.shape[0] // count
+    for i, out_ref in enumerate(out_refs[:-1]):
+        rows = out_ref.shape[0]
+        span = slice(i * step, (i + 1) * step)
+        total = dot(mine_ref[span].reshape(rows, n), ends_ref[...])
+        total = total + dot(other_ref[span].reshape(rows, n), ends_other_ref[...])
+        out_ref[...] = total.astype(BF16)
+
+
+def partial_grad(mine, other, ends, ends_other, side):
     rows, width = mine.shape[0] * mine.shape[1], ends.shape[1]
+    piece = jax.ShapeDtypeStruct((rows // side, width), BF16)
     return pl.pallas_call(
         partial_kernel,
-        out_shape=(jax.ShapeDtypeStruct((pieces, rows // pieces, width), BF16), TOKEN),
+        out_shape=(piece,) * side + (TOKEN,),
         in_specs=[VMEM] * 4,
-        out_specs=(VMEM, VMEM),
-        compiler_params=params(40),
+        out_specs=(VMEM,) * (side + 1),
+        compiler_params=params(24),
         cost_estimate=cost(1.2 * 10**9, 5 * 10**6),
         name="partial_grad",
     )(mine, other, ends, ends_other)
+
+
+def line_sum_kernel(*refs):
+    pieces, out_ref = refs[:-2], refs[-1]
+    total = functools.reduce(jnp.add, [piece[...].astype(F32) for piece in pieces])
+    out_ref[...] = total.astype(BF16).reshape(out_ref.shape)
+
+
+def line_sum(pieces, count, after):
+    rows, width = pieces[0].shape
+    return pl.pallas_call(
+        line_sum_kernel,
+        out_shape=jax.ShapeDtypeStruct((count, rows // count, width), BF16),
+        in_specs=[VMEM] * len(pieces) + [ANY],
+        out_specs=VMEM,
+        compiler_params=params(24),
+        cost_estimate=cost(10**6, 3 * 10**6),
+        name="line_sum",
+    )(*pieces, after)
 
 
 def encoder_kernel(
@@ -345,55 +381,100 @@
     )(core.reshape(1), low, high, gain.reshape(1, width), x, taps, merge, look, ask, after)
 
 
-def attend_kernel(phase_ref, logit_ref, query_own_ref, query_in_ref, *refs):
-    keys, (_, own_ref, out_ref, key_t, value) = refs[:-5], refs[-5:]
+def attend_part(logit_ref, query_own_ref, query_in_ref, keys, key_t, value, put):
     rows, width = query_own_ref.shape
     n, both = keys[0].shape
     lane = both // 2
     count = n * len(keys)
     chunk = 512
+    for i, block in enumerate(keys):
+        span = slice(i * n, (i + 1) * n)
+        turned = block[:, :lane].T
+        key_t[:lane, span] = turned
+        key_t[lane:, span] = turned
+        value[span, :lane] = block[:, lane:]
+        value[span, lane:] = jnp.ones((n, lane), BF16)
+    for head in range(width // lane):
+        span = slice(head * lane, (head + 1) * lane)
+        query = jnp.concatenate([query_own_ref[:, span], query_in_ref[:, span]], axis=0)
+        query = query.astype(F32) * logit_ref[head]
+        coarse = query.astype(BF16)
+        fine = (query - coarse.astype(F32)).astype(BF16)
+        query = jnp.concatenate([coarse, fine], axis=1)
+        scores = [dot(query, key_t[:, j : j + chunk]) for j in range(0, count, chunk)]
+        top = jnp.max(functools.reduce(jnp.maximum, scores), axis=-1, keepdims=True)
+        mixed = 0.0
+        for j, score in enumerate(scores):
+            weight = jnp.exp2(score - top).astype(BF16)
+            mixed = mixed + dot(weight, value[j * chunk : (j + 1) * chunk, :])
+        put(span, mixed[:, :lane], mixed[:, lane:], jnp.broadcast_to(top, (2 * rows, lane)))
+
+
+def attend_first_kernel(phase_ref, logit_ref, query_own_ref, query_in_ref, *refs):
+    keys, (_, mixed_ref, total_ref, top_ref, key_t, value) = refs[:-6], refs[-6:]
 
     @pl.when(phase_ref[0] == 1)
     def _():
-        for i, block in enumerate(keys):
-            span = slice(i * n, (i + 1) * n)
-            turned = block[:, :lane].T
-            key_t[:lane, span] = turned
-            key_t[lane:, span] = turned
-            value[span, :lane] = block[:, lane:]
-            value[span, lane:] = jnp.ones((n, lane), BF16)
-        for head in range(width // lane):
-            span = slice(head * lane, (head + 1) * lane)
-            query = jnp.concatenate([query_own_ref[:, span], query_in_ref[:, span]], axis=0)
-            query = query.astype(F32) * logit_ref[head]
-            coarse = query.astype(BF16)
-            fine = (query - coarse.astype(F32)).astype(BF16)
-            query = jnp.concatenate([coarse, fine], axis=1)
-            scores = [dot(query, key_t[:, j : j + chunk]) for j in range(0, count, chunk)]
-            top = jnp.max(functools.reduce(jnp.maximum, scores), axis=-1, keepdims=True)
-            mixed = 0.0
-            for j, score in enumerate(scores):
-                weight = jnp.exp2(score - top).astype(BF16)
-                mixed = mixed + dot(weight, value[j * chunk : (j + 1) * chunk, :])
-            mixed = (mixed[:, :lane] / mixed[:, lane:]).astype(BF16)
+        def put(span, mixed, total, top):
+            mixed_ref[:, span] = mixed
+            total_ref[:, span] = total
+            top_ref[:, span] = top
+
+        attend_part(logit_ref, query_own_ref, query_in_ref, keys, key_t, value, put)
+
+
+def attend_first(phase, logit, query_own, query_in, keys, after):
+    n, both = keys[0].shape
+    count = n * len(keys)
+    rows, width = query_own.shape
+    part = jax.ShapeDtypeStruct((2 * rows, width), F32)
+    return pl.pallas_call(
+        attend_first_kernel,
+        out_shape=(part, part, part),
+        in_specs=[SMEM, SMEM] + [VMEM] * (2 + len(keys)) + [ANY],
+        out_specs=(VMEM,) * 3,
+        scratch_shapes=[pltpu.VMEM((both, count), BF16), pltpu.VMEM((count, both), BF16)],
+        compiler_params=params(28),
+        cost_estimate=cost(10**9, 4 * 10**6),
+        name="attend_first",
+    )(phase.reshape(1), logit, query_own, query_in, *keys, after)
+
+
+def attend_rest_kernel(
+    phase_ref, logit_ref, query_own_ref, query_in_ref, mixed_ref, total_ref, top_ref, *refs
+):
+    keys, (own_ref, out_ref, token_ref, key_t, value) = refs[:-5], refs[-5:]
+    token_ref[...] = jnp.zeros_like(token_ref)
+    rows = query_own_ref.shape[0]
+
+    @pl.when(phase_ref[0] == 1)
+    def _():
+        def put(span, mixed, total, top):
+            highest = jnp.maximum(top, top_ref[:, span])
+            here, there = jnp.exp2(top - highest), jnp.exp2(top_ref[:, span] - highest)
+            mixed = mixed * here + mixed_ref[:, span] * there
+            total = total * here + total_ref[:, span] * there
+            mixed = (mixed / total).astype(BF16)
             own_ref[:, span] = mixed[:rows]
             out_ref[:, span] = mixed[rows:]
 
-
-def attend(phase, logit, query_own, query_in, keys, after):
+        attend_part(logit_ref, query_own_ref, query_in_ref, keys, key_t, value, put)
+
+
+def attend_rest(phase, logit, query_own, query_in, parts, keys):
     shape = jax.ShapeDtypeStruct(query_own.shape, BF16)
     n, both = keys[0].shape
     count = n * len(keys)
     return pl.pallas_call(
-        attend_kernel,
-        out_shape=(shape, shape),
-        in_specs=[SMEM, SMEM] + [VMEM] * (2 + len(keys)) + [ANY],
-        out_specs=(VMEM, VMEM),
+        attend_rest_kernel,
+        out_shape=(shape, shape, TOKEN),
+        in_specs=[SMEM, SMEM] + [VMEM] * (5 + len(keys)),
+        out_specs=(VMEM, VMEM, VMEM),
         scratch_shapes=[pltpu.VMEM((both, count), BF16), pltpu.VMEM((count, both), BF16)],
-        compiler_params=params(32),
+        compiler_params=params(28),
         cost_estimate=cost(6 * 10**10, 4 * 10**6),
-        name="attend",
-    )(phase.reshape(1), logit, query_own, query_in, *keys, after)
+        name="attend_rest",
+    )(phase.reshape(1), logit, query_own, query_in, *parts, *keys)
 
 
 def exit_kernel(phase_ref, core_ref, rows_ref, own_ref, in_ref, exit_ref, out_ref, token_ref):
@@ -470,19 +551,33 @@
     )(*blocks)
 
 
+def line_pairs(side, first, distance):
+    pairs = []
+    for y in range(side):
+        for x in range(side):
+            for core in range(2):
+                along_x = (core == 0) == first
+                to_x = (x + distance) % side if along_x else x
+                to_y = y if along_x else (y + distance) % side
+                pairs.append(((y * side + x) * 2 + core, (to_y * side + to_x) * 2 + core))
+    return pairs
+
+
+def lines_of(side, first, depth):
+    groups = []
+    for i in range(side):
+        for core in range(2):
+            along_x = (core == 0) == first
+            chips = [i * side + k if along_x else k * side + i for k in range(side)]
+            groups.append([(chip * 2 + core) * depth + d for chip in chips for d in range(depth)])
+    return groups
+
+
 def spread(block, side, first):
-    received = []
-    for distance in (1, side - 1, 2):
-        pairs = []
-        for y in range(side):
-            for x in range(side):
-                for core in range(2):
-                    along_x = (core == 0) == first
-                    to_x = (x + distance) % side if along_x else x
-                    to_y = y if along_x else (y + distance) % side
-                    pairs.append(((y * side + x) * 2 + core, (to_y * side + to_x) * 2 + core))
-        received.append(lax.ppermute(block, SEQ, pairs))
-    return received
+    return [
+        lax.ppermute(block, SEQ, line_pairs(side, first, distance))
+        for distance in (1, side - 1, 2)
+    ]
 
 
 def halo(first, last):
@@ -548,24 +643,38 @@
     query_in = lax.ppermute(query_out, "core", swap)
 
     portion = splice_readout_lines[0].reshape(batch * rows, width)
-    mine, other = turn(core, portion, shards // 2)
+    place = jnp.stack([core, lax.axis_index("y"), lax.axis_index("x")]).astype(I32)
+    mine, other = turn(place, portion, shards // 2)
     other = lax.ppermute(other, "core", swap)
 
     ends = make_ends(arrived, batch, rows, line_done, other)
     ends_other = lax.ppermute(ends, "core", swap)
-    partial, terms_done = partial_grad(mine, other, ends, ends_other, shards)
-    pieces = lax.all_to_all(partial, ("y", "x", "dp"), 0, 0, tiled=True)
+    *partial, terms_done = partial_grad(mine, other, ends, ends_other, side)
+    terms = [partial[0]] + [
+        lax.ppermute(partial[k], SEQ, line_pairs(side, True, k)) for k in (1, side - 1, 2)
+    ]
 
     row_grad = make_row_grad(ends, splice_site_projector, terms_done)
     row_grad = row_grad.reshape(batch, rows, width)[None]
 
     logit = lane_logit_factor * (math.log2(math.e) / math.sqrt(lane))
-    own, out = attend(phase, logit, query_own, query_in, keys, terms_done)
+    parts = attend_first(phase, logit, query_own, query_in, keys[:2], terms_done)
+    own, out, attended = attend_rest(phase, logit, query_own, query_in, parts, keys[2:])
     rows_out, left = leave(
         phase, core, encoded, own, lax.ppermute(out, "core", swap), attention_exit_projector
     )
     phase_rows = rows_out.reshape(batch, rows, width)[None]
 
+    depth = lax.axis_size("dp")
+    line_terms = line_sum(terms, side * depth, attended)
+    pieces = lax.all_to_all(
+        line_terms,
+        SEQ + ("dp",),
+        0,
+        0,
+        axis_index_groups=lines_of(side, False, depth),
+        tiled=True,
+    )
     weight_grad = sum_terms(pieces, left)[None]
     return (phase_rows, row_grad, weight_grad)
 

time: 98.2 us -> 94.3 us (0.960)
  waiting for transfers between devices: 24.1 us -> 8.17 us
  starting transfers between devices: 31.5 us -> 39.2 us
  Pallas kernels: 34.2 us -> 36.3 us
  local copies, waits for them, and re-layouts: 6.56 us -> 7.82 us
    all_to_all x1, waiting for transfers between devices: 11.8 us -> 0.1 us  [body(): lax.all_to_all(line_terms, SEQ + ('dp',), 0, 0, axis_index_groups=lines_o...]
    ppermute x6 -> x9, starting transfers between devices: 10.3 us -> 18.8 us  [the longest x6 10.4 us: spread(): lax.ppermute(block, SEQ, line_pairs(side, first, distance))]
    ppermute x6 -> x9, waiting for transfers between devices: 11 us -> 6.82 us  [the longest x6 6.81 us: spread(): lax.ppermute(block, SEQ, line_pairs(side, first, distance))]
    all_to_all x1, starting transfers between devices: 6.61 us -> 3.54 us  [body(): lax.all_to_all(line_terms, SEQ + ('dp',), 0, 0, axis_index_groups=lines_o...]
    pallas_call x2 -> x4, Pallas kernels: 13.8 us -> 16.4 us  [the longest x1 7.07 us: attend_first(): pl.pallas_call(attend_first_kernel, out_shape=(part, part, part), in_spec...]
    ppermute x1, starting transfers between devices: 0.09 us -> 2.49 us  [body(): lax.ppermute(out, 'core', swap)]
    unnamed x22 -> x24, local copies, waits for them, and re-layouts: 5.19 us -> 6.46 us
  transfers between devices with their start and end apart: 15 -> 18, of which waited for: 5 -> 4; matrix products, arithmetic and copies ran while one was open for 1% -> 1% of each run, Pallas kernels for 33% -> 36%
where the time goes in v5:
time: 94.3 us; the launch traced here: 92.5 us
  starting transfers between devices  39.2 us (42%)
  Pallas kernels  36.3 us (38%)
  waiting for transfers between devices  8.17 us (9%)
  local copies, waits for them, and re-layouts  7.82 us (8%)
    all_to_all x1, starting transfers between devices, body(): arrived = lax.all_to_all(payload, SEQ, 0, 0, tiled=True)  10.7 us
    ppermute x6, starting transfers between devices, spread(): lax.ppermute(block, SEQ, line_pairs(side, first, distance))  10.4 us
    pallas_call x1, Pallas kernels, encode(): pl.pallas_call(encoder_kernel, out_shape=(jax.ShapeDtypeStruct((n, width)...  8.91 us
    ppermute x3, starting transfers between devices, body(): lax.ppermute(partial[k], SEQ, line_pairs(side, True, k))  8.4 us
    pallas_call x1, Pallas kernels, attend_first(): pl.pallas_call(attend_first_kernel, out_shape=(part, part, part), in_spec...  7.07 us
    pallas_call x1, Pallas kernels, attend_rest(): pl.pallas_call(attend_rest_kernel, out_shape=(shape, shape, TOKEN), in_sp...  6.85 us
    ppermute x6, waiting for transfers between devices, spread(): lax.ppermute(block, SEQ, line_pairs(side, first, distance))  6.81 us
    unnamed x24, local copies, waits for them, and re-layouts  6.46 us
  transfers between devices with their start and end apart: 18, of which 4 were waited for; matrix products, arithmetic and copies ran while one was open for 1% of the time, Pallas kernels for 36%

profile of v5, /device:TPU:64, one launch (start us, length us, event | category | flops | bytes accessed | tf_op | source)
XLA Modules:
  0.0 92.5 jit_solution(11123333846331025393)
XLA Ops:
  1.4 1.7 %collective-permute-start = (bf16[2,2,768]{2,1,0:T(2,128)(2,1)S(1)}, bf16[2,2,768]{2,1,0:T(2,128)(2,1)S(1)}, u32[]{:S(2)}, u32[]{:S(2)}) collective-permute-start(bf16[2,2,768]{2,1,0:T(2,128)(2,1)S(1)} %get-tuple-element.54), channel_id=1, source_target_pairs={{0,2},{2,4},{4,6},{6,8},{8,10},{10,12},{12,14},{14,16},{16,18},{18... | collective-permute-start | bytes 18440 | tf_op jit(solution)/shard_map/ppermute | solution.py:587
  3.1 1.3 %collective-permute-start.1 = (bf16[2,2,768]{2,1,0:T(2,128)(2,1)S(1)}, bf16[2,2,768]{2,1,0:T(2,128)(2,1)S(1)}, u32[]{:S(2)}, u32[]{:S(2)}) collective-permute-start(bf16[2,2,768]{2,1,0:T(2,128)(2,1)S(1)} %get-tuple-element.53), channel_id=1, source_target_pairs={{2,0},{4,2},{6,4},{8,6},{10,8},{12,10},{14,12},{16,14},{18,16},{20... | collective-permute-start | bytes 18440 | tf_op jit(solution)/shard_map/ppermute | solution.py:587
  4.5 3.3 %pick.1 = (bf16[32,16,1664]{2,1,0:T(8,128)(2,1)}, f32[8,128]{1,0:T(8,128)}) custom-call(s32[2,16,32]{2,1,0:T(8,128)} %bitcast.21, s32[2,16,32]{2,1,0:T(8,128)} %bitcast.22, s32[2,32]{1,0:T(2,128)} %bitcast.23, bf16[2,128,768]{2,1,0:T(8,128)(2,1)} %bitcast.20), custom_call_target="tpu_custom_call" | custom-call | flops 200000000 | bytes 3000000 | tf_op jit(solution)/shard_map/pick/pallas_call | solution.py:101
  8.4 10.7 %all-to-all-start = ((bf16[32,16,1664]{2,1,0:T(8,128)(2,1)}), bf16[32,16,1664]{2,1,0:T(8,128)(2,1)S(1)}, u32[]{:S(2)}, u32[]{:S(2)}) async-start(bf16[32,16,1664]{2,1,0:T(8,128)(2,1)} %follow.1), calls=%async_computation | async-start | bytes 3407872 | tf_op jit(solution)/shard_map/all_to_all | solution.py:626
  21.6 8.9 %encode.1 = (bf16[256,1536]{1,0:T(8,128)(2,1)}, bf16[128,256]{1,0:T(8,128)(2,1)}, bf16[128,256]{1,0:T(8,128)(2,1)}, bf16[128,1024]{1,0:T(8,128)(2,1)}, bf16[128,1024]{1,0:T(8,128)(2,1)}, /*index=5*/f32[8,128]{1,0:T(8,128)}) custom-call(s32[1]{0:T(128)} %bitcast.1.core_ref, bf16[2,2,768]{2,1,0:T(2,128)(2,1)} %copy-done.9, bf16[2,2,768]{2,1,0:T(2,128)(2,1)} %copy-done.10, ...), custom_call_target="tpu_custom_call" | custom-call | flops 3400000000 | bytes 12000000 | tf_op jit(solution)/shard_map/encode/pallas_call | solution.py:362
  30.9 1.2 %collective-permute-done.3.refs_1_ = bf16[128,256]{1,0:T(8,128)(2,1)S(1)} collective-permute-done((bf16[128,256]{1,0:T(8,128)(2,1)}, bf16[128,256]{1,0:T(8,128)(2,1)S(1)}, u32[]{:S(2)}, u32[]{:S(2)}) %collective-permute-start.3) | collective-permute-done | bytes 65568 | tf_op jit(solution)/shard_map/ppermute | solution.py:640
  33.6 1.7 %collective-permute-start.4 = (bf16[256,256]{1,0:T(8,128)(2,1)S(1)}, bf16[256,256]{1,0:T(8,128)(2,1)S(1)}, u32[]{:S(2)}, u32[]{:S(2)}) collective-permute-start(bf16[256,256]{1,0:T(8,128)(2,1)S(1)} %get-tuple-element.34.refs_0_), channel_id=1, source_target_pairs={{0,4},{2,18},{4,8},{6,22},{8,12},{10,26},{12,0},{14,30},{16,20},{1... | collective-permute-start | bytes 393224 | tf_op jit(solution)/shard_map/ppermute | solution.py:578
  35.2 1.6 %collective-permute-start.5 = (bf16[256,256]{1,0:T(8,128)(2,1)S(1)}, bf16[256,256]{1,0:T(8,128)(2,1)S(1)}, u32[]{:S(2)}, u32[]{:S(2)}) collective-permute-start(bf16[256,256]{1,0:T(8,128)(2,1)S(1)} %get-tuple-element.34.refs_0_), channel_id=1, source_target_pairs={{0,12},{2,50},{4,0},{6,54},{8,4},{10,58},{12,8},{14,62},{16,28},{1... | collective-permute-start | bytes 393224 | tf_op jit(solution)/shard_map/ppermute | solution.py:578
  36.8 2.0 %collective-permute-start.6 = (bf16[256,256]{1,0:T(8,128)(2,1)S(1)}, bf16[256,256]{1,0:T(8,128)(2,1)S(1)}, u32[]{:S(2)}, u32[]{:S(2)}) collective-permute-start(bf16[256,256]{1,0:T(8,128)(2,1)S(1)} %get-tuple-element.34.refs_0_), channel_id=1, source_target_pairs={{0,8},{2,34},{4,12},{6,38},{8,0},{10,42},{12,4},{14,46},{16,24},{1... | collective-permute-start | bytes 393224 | tf_op jit(solution)/shard_map/ppermute | solution.py:578
  38.8 4.1 %collective-permute-done.4.refs_1_ = bf16[256,256]{1,0:T(8,128)(2,1)S(1)} collective-permute-done((bf16[256,256]{1,0:T(8,128)(2,1)S(1)}, bf16[256,256]{1,0:T(8,128)(2,1)S(1)}, u32[]{:S(2)}, u32[]{:S(2)}) %collective-permute-start.4) | collective-permute-done | bytes 131104 | tf_op jit(solution)/shard_map/ppermute | solution.py:578
  42.8 2.7 %collective-permute-done.6.refs_3_ = bf16[256,256]{1,0:T(8,128)(2,1)S(1)} collective-permute-done((bf16[256,256]{1,0:T(8,128)(2,1)S(1)}, bf16[256,256]{1,0:T(8,128)(2,1)S(1)}, u32[]{:S(2)}, u32[]{:S(2)}) %collective-permute-start.6) | collective-permute-done | bytes 131104 | tf_op jit(solution)/shard_map/ppermute | solution.py:578
  46.4 1.7 %collective-permute-start.7 = (bf16[1024,256]{1,0:T(8,128)(2,1)S(1)}, bf16[1024,256]{1,0:T(8,128)(2,1)}, u32[]{:S(2)}, u32[]{:S(2)}) collective-permute-start(bf16[1024,256]{1,0:T(8,128)(2,1)S(1)} %get-tuple-element.35.refs_0_), channel_id=1, source_target_pairs={{0,16},{2,6},{4,20},{6,10},{8,24},{10,14},{12,28},{14,2},{16,32},{... | collective-permute-start | bytes 1572872 | tf_op jit(solution)/shard_map/ppermute | solution.py:578
  48.1 1.6 %collective-permute-start.10 = (bf16[1024,256]{1,0:T(8,128)(2,1)S(1)}, bf16[1024,256]{1,0:T(8,128)(2,1)S(1)}, u32[]{:S(2)}, u32[]{:S(2)}) collective-permute-start(bf16[1024,256]{1,0:T(8,128)(2,1)S(1)} %get-tuple-element.35.refs_0_), channel_id=1, source_target_pairs={{0,48},{2,14},{4,52},{6,2},{8,56},{10,6},{12,60},{14,10},{16,0},{1... | collective-permute-start | bytes 1572872 | tf_op jit(solution)/shard_map/ppermute | solution.py:578
  49.7 1.9 %collective-permute-start.11 = (bf16[1024,256]{1,0:T(8,128)(2,1)S(1)}, bf16[1024,256]{1,0:T(8,128)(2,1)}, u32[]{:S(2)}, u32[]{:S(2)}) collective-permute-start(bf16[1024,256]{1,0:T(8,128)(2,1)S(1)} %get-tuple-element.35.refs_0_), channel_id=1, source_target_pairs={{0,32},{2,10},{4,36},{6,14},{8,40},{10,2},{12,44},{14,6},{16,48},{... | collective-permute-start | bytes 1572872 | tf_op jit(solution)/shard_map/ppermute | solution.py:578
  52.6 1.4 %partial_grad.1 = (bf16[192,1536]{1,0:T(8,128)(2,1)S(1)}, bf16[192,1536]{1,0:T(8,128)(2,1)S(1)}, bf16[192,1536]{1,0:T(8,128)(2,1)S(1)}, bf16[192,1536]{1,0:T(8,128)(2,1)S(1)}, f32[8,128]{1,0:T(8,128)S(1)}) custom-call(bf16[16,48,256]{2,1,0:T(8,128)(2,1)S(1)} %copy-done.6, bf16[16,48,256]{2,1,0:T(8,128)(2,1)S(1)} %collective-permute-done.8._other.other_ref, ...), custom_call_target="tpu_custom_call" | custom-call | flops 1200000000 | bytes 5000000 | tf_op jit(solution)/shard_map/partial_grad/pallas_call | solution.py:242
  54.1 3.2 %collective-permute-start.14 = (bf16[192,1536]{1,0:T(8,128)(2,1)S(1)}, bf16[192,1536]{1,0:T(8,128)(2,1)S(1)}, u32[]{:S(2)}, u32[]{:S(2)}) collective-permute-start(bf16[192,1536]{1,0:T(8,128)(2,1)S(1)} %get-tuple-element.49), channel_id=1, source_target_pairs={{0,12},{2,50},{4,0},{6,54},{8,4},{10,58},{12,8},{14,62},{16,28},{1... | collective-permute-start | bytes 1769480 | tf_op jit(solution)/shard_map/ppermute | solution.py:654
  57.3 5.1 %collective-permute-start.15 = (bf16[192,1536]{1,0:T(8,128)(2,1)S(1)}, bf16[192,1536]{1,0:T(8,128)(2,1)S(1)}, u32[]{:S(2)}, u32[]{:S(2)}) collective-permute-start(bf16[192,1536]{1,0:T(8,128)(2,1)S(1)} %get-tuple-element.50), channel_id=1, source_target_pairs={{0,8},{2,34},{4,12},{6,38},{8,0},{10,42},{12,4},{14,46},{16,24},{1... | collective-permute-start | bytes 1769480 | tf_op jit(solution)/shard_map/ppermute | solution.py:654
  63.4 7.1 %attend_first.1 = (f32[256,1024]{1,0:T(8,128)S(1)}, f32[256,1024]{1,0:T(8,128)S(1)}, f32[256,1024]{1,0:T(8,128)S(1)}) custom-call(s32[1]{0:T(128)} %bitcast.phase_ref, f32[8]{0:T(128)S(1)} %broadcast_multiply_fusion.logit_ref, bf16[128,1024]{1,0:T(8,128)(2,1)S(1)} %copy-done.7, bf16[128,1024]{1,0:T(8,128)(2,1)S(1)} %collective-permute-done.2.query_in_ref, ...), custom_call_target="tpu_custom_call" | custom-call | flops 1000000000 | bytes 4000000 | tf_op jit(solution)/shard_map/attend_first/pallas_call | solution.py:431
  70.5 6.8 %attend_rest.1 = (bf16[128,1024]{1,0:T(8,128)(2,1)S(1)}, bf16[128,1024]{1,0:T(8,128)(2,1)S(1)}, f32[8,128]{1,0:T(8,128)S(1)}) custom-call(s32[1]{0:T(128)} %bitcast.phase_ref, f32[8]{0:T(128)S(1)} %broadcast_multiply_fusion.logit_ref, bf16[128,1024]{1,0:T(8,128)(2,1)S(1)} %copy-done.7, bf16[128,1024]{1,0:T(8,128)(2,1)S(1)} %collective-permute-done.2.query_in_ref, ...), custom_call_target="tpu_custom_call" | custom-call | flops 60000002048 | bytes 4000000 | tf_op jit(solution)/shard_map/attend_rest/pallas_call | solution.py:468
  78.5 3.5 %all-to-all-start.1 = ((bf16[8,24,1536]{2,1,0:T(8,128)(2,1)}), bf16[8,24,1536]{2,1,0:T(8,128)(2,1)S(1)}, u32[]{:S(2)}, u32[]{:S(2)}) async-start(bf16[8,24,1536]{2,1,0:T(8,128)(2,1)} %line_sum.1), calls=%async_computation.1 | async-start | bytes 1179648 | tf_op jit(solution)/shard_map/all_to_all | solution.py:670
  82.0 2.5 %collective-permute-start.12 = (bf16[128,1024]{1,0:T(8,128)(2,1)S(1)}, bf16[128,1024]{1,0:T(8,128)(2,1)S(1)}, u32[]{:S(2)}, u32[]{:S(2)}) collective-permute-start(bf16[128,1024]{1,0:T(8,128)(2,1)S(1)} %get-tuple-element.45), channel_id=1, source_target_pairs={{0,2},{2,0},{1,3},{3,1},{4,6},{6,4},{5,7},{7,5},{8,10},{10,8},{9,1... | collective-permute-start | bytes 786440 | tf_op jit(solution)/shard_map/ppermute | solution.py:664
  84.5 2.3 %copy-done = bf16[2,1536,768]{2,1,0:T(8,128)(2,1)S(1)} copy-done((bf16[2,1536,768]{2,1,0:T(8,128)(2,1)S(1)}, bf16[2,1536,768]{2,1,0:T(8,128)(2,1)}, u32[]{:S(2)}) %copy-start) | copy-done | bytes 4718616
  86.9 2.9 %row_grad.1 = bf16[256,1536]{1,0:T(8,128)(2,1)} custom-call(bf16[256,1536]{1,0:T(8,128)(2,1)S(1)} %ends.1.ends_ref, bf16[2,1536,768]{2,1,0:T(8,128)(2,1)S(1)} %copy-done, f32[8,128]{1,0:T(8,128)S(1)} %get-tuple-element.40.refs_2_._token), custom_call_target="tpu_custom_call" | custom-call | flops 1200000000 | bytes 6000000 | tf_op jit(solution)/shard_map/row_grad/pallas_call | solution.py:176
  89.8 1.9 %leave.1 = (bf16[256,1536]{1,0:T(8,128)(2,1)}, f32[8,128]{1,0:T(8,128)S(1)}) custom-call(s32[1]{0:T(128)} %bitcast.phase_ref, s32[1]{0:T(128)} %bitcast.1.core_ref, bf16[256,1536]{1,0:T(8,128)(2,1)S(1)} %copy-done.2, bf16[128,1024]{1,0:T(8,128)(2,1)S(1)} %get-tuple-element.44.own_ref, bf16[128,1024]{1,0:T(8,128)(2,1)S(1)} %collective-permute-done.12.in_ref, ...), custom_call_target="tpu_custom_call" | custom-call | flops 800000000 | bytes 5000000 | tf_op jit(solution)/shard_map/leave/pallas_call | solution.py:502
  (54 shorter events, 10.5 us)
Async XLA Ops:
  1.4 6.4 %collective-permute-start = (bf16[2,2,768]{2,1,0:T(2,128)(2,1)S(1)}, bf16[2,2,768]{2,1,0:T(2,128)(2,1)S(1)}, u32[]{:S(2)}, u32[]{:S(2)}) collective-permute-start(bf16[2,2,768]{2,1,0:T(2,128)(2,1)S(1)} %get-tuple-element.54), channel_id=1, source_target_pairs={{0,2},{2,4},{4,6},{6,8},{8,10},{10,12},{12,14},{14,16},{16,18},{18... | collective-permute-start | bytes 18440 | tf_op jit(solution)/shard_map/ppermute | solution.py:587
  3.1 4.6 %collective-permute-start.1 = (bf16[2,2,768]{2,1,0:T(2,128)(2,1)S(1)}, bf16[2,2,768]{2,1,0:T(2,128)(2,1)S(1)}, u32[]{:S(2)}, u32[]{:S(2)}) collective-permute-start(bf16[2,2,768]{2,1,0:T(2,128)(2,1)S(1)} %get-tuple-element.53), channel_id=1, source_target_pairs={{2,0},{4,2},{6,4},{8,6},{10,8},{12,10},{14,12},{16,14},{18,16},{20... | collective-permute-start | bytes 18440 | tf_op jit(solution)/shard_map/ppermute | solution.py:587
  8.4 10.8 %copy-start.3 = (bf16[1,2,128,1536]{3,2,1,0:T(8,128)(2,1)S(1)}, bf16[1,2,128,1536]{3,2,1,0:T(8,128)(2,1)}, u32[]{:S(2)}) copy-start(bf16[1,2,128,1536]{3,2,1,0:T(8,128)(2,1)} %param.22) | copy-start | bytes 2359300
  8.4 12.7 %copy-start.8 = (f32[1536]{0:T(1024)S(1)}, f32[1536]{0:T(1024)}, u32[]{:S(2)}) copy-start(f32[1536]{0:T(1024)} %param.17) | copy-start | bytes 18436
  8.4 37.2 %all-to-all-start = ((bf16[32,16,1664]{2,1,0:T(8,128)(2,1)}), bf16[32,16,1664]{2,1,0:T(8,128)(2,1)S(1)}, u32[]{:S(2)}, u32[]{:S(2)}) async-start(bf16[32,16,1664]{2,1,0:T(8,128)(2,1)} %follow.1), calls=%async_computation | async-start | bytes 3407872 | tf_op jit(solution)/shard_map/all_to_all | solution.py:626
  20.8 24.8 %collective-permute-start.8 = (bf16[16,48,256]{2,1,0:T(8,128)(2,1)S(1)}, bf16[16,48,256]{2,1,0:T(8,128)(2,1)S(1)}, u32[]{:S(2)}, u32[]{:S(2)}) collective-permute-start(bf16[16,48,256]{2,1,0:T(8,128)(2,1)S(1)} %get-tuple-element.37), channel_id=1, source_target_pairs={{0,2},{2,0},{1,3},{3,1},{4,6},{6,4},{5,7},{7,5},{8,10},{10,8},{9,1... | collective-permute-start | bytes 1179656 | tf_op jit(solution)/shard_map/ppermute | solution.py:648
  30.6 21.1 %copy-start.11 = (f32[8]{0:T(128)S(1)}, f32[8]{0:T(128)}, u32[]{:S(2)}) copy-start(f32[8]{0:T(128)} %param.21) | copy-start | bytes 100
  30.6 1.5 %collective-permute-start.3 = (bf16[128,256]{1,0:T(8,128)(2,1)}, bf16[128,256]{1,0:T(8,128)(2,1)S(1)}, u32[]{:S(2)}, u32[]{:S(2)}) collective-permute-start(bf16[128,256]{1,0:T(8,128)(2,1)} %get-tuple-element.33), channel_id=1, source_target_pairs={{0,2},{2,0},{1,3},{3,1},{4,6},{6,4},{5,7},{7,5},{8,10},{10,8},{9,1... | collective-permute-start | bytes 196616 | tf_op jit(solution)/shard_map/ppermute | solution.py:640
  33.6 9.3 %collective-permute-start.4 = (bf16[256,256]{1,0:T(8,128)(2,1)S(1)}, bf16[256,256]{1,0:T(8,128)(2,1)S(1)}, u32[]{:S(2)}, u32[]{:S(2)}) collective-permute-start(bf16[256,256]{1,0:T(8,128)(2,1)S(1)} %get-tuple-element.34.refs_0_), channel_id=1, source_target_pairs={{0,4},{2,18},{4,8},{6,22},{8,12},{10,26},{12,0},{14,30},{16,20},{1... | collective-permute-start | bytes 393224 | tf_op jit(solution)/shard_map/ppermute | solution.py:578
  35.2 7.6 %collective-permute-start.5 = (bf16[256,256]{1,0:T(8,128)(2,1)S(1)}, bf16[256,256]{1,0:T(8,128)(2,1)S(1)}, u32[]{:S(2)}, u32[]{:S(2)}) collective-permute-start(bf16[256,256]{1,0:T(8,128)(2,1)S(1)} %get-tuple-element.34.refs_0_), channel_id=1, source_target_pairs={{0,12},{2,50},{4,0},{6,54},{8,4},{10,58},{12,8},{14,62},{16,28},{1... | collective-permute-start | bytes 393224 | tf_op jit(solution)/shard_map/ppermute | solution.py:578
  36.8 8.8 %collective-permute-start.6 = (bf16[256,256]{1,0:T(8,128)(2,1)S(1)}, bf16[256,256]{1,0:T(8,128)(2,1)S(1)}, u32[]{:S(2)}, u32[]{:S(2)}) collective-permute-start(bf16[256,256]{1,0:T(8,128)(2,1)S(1)} %get-tuple-element.34.refs_0_), channel_id=1, source_target_pairs={{0,8},{2,34},{4,12},{6,38},{8,0},{10,42},{12,4},{14,46},{16,24},{1... | collective-permute-start | bytes 393224 | tf_op jit(solution)/shard_map/ppermute | solution.py:578
  46.3 5.3 %collective-permute-start.9 = (bf16[256,1536]{1,0:T(8,128)(2,1)S(1)}, bf16[256,1536]{1,0:T(8,128)(2,1)S(1)}, u32[]{:S(2)}, u32[]{:S(2)}) collective-permute-start(bf16[256,1536]{1,0:T(8,128)(2,1)S(1)} %ends.1.ends_ref), channel_id=1, source_target_pairs={{0,2},{2,0},{1,3},{3,1},{4,6},{6,4},{5,7},{7,5},{8,10},{10,8},{9,1... | collective-permute-start | bytes 2359304 | tf_op jit(solution)/shard_map/ppermute | solution.py:651
  46.4 10.9 %collective-permute-start.7 = (bf16[1024,256]{1,0:T(8,128)(2,1)S(1)}, bf16[1024,256]{1,0:T(8,128)(2,1)}, u32[]{:S(2)}, u32[]{:S(2)}) collective-permute-start(bf16[1024,256]{1,0:T(8,128)(2,1)S(1)} %get-tuple-element.35.refs_0_), channel_id=1, source_target_pairs={{0,16},{2,6},{4,20},{6,10},{8,24},{10,14},{12,28},{14,2},{16,32},{... | collective-permute-start | bytes 1572872 | tf_op jit(solution)/shard_map/ppermute | solution.py:578
  48.1 22.4 %collective-permute-start.10 = (bf16[1024,256]{1,0:T(8,128)(2,1)S(1)}, bf16[1024,256]{1,0:T(8,128)(2,1)S(1)}, u32[]{:S(2)}, u32[]{:S(2)}) collective-permute-start(bf16[1024,256]{1,0:T(8,128)(2,1)S(1)} %get-tuple-element.35.refs_0_), channel_id=1, source_target_pairs={{0,48},{2,14},{4,52},{6,2},{8,56},{10,6},{12,60},{14,10},{16,0},{1... | collective-permute-start | bytes 1572872 | tf_op jit(solution)/shard_map/ppermute | solution.py:578
  49.7 20.8 %collective-permute-start.11 = (bf16[1024,256]{1,0:T(8,128)(2,1)S(1)}, bf16[1024,256]{1,0:T(8,128)(2,1)}, u32[]{:S(2)}, u32[]{:S(2)}) collective-permute-start(bf16[1024,256]{1,0:T(8,128)(2,1)S(1)} %get-tuple-element.35.refs_0_), channel_id=1, source_target_pairs={{0,32},{2,10},{4,36},{6,14},{8,40},{10,2},{12,44},{14,6},{16,48},{... | collective-permute-start | bytes 1572872 | tf_op jit(solution)/shard_map/ppermute | solution.py:578
  51.6 2.5 %collective-permute-start.2 = (bf16[128,1024]{1,0:T(8,128)(2,1)}, bf16[128,1024]{1,0:T(8,128)(2,1)S(1)}, u32[]{:S(2)}, u32[]{:S(2)}) collective-permute-start(bf16[128,1024]{1,0:T(8,128)(2,1)} %get-tuple-element.31), channel_id=1, source_target_pairs={{0,2},{2,0},{1,3},{3,1},{4,6},{6,4},{5,7},{7,5},{8,10},{10,8},{9,1... | collective-permute-start | bytes 786440 | tf_op jit(solution)/shard_map/ppermute | solution.py:643
  54.0 23.3 %collective-permute-start.13 = (bf16[192,1536]{1,0:T(8,128)(2,1)S(1)}, bf16[192,1536]{1,0:T(8,128)(2,1)S(1)}, u32[]{:S(2)}, u32[]{:S(2)}) collective-permute-start(bf16[192,1536]{1,0:T(8,128)(2,1)S(1)} %get-tuple-element.48), channel_id=1, source_target_pairs={{0,4},{2,18},{4,8},{6,22},{8,12},{10,26},{12,0},{14,30},{16,20},{1... | collective-permute-start | bytes 1769480 | tf_op jit(solution)/shard_map/ppermute | solution.py:654
  54.1 23.2 %collective-permute-start.14 = (bf16[192,1536]{1,0:T(8,128)(2,1)S(1)}, bf16[192,1536]{1,0:T(8,128)(2,1)S(1)}, u32[]{:S(2)}, u32[]{:S(2)}) collective-permute-start(bf16[192,1536]{1,0:T(8,128)(2,1)S(1)} %get-tuple-element.49), channel_id=1, source_target_pairs={{0,12},{2,50},{4,0},{6,54},{8,4},{10,58},{12,8},{14,62},{16,28},{1... | collective-permute-start | bytes 1769480 | tf_op jit(solution)/shard_map/ppermute | solution.py:654
  57.3 20.0 %collective-permute-start.15 = (bf16[192,1536]{1,0:T(8,128)(2,1)S(1)}, bf16[192,1536]{1,0:T(8,128)(2,1)S(1)}, u32[]{:S(2)}, u32[]{:S(2)}) collective-permute-start(bf16[192,1536]{1,0:T(8,128)(2,1)S(1)} %get-tuple-element.50), channel_id=1, source_target_pairs={{0,8},{2,34},{4,12},{6,38},{8,0},{10,42},{12,4},{14,46},{16,24},{1... | collective-permute-start | bytes 1769480 | tf_op jit(solution)/shard_map/ppermute | solution.py:654
  78.5 13.2 %all-to-all-start.1 = ((bf16[8,24,1536]{2,1,0:T(8,128)(2,1)}), bf16[8,24,1536]{2,1,0:T(8,128)(2,1)S(1)}, u32[]{:S(2)}, u32[]{:S(2)}) async-start(bf16[8,24,1536]{2,1,0:T(8,128)(2,1)} %line_sum.1), calls=%async_computation.1 | async-start | bytes 1179648 | tf_op jit(solution)/shard_map/all_to_all | solution.py:670
  82.0 7.7 %collective-permute-start.12 = (bf16[128,1024]{1,0:T(8,128)(2,1)S(1)}, bf16[128,1024]{1,0:T(8,128)(2,1)S(1)}, u32[]{:S(2)}, u32[]{:S(2)}) collective-permute-start(bf16[128,1024]{1,0:T(8,128)(2,1)S(1)} %get-tuple-element.45), channel_id=1, source_target_pairs={{0,2},{2,0},{1,3},{3,1},{4,6},{6,4},{5,7},{7,5},{8,10},{10,8},{9,1... | collective-permute-start | bytes 786440 | tf_op jit(solution)/shard_map/ppermute | solution.py:664
  84.5 2.3 %copy-start = (bf16[2,1536,768]{2,1,0:T(8,128)(2,1)S(1)}, bf16[2,1536,768]{2,1,0:T(8,128)(2,1)}, u32[]{:S(2)}) copy-start(bf16[2,1536,768]{2,1,0:T(8,128)(2,1)} %head_ref.1) | copy-start | bytes 14155780
  86.9 2.9 %copy-start.1 = (bf16[1024,1536]{1,0:T(8,128)(2,1)S(1)}, bf16[1024,1536]{1,0:T(8,128)(2,1)}, u32[]{:S(2)}) copy-start(bf16[1024,1536]{1,0:T(8,128)(2,1)} %exit_ref.1) | copy-start | bytes 9437188
  86.9 2.9 %copy-start.2 = (bf16[256,1536]{1,0:T(8,128)(2,1)S(1)}, bf16[256,1536]{1,0:T(8,128)(2,1)}, u32[]{:S(2)}) copy-start(bf16[256,1536]{1,0:T(8,128)(2,1)} %get-tuple-element.29.rows_ref) | copy-start | bytes 2359300
  (6 other events, 4.7 us)

commit v6 on v5

--- a/solution.py
+++ b/solution.py
@@ -189,7 +189,7 @@
     )(ends, head, token)
 
 
-def turn_kernel(place_ref, lines_ref, mine_ref, other_ref, turned):
+def turn_kernel(place_ref, lines_ref, _token, mine_ref, other_ref, turned):
     core, spot_y, spot_x = place_ref[0], place_ref[1], place_ref[2]
     blocks, part, n = mine_ref.shape
     side = math.isqrt(blocks)
@@ -206,20 +206,20 @@
             other_ref[k * side + i] = turned[block(1 - core, k, i)]
 
 
-def turn(place, lines, blocks):
+def turn(place, lines, blocks, after):
     n, width = lines.shape
     part = width // (2 * blocks)
     half = jax.ShapeDtypeStruct((blocks, part, n), BF16)
     return pl.pallas_call(
         turn_kernel,
         out_shape=(half, half),
-        in_specs=[SMEM, VMEM],
+        in_specs=[SMEM, VMEM, ANY],
         out_specs=(VMEM, VMEM),
         scratch_shapes=[pltpu.VMEM((2 * blocks, part, n), BF16)],
         compiler_params=params(24),
         cost_estimate=cost(10**6, 2 * 10**6),
         name="turn",
-    )(place, lines)
+    )(place, lines, after)
 
 
 def partial_kernel(mine_ref, other_ref, ends_ref, ends_other_ref, *out_refs):
@@ -573,11 +573,8 @@
     return groups
 
 
-def spread(block, side, first):
-    return [
-        lax.ppermute(block, SEQ, line_pairs(side, first, distance))
-        for distance in (1, side - 1, 2)
-    ]
+def spread(block, side, first, order):
+    return [lax.ppermute(block, SEQ, line_pairs(side, first, k)) for k in order]
 
 
 def halo(first, last):
@@ -637,14 +634,14 @@
         asking_projector,
         picked,
     )
-    chip_keys, _ = stack([key_own, lax.ppermute(key_out, "core", swap)])
-    line_keys, line_done = stack([chip_keys] + spread(chip_keys, side, True))
-    keys = [line_keys] + spread(line_keys, side, False)
+    chip_keys, chip_done = stack([key_own, lax.ppermute(key_out, "core", swap)])
+    line_keys, line_done = stack([chip_keys] + spread(chip_keys, side, True, (2, 1, side - 1)))
+    keys = [line_keys] + spread(line_keys, side, False, (1, side - 1, 2))
     query_in = lax.ppermute(query_out, "core", swap)
 
     portion = splice_readout_lines[0].reshape(batch * rows, width)
     place = jnp.stack([core, lax.axis_index("y"), lax.axis_index("x")]).astype(I32)
-    mine, other = turn(place, portion, shards // 2)
+    mine, other = turn(place, portion, shards // 2, chip_done)
     other = lax.ppermute(other, "core", swap)
 
     ends = make_ends(arrived, batch, rows, line_done, other)

time: 94.3 us -> 91.6 us (0.971); the launches traced: 92.5 us -> 90.9 us
  starting transfers between devices: 39.2 us -> 37.7 us
  waiting for transfers between devices: 8.17 us -> 9.35 us
    ppermute x1, starting transfers between devices: 2.49 us -> 0.01 us  [body(): lax.ppermute(out, 'core', swap)]
    all_to_all x1, waiting for transfers between devices: 0.1 us -> 2.18 us  [body(): lax.all_to_all(line_terms, SEQ + ('dp',), 0, 0, axis_index_groups=lines_o...]
    all_to_all x1, starting transfers between devices: 3.54 us -> 5.26 us  [body(): lax.all_to_all(line_terms, SEQ + ('dp',), 0, 0, axis_index_groups=lines_o...]
    ppermute x3, starting transfers between devices: 8.4 us -> 6.68 us  [body(): lax.ppermute(partial[k], SEQ, line_pairs(side, True, k))]
    ppermute x7, waiting for transfers between devices: 8.04 us -> 6.84 us  [the longest x6 5.73 us: spread(): return [lax.ppermute(block, SEQ, line_pairs(side, first, k)) for k in order]]
  transfers between devices with their start and end apart: 18 -> 18, of which waited for: 4 -> 6; matrix products, arithmetic and copies ran while one was open for 1% -> 1% of each run, Pallas kernels for 36% -> 37%
where the time goes in v6:
time: 91.6 us; the launch traced here: 90.9 us
  starting transfers between devices  37.7 us (41%)
  Pallas kernels  35.8 us (39%)
  waiting for transfers between devices  9.35 us (10%)
  local copies, waits for them, and re-layouts  7.09 us (8%)
    ppermute x6, starting transfers between devices, spread(): return [lax.ppermute(block, SEQ, line_pairs(side, first, k)) for k in order]  11.2 us
    all_to_all x1, starting transfers between devices, body(): arrived = lax.all_to_all(payload, SEQ, 0, 0, tiled=True)  10.7 us
    pallas_call x1, Pallas kernels, encode(): pl.pallas_call(encoder_kernel, out_shape=(jax.ShapeDtypeStruct((n, width)...  8.98 us
    pallas_call x1, Pallas kernels, attend_first(): pl.pallas_call(attend_first_kernel, out_shape=(part, part, part), in_spec...  7.07 us
    pallas_call x1, Pallas kernels, attend_rest(): pl.pallas_call(attend_rest_kernel, out_shape=(shape, shape, TOKEN), in_sp...  6.84 us
    ppermute x3, starting transfers between devices, body(): lax.ppermute(partial[k], SEQ, line_pairs(side, True, k))  6.68 us
    ppermute x6, waiting for transfers between devices, spread(): return [lax.ppermute(block, SEQ, line_pairs(side, first, k)) for k in order]  5.73 us
    unnamed x24, local copies, waits for them, and re-layouts  5.73 us
  transfers between devices with their start and end apart: 18, of which 6 were waited for; matrix products, arithmetic and copies ran while one was open for 1% of the time, Pallas kernels for 37%

profile of v6, /device:TPU:64, one launch (start us, length us, event | category | flops | bytes accessed | tf_op | source)
XLA Modules:
  0.0 90.9 jit_solution(11703960296890459568)
XLA Ops:
  1.4 1.7 %collective-permute-start = (bf16[2,2,768]{2,1,0:T(2,128)(2,1)S(1)}, bf16[2,2,768]{2,1,0:T(2,128)(2,1)S(1)}, u32[]{:S(2)}, u32[]{:S(2)}) collective-permute-start(bf16[2,2,768]{2,1,0:T(2,128)(2,1)S(1)} %get-tuple-element.56), channel_id=1, source_target_pairs={{0,2},{2,4},{4,6},{6,8},{8,10},{10,12},{12,14},{14,16},{16,18},{18... | collective-permute-start | bytes 18440 | tf_op jit(solution)/shard_map/ppermute | solution.py:584
  3.1 1.3 %collective-permute-start.1 = (bf16[2,2,768]{2,1,0:T(2,128)(2,1)S(1)}, bf16[2,2,768]{2,1,0:T(2,128)(2,1)S(1)}, u32[]{:S(2)}, u32[]{:S(2)}) collective-permute-start(bf16[2,2,768]{2,1,0:T(2,128)(2,1)S(1)} %get-tuple-element.55), channel_id=1, source_target_pairs={{2,0},{4,2},{6,4},{8,6},{10,8},{12,10},{14,12},{16,14},{18,16},{20... | collective-permute-start | bytes 18440 | tf_op jit(solution)/shard_map/ppermute | solution.py:584
  4.5 3.3 %pick.1 = (bf16[32,16,1664]{2,1,0:T(8,128)(2,1)}, f32[8,128]{1,0:T(8,128)}) custom-call(s32[2,16,32]{2,1,0:T(8,128)} %bitcast.21, s32[2,16,32]{2,1,0:T(8,128)} %bitcast.22, s32[2,32]{1,0:T(2,128)} %bitcast.23, bf16[2,128,768]{2,1,0:T(8,128)(2,1)} %bitcast.20), custom_call_target="tpu_custom_call" | custom-call | flops 200000000 | bytes 3000000 | tf_op jit(solution)/shard_map/pick/pallas_call | solution.py:101
  8.4 10.7 %all-to-all-start = ((bf16[32,16,1664]{2,1,0:T(8,128)(2,1)}), bf16[32,16,1664]{2,1,0:T(8,128)(2,1)S(1)}, u32[]{:S(2)}, u32[]{:S(2)}) async-start(bf16[32,16,1664]{2,1,0:T(8,128)(2,1)} %follow.1), calls=%async_computation | async-start | bytes 3407872 | tf_op jit(solution)/shard_map/all_to_all | solution.py:623
  19.7 9.0 %encode.1 = (bf16[256,1536]{1,0:T(8,128)(2,1)}, bf16[128,256]{1,0:T(8,128)(2,1)}, bf16[128,256]{1,0:T(8,128)(2,1)}, bf16[128,1024]{1,0:T(8,128)(2,1)}, bf16[128,1024]{1,0:T(8,128)(2,1)}, /*index=5*/f32[8,128]{1,0:T(8,128)}) custom-call(s32[1]{0:T(128)} %bitcast.1.core_ref, bf16[2,2,768]{2,1,0:T(2,128)(2,1)} %copy-done.9, bf16[2,2,768]{2,1,0:T(2,128)(2,1)} %copy-done.10, ...), custom_call_target="tpu_custom_call" | custom-call | flops 3400000000 | bytes 12000000 | tf_op jit(solution)/shard_map/encode/pallas_call | solution.py:362
  29.1 1.1 %collective-permute-done.3.refs_1_ = bf16[128,256]{1,0:T(8,128)(2,1)S(1)} collective-permute-done((bf16[128,256]{1,0:T(8,128)(2,1)}, bf16[128,256]{1,0:T(8,128)(2,1)S(1)}, u32[]{:S(2)}, u32[]{:S(2)}) %collective-permute-start.3) | collective-permute-done | bytes 65568 | tf_op jit(solution)/shard_map/ppermute | solution.py:637
  32.3 3.2 %collective-permute-start.4 = (bf16[256,256]{1,0:T(8,128)(2,1)S(1)}, bf16[256,256]{1,0:T(8,128)(2,1)S(1)}, u32[]{:S(2)}, u32[]{:S(2)}) collective-permute-start(bf16[256,256]{1,0:T(8,128)(2,1)S(1)} %get-tuple-element.35.refs_0_), channel_id=1, source_target_pairs={{0,8},{2,34},{4,12},{6,38},{8,0},{10,42},{12,4},{14,46},{16,24},{1... | collective-permute-start | bytes 393224 | tf_op jit(solution)/shard_map/ppermute | solution.py:577
  36.1 2.7 %collective-permute-start.6 = (bf16[256,256]{1,0:T(8,128)(2,1)S(1)}, bf16[256,256]{1,0:T(8,128)(2,1)S(1)}, u32[]{:S(2)}, u32[]{:S(2)}) collective-permute-start(bf16[256,256]{1,0:T(8,128)(2,1)S(1)} %get-tuple-element.35.refs_0_), channel_id=1, source_target_pairs={{0,12},{2,50},{4,0},{6,54},{8,4},{10,58},{12,8},{14,62},{16,28},{1... | collective-permute-start | bytes 393224 | tf_op jit(solution)/shard_map/ppermute | solution.py:577
  38.8 5.1 %collective-permute-done.4.refs_1_ = bf16[256,256]{1,0:T(8,128)(2,1)S(1)} collective-permute-done((bf16[256,256]{1,0:T(8,128)(2,1)S(1)}, bf16[256,256]{1,0:T(8,128)(2,1)S(1)}, u32[]{:S(2)}, u32[]{:S(2)}) %collective-permute-start.4) | collective-permute-done | bytes 131104 | tf_op jit(solution)/shard_map/ppermute | solution.py:577
  45.4 1.8 %collective-permute-start.7 = (bf16[1024,256]{1,0:T(8,128)(2,1)S(1)}, bf16[1024,256]{1,0:T(8,128)(2,1)}, u32[]{:S(2)}, u32[]{:S(2)}) collective-permute-start(bf16[1024,256]{1,0:T(8,128)(2,1)S(1)} %get-tuple-element.36.refs_0_), channel_id=1, source_target_pairs={{0,16},{2,6},{4,20},{6,10},{8,24},{10,14},{12,28},{14,2},{16,32},{... | collective-permute-start | bytes 1572872 | tf_op jit(solution)/shard_map/ppermute | solution.py:577
  47.2 1.5 %collective-permute-start.10 = (bf16[1024,256]{1,0:T(8,128)(2,1)S(1)}, bf16[1024,256]{1,0:T(8,128)(2,1)S(1)}, u32[]{:S(2)}, u32[]{:S(2)}) collective-permute-start(bf16[1024,256]{1,0:T(8,128)(2,1)S(1)} %get-tuple-element.36.refs_0_), channel_id=1, source_target_pairs={{0,48},{2,14},{4,52},{6,2},{8,56},{10,6},{12,60},{14,10},{16,0},{1... | collective-permute-start | bytes 1572872 | tf_op jit(solution)/shard_map/ppermute | solution.py:577
  48.7 1.5 %collective-permute-start.11 = (bf16[1024,256]{1,0:T(8,128)(2,1)S(1)}, bf16[1024,256]{1,0:T(8,128)(2,1)}, u32[]{:S(2)}, u32[]{:S(2)}) collective-permute-start(bf16[1024,256]{1,0:T(8,128)(2,1)S(1)} %get-tuple-element.36.refs_0_), channel_id=1, source_target_pairs={{0,32},{2,10},{4,36},{6,14},{8,40},{10,2},{12,44},{14,6},{16,48},{... | collective-permute-start | bytes 1572872 | tf_op jit(solution)/shard_map/ppermute | solution.py:577
  50.2 1.0 %copy-done.6 = bf16[16,48,256]{2,1,0:T(8,128)(2,1)S(1)} copy-done((bf16[16,48,256]{2,1,0:T(8,128)(2,1)S(1)}, bf16[16,48,256]{2,1,0:T(8,128)(2,1)}, u32[]{:S(2)}) %copy-start.6) | copy-done | bytes 393240
  51.2 1.4 %partial_grad.1 = (bf16[192,1536]{1,0:T(8,128)(2,1)S(1)}, bf16[192,1536]{1,0:T(8,128)(2,1)S(1)}, bf16[192,1536]{1,0:T(8,128)(2,1)S(1)}, bf16[192,1536]{1,0:T(8,128)(2,1)S(1)}, f32[8,128]{1,0:T(8,128)S(1)}) custom-call(bf16[16,48,256]{2,1,0:T(8,128)(2,1)S(1)} %copy-done.6, bf16[16,48,256]{2,1,0:T(8,128)(2,1)S(1)} %collective-permute-done.8._other.other_ref, ...), custom_call_target="tpu_custom_call" | custom-call | flops 1200000000 | bytes 5000000 | tf_op jit(solution)/shard_map/partial_grad/pallas_call | solution.py:242
  53.3 2.7 %collective-permute-start.14 = (bf16[192,1536]{1,0:T(8,128)(2,1)S(1)}, bf16[192,1536]{1,0:T(8,128)(2,1)S(1)}, u32[]{:S(2)}, u32[]{:S(2)}) collective-permute-start(bf16[192,1536]{1,0:T(8,128)(2,1)S(1)} %get-tuple-element.51), channel_id=1, source_target_pairs={{0,12},{2,50},{4,0},{6,54},{8,4},{10,58},{12,8},{14,62},{16,28},{1... | collective-permute-start | bytes 1769480 | tf_op jit(solution)/shard_map/ppermute | solution.py:651
  56.0 3.4 %collective-permute-start.15 = (bf16[192,1536]{1,0:T(8,128)(2,1)S(1)}, bf16[192,1536]{1,0:T(8,128)(2,1)S(1)}, u32[]{:S(2)}, u32[]{:S(2)}) collective-permute-start(bf16[192,1536]{1,0:T(8,128)(2,1)S(1)} %get-tuple-element.52), channel_id=1, source_target_pairs={{0,8},{2,34},{4,12},{6,38},{8,0},{10,42},{12,4},{14,46},{16,24},{1... | collective-permute-start | bytes 1769480 | tf_op jit(solution)/shard_map/ppermute | solution.py:651
  60.3 7.1 %attend_first.1 = (f32[256,1024]{1,0:T(8,128)S(1)}, f32[256,1024]{1,0:T(8,128)S(1)}, f32[256,1024]{1,0:T(8,128)S(1)}) custom-call(s32[1]{0:T(128)} %bitcast.phase_ref, f32[8]{0:T(128)S(1)} %broadcast_multiply_fusion.logit_ref, bf16[128,1024]{1,0:T(8,128)(2,1)S(1)} %copy-done.7, bf16[128,1024]{1,0:T(8,128)(2,1)S(1)} %collective-permute-done.2.query_in_ref, ...), custom_call_target="tpu_custom_call" | custom-call | flops 1000000000 | bytes 4000000 | tf_op jit(solution)/shard_map/attend_first/pallas_call | solution.py:431
  67.6 6.8 %attend_rest.1 = (bf16[128,1024]{1,0:T(8,128)(2,1)S(1)}, bf16[128,1024]{1,0:T(8,128)(2,1)S(1)}, f32[8,128]{1,0:T(8,128)S(1)}) custom-call(s32[1]{0:T(128)} %bitcast.phase_ref, f32[8]{0:T(128)S(1)} %broadcast_multiply_fusion.logit_ref, bf16[128,1024]{1,0:T(8,128)(2,1)S(1)} %copy-done.7, bf16[128,1024]{1,0:T(8,128)(2,1)S(1)} %collective-permute-done.2.query_in_ref, ...), custom_call_target="tpu_custom_call" | custom-call | flops 60000002048 | bytes 4000000 | tf_op jit(solution)/shard_map/attend_rest/pallas_call | solution.py:468
  74.5 1.1 %line_sum.1 = bf16[8,24,1536]{2,1,0:T(8,128)(2,1)} custom-call(bf16[192,1536]{1,0:T(8,128)(2,1)S(1)} %get-tuple-element.49.refs_0_, bf16[192,1536]{1,0:T(8,128)(2,1)S(1)} %collective-permute-done.13.refs_1_, bf16[192,1536]{1,0:T(8,128)(2,1)S(1)} %collective-permute-done.14.refs_2_, bf16[192,1536]{1,0:T(8,128)(2,1)S(1)} %collective-permute-done.15.refs_3_, ...), custom_call_target="tpu_custom_call" | custom-call | flops 1000000 | bytes 3000000 | tf_op jit(solution)/shard_map/line_sum/pallas_call | solution.py:261
  75.6 5.3 %all-to-all-start.1 = ((bf16[8,24,1536]{2,1,0:T(8,128)(2,1)}), bf16[8,24,1536]{2,1,0:T(8,128)(2,1)S(1)}, u32[]{:S(2)}, u32[]{:S(2)}) async-start(bf16[8,24,1536]{2,1,0:T(8,128)(2,1)} %line_sum.1), calls=%async_computation.1 | async-start | bytes 1179648 | tf_op jit(solution)/shard_map/all_to_all | solution.py:667
  80.9 2.3 %copy-done = bf16[2,1536,768]{2,1,0:T(8,128)(2,1)S(1)} copy-done((bf16[2,1536,768]{2,1,0:T(8,128)(2,1)S(1)}, bf16[2,1536,768]{2,1,0:T(8,128)(2,1)}, u32[]{:S(2)}) %copy-start) | copy-done | bytes 4718616
  83.2 2.9 %row_grad.1 = bf16[256,1536]{1,0:T(8,128)(2,1)} custom-call(bf16[256,1536]{1,0:T(8,128)(2,1)S(1)} %ends.1.ends_ref, bf16[2,1536,768]{2,1,0:T(8,128)(2,1)S(1)} %copy-done, f32[8,128]{1,0:T(8,128)S(1)} %get-tuple-element.42.refs_2_._token), custom_call_target="tpu_custom_call" | custom-call | flops 1200000000 | bytes 6000000 | tf_op jit(solution)/shard_map/row_grad/pallas_call | solution.py:176
  86.1 1.9 %leave.1 = (bf16[256,1536]{1,0:T(8,128)(2,1)}, f32[8,128]{1,0:T(8,128)S(1)}) custom-call(s32[1]{0:T(128)} %bitcast.phase_ref, s32[1]{0:T(128)} %bitcast.1.core_ref, bf16[256,1536]{1,0:T(8,128)(2,1)S(1)} %copy-done.2, bf16[128,1024]{1,0:T(8,128)(2,1)S(1)} %get-tuple-element.46.own_ref, bf16[128,1024]{1,0:T(8,128)(2,1)S(1)} %collective-permute-done.12.in_ref, ...), custom_call_target="tpu_custom_call" | custom-call | flops 800000000 | bytes 5000000 | tf_op jit(solution)/shard_map/leave/pallas_call | solution.py:502
  87.9 2.2 %all-to-all-done.1.pieces_ref = bf16[8,24,1536]{2,1,0:T(8,128)(2,1)S(1)} async-done(((bf16[8,24,1536]{2,1,0:T(8,128)(2,1)}), bf16[8,24,1536]{2,1,0:T(8,128)(2,1)S(1)}, u32[]{:S(2)}, u32[]{:S(2)}) %all-to-all-start.1) | async-done | bytes 589856 | tf_op jit(solution)/shard_map/all_to_all | solution.py:667
  (54 shorter events, 9.1 us)
Async XLA Ops:
  1.4 6.4 %collective-permute-start = (bf16[2,2,768]{2,1,0:T(2,128)(2,1)S(1)}, bf16[2,2,768]{2,1,0:T(2,128)(2,1)S(1)}, u32[]{:S(2)}, u32[]{:S(2)}) collective-permute-start(bf16[2,2,768]{2,1,0:T(2,128)(2,1)S(1)} %get-tuple-element.56), channel_id=1, source_target_pairs={{0,2},{2,4},{4,6},{6,8},{8,10},{10,12},{12,14},{14,16},{16,18},{18... | collective-permute-start | bytes 18440 | tf_op jit(solution)/shard_map/ppermute | solution.py:584
  3.1 4.6 %collective-permute-start.1 = (bf16[2,2,768]{2,1,0:T(2,128)(2,1)S(1)}, bf16[2,2,768]{2,1,0:T(2,128)(2,1)S(1)}, u32[]{:S(2)}, u32[]{:S(2)}) collective-permute-start(bf16[2,2,768]{2,1,0:T(2,128)(2,1)S(1)} %get-tuple-element.55), channel_id=1, source_target_pairs={{2,0},{4,2},{6,4},{8,6},{10,8},{12,10},{14,12},{16,14},{18,16},{20... | collective-permute-start | bytes 18440 | tf_op jit(solution)/shard_map/ppermute | solution.py:584
  8.4 10.7 %copy-start.8 = (f32[1536]{0:T(1024)S(1)}, f32[1536]{0:T(1024)}, u32[]{:S(2)}) copy-start(f32[1536]{0:T(1024)} %param.17) | copy-start | bytes 18436
  8.4 36.2 %all-to-all-start = ((bf16[32,16,1664]{2,1,0:T(8,128)(2,1)}), bf16[32,16,1664]{2,1,0:T(8,128)(2,1)S(1)}, u32[]{:S(2)}, u32[]{:S(2)}) async-start(bf16[32,16,1664]{2,1,0:T(8,128)(2,1)} %follow.1), calls=%async_computation | async-start | bytes 3407872 | tf_op jit(solution)/shard_map/all_to_all | solution.py:623
  19.7 11.4 %copy-start.3 = (bf16[1,2,128,1536]{3,2,1,0:T(8,128)(2,1)S(1)}, bf16[1,2,128,1536]{3,2,1,0:T(8,128)(2,1)}, u32[]{:S(2)}) copy-start(bf16[1,2,128,1536]{3,2,1,0:T(8,128)(2,1)} %param.22) | copy-start | bytes 2359300
  28.7 21.5 %copy-start.11 = (f32[8]{0:T(128)S(1)}, f32[8]{0:T(128)}, u32[]{:S(2)}) copy-start(f32[8]{0:T(128)} %param.21) | copy-start | bytes 100
  28.7 1.5 %collective-permute-start.3 = (bf16[128,256]{1,0:T(8,128)(2,1)}, bf16[128,256]{1,0:T(8,128)(2,1)S(1)}, u32[]{:S(2)}, u32[]{:S(2)}) collective-permute-start(bf16[128,256]{1,0:T(8,128)(2,1)} %get-tuple-element.34), channel_id=1, source_target_pairs={{0,2},{2,0},{1,3},{3,1},{4,6},{6,4},{5,7},{7,5},{8,10},{10,8},{9,1... | collective-permute-start | bytes 196616 | tf_op jit(solution)/shard_map/ppermute | solution.py:637
  32.0 12.3 %copy-start.5 = (bf16[16,48,256]{2,1,0:T(8,128)(2,1)}, bf16[16,48,256]{2,1,0:T(8,128)(2,1)S(1)}, u32[]{:S(2)}) copy-start(bf16[16,48,256]{2,1,0:T(8,128)(2,1)S(1)} %get-tuple-element.38.mine_ref) | copy-start | bytes 1179652
  32.0 12.3 %collective-permute-start.8 = (bf16[16,48,256]{2,1,0:T(8,128)(2,1)S(1)}, bf16[16,48,256]{2,1,0:T(8,128)(2,1)S(1)}, u32[]{:S(2)}, u32[]{:S(2)}) collective-permute-start(bf16[16,48,256]{2,1,0:T(8,128)(2,1)S(1)} %get-tuple-element.39), channel_id=1, source_target_pairs={{0,2},{2,0},{1,3},{3,1},{4,6},{6,4},{5,7},{7,5},{8,10},{10,8},{9,1... | collective-permute-start | bytes 1179656 | tf_op jit(solution)/shard_map/ppermute | solution.py:645
  32.3 11.6 %collective-permute-start.4 = (bf16[256,256]{1,0:T(8,128)(2,1)S(1)}, bf16[256,256]{1,0:T(8,128)(2,1)S(1)}, u32[]{:S(2)}, u32[]{:S(2)}) collective-permute-start(bf16[256,256]{1,0:T(8,128)(2,1)S(1)} %get-tuple-element.35.refs_0_), channel_id=1, source_target_pairs={{0,8},{2,34},{4,12},{6,38},{8,0},{10,42},{12,4},{14,46},{16,24},{1... | collective-permute-start | bytes 393224 | tf_op jit(solution)/shard_map/ppermute | solution.py:577
  35.5 8.7 %collective-permute-start.5 = (bf16[256,256]{1,0:T(8,128)(2,1)S(1)}, bf16[256,256]{1,0:T(8,128)(2,1)S(1)}, u32[]{:S(2)}, u32[]{:S(2)}) collective-permute-start(bf16[256,256]{1,0:T(8,128)(2,1)S(1)} %get-tuple-element.35.refs_0_), channel_id=1, source_target_pairs={{0,4},{2,18},{4,8},{6,22},{8,12},{10,26},{12,0},{14,30},{16,20},{1... | collective-permute-start | bytes 393224 | tf_op jit(solution)/shard_map/ppermute | solution.py:577
  36.1 8.2 %collective-permute-start.6 = (bf16[256,256]{1,0:T(8,128)(2,1)S(1)}, bf16[256,256]{1,0:T(8,128)(2,1)S(1)}, u32[]{:S(2)}, u32[]{:S(2)}) collective-permute-start(bf16[256,256]{1,0:T(8,128)(2,1)S(1)} %get-tuple-element.35.refs_0_), channel_id=1, source_target_pairs={{0,12},{2,50},{4,0},{6,54},{8,4},{10,58},{12,8},{14,62},{16,28},{1... | collective-permute-start | bytes 393224 | tf_op jit(solution)/shard_map/ppermute | solution.py:577
  45.3 4.9 %collective-permute-start.9 = (bf16[256,1536]{1,0:T(8,128)(2,1)S(1)}, bf16[256,1536]{1,0:T(8,128)(2,1)S(1)}, u32[]{:S(2)}, u32[]{:S(2)}) collective-permute-start(bf16[256,1536]{1,0:T(8,128)(2,1)S(1)} %ends.1.ends_ref), channel_id=1, source_target_pairs={{0,2},{2,0},{1,3},{3,1},{4,6},{6,4},{5,7},{7,5},{8,10},{10,8},{9,1... | collective-permute-start | bytes 2359304 | tf_op jit(solution)/shard_map/ppermute | solution.py:648
  45.4 10.6 %collective-permute-start.7 = (bf16[1024,256]{1,0:T(8,128)(2,1)S(1)}, bf16[1024,256]{1,0:T(8,128)(2,1)}, u32[]{:S(2)}, u32[]{:S(2)}) collective-permute-start(bf16[1024,256]{1,0:T(8,128)(2,1)S(1)} %get-tuple-element.36.refs_0_), channel_id=1, source_target_pairs={{0,16},{2,6},{4,20},{6,10},{8,24},{10,14},{12,28},{14,2},{16,32},{... | collective-permute-start | bytes 1572872 | tf_op jit(solution)/shard_map/ppermute | solution.py:577
  47.2 20.2 %collective-permute-start.10 = (bf16[1024,256]{1,0:T(8,128)(2,1)S(1)}, bf16[1024,256]{1,0:T(8,128)(2,1)S(1)}, u32[]{:S(2)}, u32[]{:S(2)}) collective-permute-start(bf16[1024,256]{1,0:T(8,128)(2,1)S(1)} %get-tuple-element.36.refs_0_), channel_id=1, source_target_pairs={{0,48},{2,14},{4,52},{6,2},{8,56},{10,6},{12,60},{14,10},{16,0},{1... | collective-permute-start | bytes 1572872 | tf_op jit(solution)/shard_map/ppermute | solution.py:577
  48.7 18.9 %collective-permute-start.11 = (bf16[1024,256]{1,0:T(8,128)(2,1)S(1)}, bf16[1024,256]{1,0:T(8,128)(2,1)}, u32[]{:S(2)}, u32[]{:S(2)}) collective-permute-start(bf16[1024,256]{1,0:T(8,128)(2,1)S(1)} %get-tuple-element.36.refs_0_), channel_id=1, source_target_pairs={{0,32},{2,10},{4,36},{6,14},{8,40},{10,2},{12,44},{14,6},{16,48},{... | collective-permute-start | bytes 1572872 | tf_op jit(solution)/shard_map/ppermute | solution.py:577
  50.2 3.1 %collective-permute-start.2 = (bf16[128,1024]{1,0:T(8,128)(2,1)}, bf16[128,1024]{1,0:T(8,128)(2,1)S(1)}, u32[]{:S(2)}, u32[]{:S(2)}) collective-permute-start(bf16[128,1024]{1,0:T(8,128)(2,1)} %get-tuple-element.32), channel_id=1, source_target_pairs={{0,2},{2,0},{1,3},{3,1},{4,6},{6,4},{5,7},{7,5},{8,10},{10,8},{9,1... | collective-permute-start | bytes 786440 | tf_op jit(solution)/shard_map/ppermute | solution.py:640
  52.6 21.8 %collective-permute-start.13 = (bf16[192,1536]{1,0:T(8,128)(2,1)S(1)}, bf16[192,1536]{1,0:T(8,128)(2,1)S(1)}, u32[]{:S(2)}, u32[]{:S(2)}) collective-permute-start(bf16[192,1536]{1,0:T(8,128)(2,1)S(1)} %get-tuple-element.50), channel_id=1, source_target_pairs={{0,4},{2,18},{4,8},{6,22},{8,12},{10,26},{12,0},{14,30},{16,20},{1... | collective-permute-start | bytes 1769480 | tf_op jit(solution)/shard_map/ppermute | solution.py:651
  53.3 21.2 %collective-permute-start.14 = (bf16[192,1536]{1,0:T(8,128)(2,1)S(1)}, bf16[192,1536]{1,0:T(8,128)(2,1)S(1)}, u32[]{:S(2)}, u32[]{:S(2)}) collective-permute-start(bf16[192,1536]{1,0:T(8,128)(2,1)S(1)} %get-tuple-element.51), channel_id=1, source_target_pairs={{0,12},{2,50},{4,0},{6,54},{8,4},{10,58},{12,8},{14,62},{16,28},{1... | collective-permute-start | bytes 1769480 | tf_op jit(solution)/shard_map/ppermute | solution.py:651
  56.0 18.5 %collective-permute-start.15 = (bf16[192,1536]{1,0:T(8,128)(2,1)S(1)}, bf16[192,1536]{1,0:T(8,128)(2,1)S(1)}, u32[]{:S(2)}, u32[]{:S(2)}) collective-permute-start(bf16[192,1536]{1,0:T(8,128)(2,1)S(1)} %get-tuple-element.52), channel_id=1, source_target_pairs={{0,8},{2,34},{4,12},{6,38},{8,0},{10,42},{12,4},{14,46},{16,24},{1... | collective-permute-start | bytes 1769480 | tf_op jit(solution)/shard_map/ppermute | solution.py:651
  75.6 14.6 %all-to-all-start.1 = ((bf16[8,24,1536]{2,1,0:T(8,128)(2,1)}), bf16[8,24,1536]{2,1,0:T(8,128)(2,1)S(1)}, u32[]{:S(2)}, u32[]{:S(2)}) async-start(bf16[8,24,1536]{2,1,0:T(8,128)(2,1)} %line_sum.1), calls=%async_computation.1 | async-start | bytes 1179648 | tf_op jit(solution)/shard_map/all_to_all | solution.py:667
  80.8 5.2 %collective-permute-start.12 = (bf16[128,1024]{1,0:T(8,128)(2,1)S(1)}, bf16[128,1024]{1,0:T(8,128)(2,1)S(1)}, u32[]{:S(2)}, u32[]{:S(2)}) collective-permute-start(bf16[128,1024]{1,0:T(8,128)(2,1)S(1)} %get-tuple-element.47), channel_id=1, source_target_pairs={{0,2},{2,0},{1,3},{3,1},{4,6},{6,4},{5,7},{7,5},{8,10},{10,8},{9,1... | collective-permute-start | bytes 786440 | tf_op jit(solution)/shard_map/ppermute | solution.py:661
  83.2 2.9 %copy-start.1 = (bf16[1024,1536]{1,0:T(8,128)(2,1)S(1)}, bf16[1024,1536]{1,0:T(8,128)(2,1)}, u32[]{:S(2)}) copy-start(bf16[1024,1536]{1,0:T(8,128)(2,1)} %exit_ref.1) | copy-start | bytes 9437188
  83.2 2.9 %copy-start.2 = (bf16[256,1536]{1,0:T(8,128)(2,1)S(1)}, bf16[256,1536]{1,0:T(8,128)(2,1)}, u32[]{:S(2)}) copy-start(bf16[256,1536]{1,0:T(8,128)(2,1)} %get-tuple-element.30.rows_ref) | copy-start | bytes 2359300
  (6 other events, 6.3 us)

commit v7 on v6

--- a/solution.py
+++ b/solution.py
@@ -156,7 +156,7 @@
         out_shape=jax.ShapeDtypeStruct((batch * rows, 2 * embed), BF16),
         in_specs=[VMEM, ANY, ANY],
         out_specs=VMEM,
-        compiler_params=params(24),
+        compiler_params=params(14),
         cost_estimate=cost(4 * 10**8, 3 * 10**6),
         name="ends",
     )(arrived, token, other)
@@ -183,7 +183,7 @@
             ANY,
         ],
         out_specs=pl.BlockSpec((n, step), lambda i: (0, i)),
-        compiler_params=params(24),
+        compiler_params=params(16),
         cost_estimate=cost(1.2 * 10**9, 6 * 10**6),
         name="row_grad",
     )(ends, head, token)
@@ -216,7 +216,7 @@
         in_specs=[SMEM, VMEM, ANY],
         out_specs=(VMEM, VMEM),
         scratch_shapes=[pltpu.VMEM((2 * blocks, part, n), BF16)],
-        compiler_params=params(24),
+        compiler_params=params(10),
         cost_estimate=cost(10**6, 2 * 10**6),
         name="turn",
     )(place, lines, after)
@@ -244,7 +244,7 @@
         out_shape=(piece,) * side + (TOKEN,),
         in_specs=[VMEM] * 4,
         out_specs=(VMEM,) * (side + 1),
-        compiler_params=params(24),
+        compiler_params=params(14),
         cost_estimate=cost(1.2 * 10**9, 5 * 10**6),
         name="partial_grad",
     )(mine, other, ends, ends_other)
@@ -263,7 +263,7 @@
         out_shape=jax.ShapeDtypeStruct((count, rows // count, width), BF16),
         in_specs=[VMEM] * len(pieces) + [ANY],
         out_specs=VMEM,
-        compiler_params=params(24),
+        compiler_params=params(14),
         cost_estimate=cost(10**6, 3 * 10**6),
         name="line_sum",
     )(*pieces, after)
@@ -504,7 +504,7 @@
         out_shape=(jax.ShapeDtypeStruct(encoded.shape, BF16), TOKEN),
         in_specs=[SMEM, SMEM] + [VMEM] * 4,
         out_specs=(VMEM, VMEM),
-        compiler_params=params(32),
+        compiler_params=params(14),
         cost_estimate=cost(8 * 10**8, 5 * 10**6),
         name="leave",
     )(phase.reshape(1), core.reshape(1), encoded, own, arrived, exit_projector)
@@ -524,7 +524,7 @@
         out_shape=jax.ShapeDtypeStruct((2, rows, width // 2), F32),
         in_specs=[VMEM, ANY],
         out_specs=VMEM,
-        compiler_params=params(32),
+        compiler_params=params(10),
         cost_estimate=cost(10**6, 3 * 10**6),
         name="sum_terms",
     )(pieces, after)

time: 91.6 us -> 91.6 us (level)
  no operation moved by 1% of the time
where the time goes in v7:
time: 91.6 us; the launch traced here: 90.9 us
  starting transfers between devices  37.7 us (41%)
  Pallas kernels  35.8 us (39%)
  waiting for transfers between devices  9.33 us (10%)
  local copies, waits for them, and re-layouts  7.09 us (8%)
    ppermute x6, starting transfers between devices, spread(): return [lax.ppermute(block, SEQ, line_pairs(side, first, k)) for k in order]  11.2 us
    all_to_all x1, starting transfers between devices, body(): arrived = lax.all_to_all(payload, SEQ, 0, 0, tiled=True)  10.7 us
    pallas_call x1, Pallas kernels, encode(): pl.pallas_call(encoder_kernel, out_shape=(jax.ShapeDtypeStruct((n, width)...  8.98 us
    pallas_call x1, Pallas kernels, attend_first(): pl.pallas_call(attend_first_kernel, out_shape=(part, part, part), in_spec...  7.07 us
    pallas_call x1, Pallas kernels, attend_rest(): pl.pallas_call(attend_rest_kernel, out_shape=(shape, shape, TOKEN), in_sp...  6.84 us
    ppermute x3, starting transfers between devices, body(): lax.ppermute(partial[k], SEQ, line_pairs(side, True, k))  6.68 us
    ppermute x6, waiting for transfers between devices, spread(): return [lax.ppermute(block, SEQ, line_pairs(side, first, k)) for k in order]  5.73 us
    unnamed x24, local copies, waits for them, and re-layouts  5.73 us
  transfers between devices with their start and end apart: 18, of which 6 were waited for; matrix products, arithmetic and copies ran while one was open for 1% of the time, Pallas kernels for 37%

profile of v7, /device:TPU:64, one launch (start us, length us, event | category | flops | bytes accessed | tf_op | source)
XLA Modules:
  0.0 90.9 jit_solution(14921962678376822753)
XLA Ops:
  1.4 1.7 %collective-permute-start = (bf16[2,2,768]{2,1,0:T(2,128)(2,1)S(1)}, bf16[2,2,768]{2,1,0:T(2,128)(2,1)S(1)}, u32[]{:S(2)}, u32[]{:S(2)}) collective-permute-start(bf16[2,2,768]{2,1,0:T(2,128)(2,1)S(1)} %get-tuple-element.56), channel_id=1, source_target_pairs={{0,2},{2,4},{4,6},{6,8},{8,10},{10,12},{12,14},{14,16},{16,18},{18... | collective-permute-start | bytes 18440 | tf_op jit(solution)/shard_map/ppermute | solution.py:584
  3.1 1.3 %collective-permute-start.1 = (bf16[2,2,768]{2,1,0:T(2,128)(2,1)S(1)}, bf16[2,2,768]{2,1,0:T(2,128)(2,1)S(1)}, u32[]{:S(2)}, u32[]{:S(2)}) collective-permute-start(bf16[2,2,768]{2,1,0:T(2,128)(2,1)S(1)} %get-tuple-element.55), channel_id=1, source_target_pairs={{2,0},{4,2},{6,4},{8,6},{10,8},{12,10},{14,12},{16,14},{18,16},{20... | collective-permute-start | bytes 18440 | tf_op jit(solution)/shard_map/ppermute | solution.py:584
  4.5 3.3 %pick.1 = (bf16[32,16,1664]{2,1,0:T(8,128)(2,1)}, f32[8,128]{1,0:T(8,128)}) custom-call(s32[2,16,32]{2,1,0:T(8,128)} %bitcast.21, s32[2,16,32]{2,1,0:T(8,128)} %bitcast.22, s32[2,32]{1,0:T(2,128)} %bitcast.23, bf16[2,128,768]{2,1,0:T(8,128)(2,1)} %bitcast.20), custom_call_target="tpu_custom_call" | custom-call | flops 200000000 | bytes 3000000 | tf_op jit(solution)/shard_map/pick/pallas_call | solution.py:101
  8.4 10.7 %all-to-all-start = ((bf16[32,16,1664]{2,1,0:T(8,128)(2,1)}), bf16[32,16,1664]{2,1,0:T(8,128)(2,1)S(1)}, u32[]{:S(2)}, u32[]{:S(2)}) async-start(bf16[32,16,1664]{2,1,0:T(8,128)(2,1)} %follow.1), calls=%async_computation | async-start | bytes 3407872 | tf_op jit(solution)/shard_map/all_to_all | solution.py:623
  19.7 9.0 %encode.1 = (bf16[256,1536]{1,0:T(8,128)(2,1)}, bf16[128,256]{1,0:T(8,128)(2,1)}, bf16[128,256]{1,0:T(8,128)(2,1)}, bf16[128,1024]{1,0:T(8,128)(2,1)}, bf16[128,1024]{1,0:T(8,128)(2,1)}, /*index=5*/f32[8,128]{1,0:T(8,128)}) custom-call(s32[1]{0:T(128)} %bitcast.1.core_ref, bf16[2,2,768]{2,1,0:T(2,128)(2,1)} %copy-done.9, bf16[2,2,768]{2,1,0:T(2,128)(2,1)} %copy-done.10, ...), custom_call_target="tpu_custom_call" | custom-call | flops 3400000000 | bytes 12000000 | tf_op jit(solution)/shard_map/encode/pallas_call | solution.py:362
  29.1 1.1 %collective-permute-done.3.refs_1_ = bf16[128,256]{1,0:T(8,128)(2,1)S(1)} collective-permute-done((bf16[128,256]{1,0:T(8,128)(2,1)}, bf16[128,256]{1,0:T(8,128)(2,1)S(1)}, u32[]{:S(2)}, u32[]{:S(2)}) %collective-permute-start.3) | collective-permute-done | bytes 65568 | tf_op jit(solution)/shard_map/ppermute | solution.py:637
  32.3 3.2 %collective-permute-start.4 = (bf16[256,256]{1,0:T(8,128)(2,1)S(1)}, bf16[256,256]{1,0:T(8,128)(2,1)S(1)}, u32[]{:S(2)}, u32[]{:S(2)}) collective-permute-start(bf16[256,256]{1,0:T(8,128)(2,1)S(1)} %get-tuple-element.35.refs_0_), channel_id=1, source_target_pairs={{0,8},{2,34},{4,12},{6,38},{8,0},{10,42},{12,4},{14,46},{16,24},{1... | collective-permute-start | bytes 393224 | tf_op jit(solution)/shard_map/ppermute | solution.py:577
  36.1 2.7 %collective-permute-start.6 = (bf16[256,256]{1,0:T(8,128)(2,1)S(1)}, bf16[256,256]{1,0:T(8,128)(2,1)S(1)}, u32[]{:S(2)}, u32[]{:S(2)}) collective-permute-start(bf16[256,256]{1,0:T(8,128)(2,1)S(1)} %get-tuple-element.35.refs_0_), channel_id=1, source_target_pairs={{0,12},{2,50},{4,0},{6,54},{8,4},{10,58},{12,8},{14,62},{16,28},{1... | collective-permute-start | bytes 393224 | tf_op jit(solution)/shard_map/ppermute | solution.py:577
  38.8 5.1 %collective-permute-done.4.refs_1_ = bf16[256,256]{1,0:T(8,128)(2,1)S(1)} collective-permute-done((bf16[256,256]{1,0:T(8,128)(2,1)S(1)}, bf16[256,256]{1,0:T(8,128)(2,1)S(1)}, u32[]{:S(2)}, u32[]{:S(2)}) %collective-permute-start.4) | collective-permute-done | bytes 131104 | tf_op jit(solution)/shard_map/ppermute | solution.py:577
  45.4 1.8 %collective-permute-start.7 = (bf16[1024,256]{1,0:T(8,128)(2,1)S(1)}, bf16[1024,256]{1,0:T(8,128)(2,1)}, u32[]{:S(2)}, u32[]{:S(2)}) collective-permute-start(bf16[1024,256]{1,0:T(8,128)(2,1)S(1)} %get-tuple-element.36.refs_0_), channel_id=1, source_target_pairs={{0,16},{2,6},{4,20},{6,10},{8,24},{10,14},{12,28},{14,2},{16,32},{... | collective-permute-start | bytes 1572872 | tf_op jit(solution)/shard_map/ppermute | solution.py:577
  47.2 1.5 %collective-permute-start.10 = (bf16[1024,256]{1,0:T(8,128)(2,1)S(1)}, bf16[1024,256]{1,0:T(8,128)(2,1)S(1)}, u32[]{:S(2)}, u32[]{:S(2)}) collective-permute-start(bf16[1024,256]{1,0:T(8,128)(2,1)S(1)} %get-tuple-element.36.refs_0_), channel_id=1, source_target_pairs={{0,48},{2,14},{4,52},{6,2},{8,56},{10,6},{12,60},{14,10},{16,0},{1... | collective-permute-start | bytes 1572872 | tf_op jit(solution)/shard_map/ppermute | solution.py:577
  48.7 1.5 %collective-permute-start.11 = (bf16[1024,256]{1,0:T(8,128)(2,1)S(1)}, bf16[1024,256]{1,0:T(8,128)(2,1)}, u32[]{:S(2)}, u32[]{:S(2)}) collective-permute-start(bf16[1024,256]{1,0:T(8,128)(2,1)S(1)} %get-tuple-element.36.refs_0_), channel_id=1, source_target_pairs={{0,32},{2,10},{4,36},{6,14},{8,40},{10,2},{12,44},{14,6},{16,48},{... | collective-permute-start | bytes 1572872 | tf_op jit(solution)/shard_map/ppermute | solution.py:577
  50.2 1.0 %copy-done.6 = bf16[16,48,256]{2,1,0:T(8,128)(2,1)S(1)} copy-done((bf16[16,48,256]{2,1,0:T(8,128)(2,1)S(1)}, bf16[16,48,256]{2,1,0:T(8,128)(2,1)}, u32[]{:S(2)}) %copy-start.6) | copy-done | bytes 393240
  51.2 1.4 %partial_grad.1 = (bf16[192,1536]{1,0:T(8,128)(2,1)S(1)}, bf16[192,1536]{1,0:T(8,128)(2,1)S(1)}, bf16[192,1536]{1,0:T(8,128)(2,1)S(1)}, bf16[192,1536]{1,0:T(8,128)(2,1)S(1)}, f32[8,128]{1,0:T(8,128)S(1)}) custom-call(bf16[16,48,256]{2,1,0:T(8,128)(2,1)S(1)} %copy-done.6, bf16[16,48,256]{2,1,0:T(8,128)(2,1)S(1)} %collective-permute-done.8._other.other_ref, ...), custom_call_target="tpu_custom_call" | custom-call | flops 1200000000 | bytes 5000000 | tf_op jit(solution)/shard_map/partial_grad/pallas_call | solution.py:242
  53.3 2.7 %collective-permute-start.14 = (bf16[192,1536]{1,0:T(8,128)(2,1)S(1)}, bf16[192,1536]{1,0:T(8,128)(2,1)S(1)}, u32[]{:S(2)}, u32[]{:S(2)}) collective-permute-start(bf16[192,1536]{1,0:T(8,128)(2,1)S(1)} %get-tuple-element.51), channel_id=1, source_target_pairs={{0,12},{2,50},{4,0},{6,54},{8,4},{10,58},{12,8},{14,62},{16,28},{1... | collective-permute-start | bytes 1769480 | tf_op jit(solution)/shard_map/ppermute | solution.py:651
  56.0 3.4 %collective-permute-start.15 = (bf16[192,1536]{1,0:T(8,128)(2,1)S(1)}, bf16[192,1536]{1,0:T(8,128)(2,1)S(1)}, u32[]{:S(2)}, u32[]{:S(2)}) collective-permute-start(bf16[192,1536]{1,0:T(8,128)(2,1)S(1)} %get-tuple-element.52), channel_id=1, source_target_pairs={{0,8},{2,34},{4,12},{6,38},{8,0},{10,42},{12,4},{14,46},{16,24},{1... | collective-permute-start | bytes 1769480 | tf_op jit(solution)/shard_map/ppermute | solution.py:651
  60.3 7.1 %attend_first.1 = (f32[256,1024]{1,0:T(8,128)S(1)}, f32[256,1024]{1,0:T(8,128)S(1)}, f32[256,1024]{1,0:T(8,128)S(1)}) custom-call(s32[1]{0:T(128)} %bitcast.phase_ref, f32[8]{0:T(128)S(1)} %broadcast_multiply_fusion.logit_ref, bf16[128,1024]{1,0:T(8,128)(2,1)S(1)} %copy-done.7, bf16[128,1024]{1,0:T(8,128)(2,1)S(1)} %collective-permute-done.2.query_in_ref, ...), custom_call_target="tpu_custom_call" | custom-call | flops 1000000000 | bytes 4000000 | tf_op jit(solution)/shard_map/attend_first/pallas_call | solution.py:431
  67.6 6.8 %attend_rest.1 = (bf16[128,1024]{1,0:T(8,128)(2,1)S(1)}, bf16[128,1024]{1,0:T(8,128)(2,1)S(1)}, f32[8,128]{1,0:T(8,128)S(1)}) custom-call(s32[1]{0:T(128)} %bitcast.phase_ref, f32[8]{0:T(128)S(1)} %broadcast_multiply_fusion.logit_ref, bf16[128,1024]{1,0:T(8,128)(2,1)S(1)} %copy-done.7, bf16[128,1024]{1,0:T(8,128)(2,1)S(1)} %collective-permute-done.2.query_in_ref, ...), custom_call_target="tpu_custom_call" | custom-call | flops 60000002048 | bytes 4000000 | tf_op jit(solution)/shard_map/attend_rest/pallas_call | solution.py:468
  74.5 1.1 %line_sum.1 = bf16[8,24,1536]{2,1,0:T(8,128)(2,1)} custom-call(bf16[192,1536]{1,0:T(8,128)(2,1)S(1)} %get-tuple-element.49.refs_0_, bf16[192,1536]{1,0:T(8,128)(2,1)S(1)} %collective-permute-done.13.refs_1_, bf16[192,1536]{1,0:T(8,128)(2,1)S(1)} %collective-permute-done.14.refs_2_, bf16[192,1536]{1,0:T(8,128)(2,1)S(1)} %collective-permute-done.15.refs_3_, ...), custom_call_target="tpu_custom_call" | custom-call | flops 1000000 | bytes 3000000 | tf_op jit(solution)/shard_map/line_sum/pallas_call | solution.py:261
  75.6 5.3 %all-to-all-start.1 = ((bf16[8,24,1536]{2,1,0:T(8,128)(2,1)}), bf16[8,24,1536]{2,1,0:T(8,128)(2,1)S(1)}, u32[]{:S(2)}, u32[]{:S(2)}) async-start(bf16[8,24,1536]{2,1,0:T(8,128)(2,1)} %line_sum.1), calls=%async_computation.1 | async-start | bytes 1179648 | tf_op jit(solution)/shard_map/all_to_all | solution.py:667
  80.8 2.3 %copy-done = bf16[2,1536,768]{2,1,0:T(8,128)(2,1)S(1)} copy-done((bf16[2,1536,768]{2,1,0:T(8,128)(2,1)S(1)}, bf16[2,1536,768]{2,1,0:T(8,128)(2,1)}, u32[]{:S(2)}) %copy-start) | copy-done | bytes 4718616
  83.2 2.9 %row_grad.1 = bf16[256,1536]{1,0:T(8,128)(2,1)} custom-call(bf16[256,1536]{1,0:T(8,128)(2,1)S(1)} %ends.1.ends_ref, bf16[2,1536,768]{2,1,0:T(8,128)(2,1)S(1)} %copy-done, f32[8,128]{1,0:T(8,128)S(1)} %get-tuple-element.42.refs_2_._token), custom_call_target="tpu_custom_call" | custom-call | flops 1200000000 | bytes 6000000 | tf_op jit(solution)/shard_map/row_grad/pallas_call | solution.py:176
  86.1 1.9 %leave.1 = (bf16[256,1536]{1,0:T(8,128)(2,1)}, f32[8,128]{1,0:T(8,128)S(1)}) custom-call(s32[1]{0:T(128)} %bitcast.phase_ref, s32[1]{0:T(128)} %bitcast.1.core_ref, bf16[256,1536]{1,0:T(8,128)(2,1)S(1)} %copy-done.2, bf16[128,1024]{1,0:T(8,128)(2,1)S(1)} %get-tuple-element.46.own_ref, bf16[128,1024]{1,0:T(8,128)(2,1)S(1)} %collective-permute-done.12.in_ref, ...), custom_call_target="tpu_custom_call" | custom-call | flops 800000000 | bytes 5000000 | tf_op jit(solution)/shard_map/leave/pallas_call | solution.py:502
  88.0 2.1 %all-to-all-done.1.pieces_ref = bf16[8,24,1536]{2,1,0:T(8,128)(2,1)S(1)} async-done(((bf16[8,24,1536]{2,1,0:T(8,128)(2,1)}), bf16[8,24,1536]{2,1,0:T(8,128)(2,1)S(1)}, u32[]{:S(2)}, u32[]{:S(2)}) %all-to-all-start.1) | async-done | bytes 589856 | tf_op jit(solution)/shard_map/all_to_all | solution.py:667
  (54 shorter events, 9.1 us)
Async XLA Ops:
  1.4 6.4 %collective-permute-start = (bf16[2,2,768]{2,1,0:T(2,128)(2,1)S(1)}, bf16[2,2,768]{2,1,0:T(2,128)(2,1)S(1)}, u32[]{:S(2)}, u32[]{:S(2)}) collective-permute-start(bf16[2,2,768]{2,1,0:T(2,128)(2,1)S(1)} %get-tuple-element.56), channel_id=1, source_target_pairs={{0,2},{2,4},{4,6},{6,8},{8,10},{10,12},{12,14},{14,16},{16,18},{18... | collective-permute-start | bytes 18440 | tf_op jit(solution)/shard_map/ppermute | solution.py:584
  3.1 4.6 %collective-permute-start.1 = (bf16[2,2,768]{2,1,0:T(2,128)(2,1)S(1)}, bf16[2,2,768]{2,1,0:T(2,128)(2,1)S(1)}, u32[]{:S(2)}, u32[]{:S(2)}) collective-permute-start(bf16[2,2,768]{2,1,0:T(2,128)(2,1)S(1)} %get-tuple-element.55), channel_id=1, source_target_pairs={{2,0},{4,2},{6,4},{8,6},{10,8},{12,10},{14,12},{16,14},{18,16},{20... | collective-permute-start | bytes 18440 | tf_op jit(solution)/shard_map/ppermute | solution.py:584
  8.4 10.7 %copy-start.8 = (f32[1536]{0:T(1024)S(1)}, f32[1536]{0:T(1024)}, u32[]{:S(2)}) copy-start(f32[1536]{0:T(1024)} %param.17) | copy-start | bytes 18436
  8.4 36.2 %all-to-all-start = ((bf16[32,16,1664]{2,1,0:T(8,128)(2,1)}), bf16[32,16,1664]{2,1,0:T(8,128)(2,1)S(1)}, u32[]{:S(2)}, u32[]{:S(2)}) async-start(bf16[32,16,1664]{2,1,0:T(8,128)(2,1)} %follow.1), calls=%async_computation | async-start | bytes 3407872 | tf_op jit(solution)/shard_map/all_to_all | solution.py:623
  19.7 11.4 %copy-start.3 = (bf16[1,2,128,1536]{3,2,1,0:T(8,128)(2,1)S(1)}, bf16[1,2,128,1536]{3,2,1,0:T(8,128)(2,1)}, u32[]{:S(2)}) copy-start(bf16[1,2,128,1536]{3,2,1,0:T(8,128)(2,1)} %param.22) | copy-start | bytes 2359300
  28.7 21.5 %copy-start.11 = (f32[8]{0:T(128)S(1)}, f32[8]{0:T(128)}, u32[]{:S(2)}) copy-start(f32[8]{0:T(128)} %param.21) | copy-start | bytes 100
  28.7 1.5 %collective-permute-start.3 = (bf16[128,256]{1,0:T(8,128)(2,1)}, bf16[128,256]{1,0:T(8,128)(2,1)S(1)}, u32[]{:S(2)}, u32[]{:S(2)}) collective-permute-start(bf16[128,256]{1,0:T(8,128)(2,1)} %get-tuple-element.34), channel_id=1, source_target_pairs={{0,2},{2,0},{1,3},{3,1},{4,6},{6,4},{5,7},{7,5},{8,10},{10,8},{9,1... | collective-permute-start | bytes 196616 | tf_op jit(solution)/shard_map/ppermute | solution.py:637
  32.0 12.3 %copy-start.5 = (bf16[16,48,256]{2,1,0:T(8,128)(2,1)}, bf16[16,48,256]{2,1,0:T(8,128)(2,1)S(1)}, u32[]{:S(2)}) copy-start(bf16[16,48,256]{2,1,0:T(8,128)(2,1)S(1)} %get-tuple-element.38.mine_ref) | copy-start | bytes 1179652
  32.0 12.3 %collective-permute-start.8 = (bf16[16,48,256]{2,1,0:T(8,128)(2,1)S(1)}, bf16[16,48,256]{2,1,0:T(8,128)(2,1)S(1)}, u32[]{:S(2)}, u32[]{:S(2)}) collective-permute-start(bf16[16,48,256]{2,1,0:T(8,128)(2,1)S(1)} %get-tuple-element.39), channel_id=1, source_target_pairs={{0,2},{2,0},{1,3},{3,1},{4,6},{6,4},{5,7},{7,5},{8,10},{10,8},{9,1... | collective-permute-start | bytes 1179656 | tf_op jit(solution)/shard_map/ppermute | solution.py:645
  32.3 11.6 %collective-permute-start.4 = (bf16[256,256]{1,0:T(8,128)(2,1)S(1)}, bf16[256,256]{1,0:T(8,128)(2,1)S(1)}, u32[]{:S(2)}, u32[]{:S(2)}) collective-permute-start(bf16[256,256]{1,0:T(8,128)(2,1)S(1)} %get-tuple-element.35.refs_0_), channel_id=1, source_target_pairs={{0,8},{2,34},{4,12},{6,38},{8,0},{10,42},{12,4},{14,46},{16,24},{1... | collective-permute-start | bytes 393224 | tf_op jit(solution)/shard_map/ppermute | solution.py:577
  35.5 8.7 %collective-permute-start.5 = (bf16[256,256]{1,0:T(8,128)(2,1)S(1)}, bf16[256,256]{1,0:T(8,128)(2,1)S(1)}, u32[]{:S(2)}, u32[]{:S(2)}) collective-permute-start(bf16[256,256]{1,0:T(8,128)(2,1)S(1)} %get-tuple-element.35.refs_0_), channel_id=1, source_target_pairs={{0,4},{2,18},{4,8},{6,22},{8,12},{10,26},{12,0},{14,30},{16,20},{1... | collective-permute-start | bytes 393224 | tf_op jit(solution)/shard_map/ppermute | solution.py:577
  36.1 8.2 %collective-permute-start.6 = (bf16[256,256]{1,0:T(8,128)(2,1)S(1)}, bf16[256,256]{1,0:T(8,128)(2,1)S(1)}, u32[]{:S(2)}, u32[]{:S(2)}) collective-permute-start(bf16[256,256]{1,0:T(8,128)(2,1)S(1)} %get-tuple-element.35.refs_0_), channel_id=1, source_target_pairs={{0,12},{2,50},{4,0},{6,54},{8,4},{10,58},{12,8},{14,62},{16,28},{1... | collective-permute-start | bytes 393224 | tf_op jit(solution)/shard_map/ppermute | solution.py:577
  45.3 4.9 %collective-permute-start.9 = (bf16[256,1536]{1,0:T(8,128)(2,1)S(1)}, bf16[256,1536]{1,0:T(8,128)(2,1)S(1)}, u32[]{:S(2)}, u32[]{:S(2)}) collective-permute-start(bf16[256,1536]{1,0:T(8,128)(2,1)S(1)} %ends.1.ends_ref), channel_id=1, source_target_pairs={{0,2},{2,0},{1,3},{3,1},{4,6},{6,4},{5,7},{7,5},{8,10},{10,8},{9,1... | collective-permute-start | bytes 2359304 | tf_op jit(solution)/shard_map/ppermute | solution.py:648
  45.4 10.6 %collective-permute-start.7 = (bf16[1024,256]{1,0:T(8,128)(2,1)S(1)}, bf16[1024,256]{1,0:T(8,128)(2,1)}, u32[]{:S(2)}, u32[]{:S(2)}) collective-permute-start(bf16[1024,256]{1,0:T(8,128)(2,1)S(1)} %get-tuple-element.36.refs_0_), channel_id=1, source_target_pairs={{0,16},{2,6},{4,20},{6,10},{8,24},{10,14},{12,28},{14,2},{16,32},{... | collective-permute-start | bytes 1572872 | tf_op jit(solution)/shard_map/ppermute | solution.py:577
  47.2 20.2 %collective-permute-start.10 = (bf16[1024,256]{1,0:T(8,128)(2,1)S(1)}, bf16[1024,256]{1,0:T(8,128)(2,1)S(1)}, u32[]{:S(2)}, u32[]{:S(2)}) collective-permute-start(bf16[1024,256]{1,0:T(8,128)(2,1)S(1)} %get-tuple-element.36.refs_0_), channel_id=1, source_target_pairs={{0,48},{2,14},{4,52},{6,2},{8,56},{10,6},{12,60},{14,10},{16,0},{1... | collective-permute-start | bytes 1572872 | tf_op jit(solution)/shard_map/ppermute | solution.py:577
  48.7 18.9 %collective-permute-start.11 = (bf16[1024,256]{1,0:T(8,128)(2,1)S(1)}, bf16[1024,256]{1,0:T(8,128)(2,1)}, u32[]{:S(2)}, u32[]{:S(2)}) collective-permute-start(bf16[1024,256]{1,0:T(8,128)(2,1)S(1)} %get-tuple-element.36.refs_0_), channel_id=1, source_target_pairs={{0,32},{2,10},{4,36},{6,14},{8,40},{10,2},{12,44},{14,6},{16,48},{... | collective-permute-start | bytes 1572872 | tf_op jit(solution)/shard_map/ppermute | solution.py:577
  50.2 3.1 %collective-permute-start.2 = (bf16[128,1024]{1,0:T(8,128)(2,1)}, bf16[128,1024]{1,0:T(8,128)(2,1)S(1)}, u32[]{:S(2)}, u32[]{:S(2)}) collective-permute-start(bf16[128,1024]{1,0:T(8,128)(2,1)} %get-tuple-element.32), channel_id=1, source_target_pairs={{0,2},{2,0},{1,3},{3,1},{4,6},{6,4},{5,7},{7,5},{8,10},{10,8},{9,1... | collective-permute-start | bytes 786440 | tf_op jit(solution)/shard_map/ppermute | solution.py:640
  52.6 21.8 %collective-permute-start.13 = (bf16[192,1536]{1,0:T(8,128)(2,1)S(1)}, bf16[192,1536]{1,0:T(8,128)(2,1)S(1)}, u32[]{:S(2)}, u32[]{:S(2)}) collective-permute-start(bf16[192,1536]{1,0:T(8,128)(2,1)S(1)} %get-tuple-element.50), channel_id=1, source_target_pairs={{0,4},{2,18},{4,8},{6,22},{8,12},{10,26},{12,0},{14,30},{16,20},{1... | collective-permute-start | bytes 1769480 | tf_op jit(solution)/shard_map/ppermute | solution.py:651
  53.3 21.2 %collective-permute-start.14 = (bf16[192,1536]{1,0:T(8,128)(2,1)S(1)}, bf16[192,1536]{1,0:T(8,128)(2,1)S(1)}, u32[]{:S(2)}, u32[]{:S(2)}) collective-permute-start(bf16[192,1536]{1,0:T(8,128)(2,1)S(1)} %get-tuple-element.51), channel_id=1, source_target_pairs={{0,12},{2,50},{4,0},{6,54},{8,4},{10,58},{12,8},{14,62},{16,28},{1... | collective-permute-start | bytes 1769480 | tf_op jit(solution)/shard_map/ppermute | solution.py:651
  56.0 18.5 %collective-permute-start.15 = (bf16[192,1536]{1,0:T(8,128)(2,1)S(1)}, bf16[192,1536]{1,0:T(8,128)(2,1)S(1)}, u32[]{:S(2)}, u32[]{:S(2)}) collective-permute-start(bf16[192,1536]{1,0:T(8,128)(2,1)S(1)} %get-tuple-element.52), channel_id=1, source_target_pairs={{0,8},{2,34},{4,12},{6,38},{8,0},{10,42},{12,4},{14,46},{16,24},{1... | collective-permute-start | bytes 1769480 | tf_op jit(solution)/shard_map/ppermute | solution.py:651
  75.6 14.6 %all-to-all-start.1 = ((bf16[8,24,1536]{2,1,0:T(8,128)(2,1)}), bf16[8,24,1536]{2,1,0:T(8,128)(2,1)S(1)}, u32[]{:S(2)}, u32[]{:S(2)}) async-start(bf16[8,24,1536]{2,1,0:T(8,128)(2,1)} %line_sum.1), calls=%async_computation.1 | async-start | bytes 1179648 | tf_op jit(solution)/shard_map/all_to_all | solution.py:667
  80.8 5.2 %collective-permute-start.12 = (bf16[128,1024]{1,0:T(8,128)(2,1)S(1)}, bf16[128,1024]{1,0:T(8,128)(2,1)S(1)}, u32[]{:S(2)}, u32[]{:S(2)}) collective-permute-start(bf16[128,1024]{1,0:T(8,128)(2,1)S(1)} %get-tuple-element.47), channel_id=1, source_target_pairs={{0,2},{2,0},{1,3},{3,1},{4,6},{6,4},{5,7},{7,5},{8,10},{10,8},{9,1... | collective-permute-start | bytes 786440 | tf_op jit(solution)/shard_map/ppermute | solution.py:661
  83.2 2.9 %copy-start.1 = (bf16[1024,1536]{1,0:T(8,128)(2,1)S(1)}, bf16[1024,1536]{1,0:T(8,128)(2,1)}, u32[]{:S(2)}) copy-start(bf16[1024,1536]{1,0:T(8,128)(2,1)} %exit_ref.1) | copy-start | bytes 9437188
  83.2 2.9 %copy-start.2 = (bf16[256,1536]{1,0:T(8,128)(2,1)S(1)}, bf16[256,1536]{1,0:T(8,128)(2,1)}, u32[]{:S(2)}) copy-start(bf16[256,1536]{1,0:T(8,128)(2,1)} %get-tuple-element.30.rows_ref) | copy-start | bytes 2359300
  (6 other events, 6.3 us)
